TPU v7x, 512 devices: a whole 4x4x16 slice. The times are simulated.
512 devices in a mesh: leaf: 64 (over z, x), front: 8 (over y, core).
Axes of the slice: x: 4, y: 4, z: 16, core: 2. Of those that a mesh axis runs over, the one named last changes fastest.
Arguments:
- fields: bfloat16 [2, 48, 65536], P(None, None, ('leaf', 'front')), may hold values from -6 to 6
- direction: float32 [2, 65536], P(None, ('leaf', 'front')), may hold values from -6 to 6
- inverse_blocks: bfloat16 [2, 65536, 1024], P(None, ('leaf', 'front')), may hold values from -1.5 to 1.5
- update_blocks: bfloat16 [2, 65536, 1024], P(None, ('leaf', 'front')), may hold values from -0.125 to 0.125
- row_map: int32 [2, 64, 1024], P(None, 'leaf'), may hold values from 0 to 1023, each once within a row
- receivers: int32 [64, 128], P('leaf'), may hold values from 0 to 1023
- weights: float32 [64, 128], P('leaf'), may hold values from 0.05 to 0.5
Outputs:
- data_change: bfloat16 [48, 8192], P(None, 'leaf')
- curvature: float32 [2, 65536], P(None, ('leaf', 'front'))
Inputs may be any that keep to these rules, and one draw needn't show every extreme that they name: Each row_map[k, g] is a permutation of 0 .. 1023.
All inputs are finite; a program needn't handle non-finite values.
Results may differ from a plain program's by a relative error of at most 0.033.
Values may be sent and summed in bfloat16 or wider, within the bound.
No kernel may reach another device: no remote copies, remote signals or barrier semaphores. Data moves between devices by JAX's collectives and lax.ppermute only.
A program may use at most 64 MiB of HBM per device.

v0:
```python
import jax
import jax.numpy as jnp
from jax import lax
from jax.sharding import PartitionSpec as P

CONTRACT_LAST = (((1,), (1,)), ((), ()))


def passed_along(value, axis, steps):
    count = lax.axis_size(axis)
    initial, last = (max(0, -steps), min(count, count - steps))
    return lax.ppermute(value, axis, [(source, source + steps) for source in range(initial, last)])


def apply_rows(vectors, block):
    return lax.dot_general(vectors, block, CONTRACT_LAST, preferred_element_type=jnp.float32)


def front_forward(residual, inverse_rows, update_rows):
    solved = apply_rows(residual, inverse_rows).astype(jnp.bfloat16)
    update = apply_rows(residual, update_rows).astype(jnp.bfloat16)
    return (solved, update)


def front_backward(solved_rows, parent_rows, inverse_rows, update_rows):
    first_term = jnp.dot(solved_rows, inverse_rows, preferred_element_type=jnp.float32)
    return first_term - jnp.dot(parent_rows, update_rows, preferred_element_type=jnp.float32)


def send_up(message, shift_by):
    return passed_along((message[0], message[1]), "leaf", shift_by)


def send_down(values, shift_by):
    return passed_along(values, "leaf", shift_by)


def assemble(partial_sum):
    return lax.psum(partial_sum.astype(jnp.bfloat16), "front")


def scatter_columns(base, columns, values):
    return base.at[:, columns].add(-values.astype(jnp.float32))


def solve(
    leaf_source,
    node_source,
    inverse_blocks,
    update_blocks,
    leaf_map,
    node_map,
    group_id,
    own_height,
    height_top,
    row_start,
):
    block_rows = inverse_blocks.shape[1]
    leaf_solved, leaf_update = front_forward(leaf_source, inverse_blocks[0], update_blocks[0])
    node_solved = jnp.zeros_like(leaf_solved)
    sent_update = leaf_update
    sent_map = leaf_map
    kept_left = node_map
    kept_right = node_map
    for height in range(1, height_top + 1):
        if height == 1:
            left_update, left_map = send_up((sent_update, sent_map), 1)
            right_update, right_map = (leaf_update, leaf_map)
        else:
            offset = 2 ** (height - 2)
            left_update, left_map = send_up((sent_update, sent_map), offset)
            right_update, right_map = send_up((sent_update, sent_map), -offset)
        left_whole, right_whole = (
            lax.all_gather(left_update, "front", axis=1, tiled=True),
            lax.all_gather(right_update, "front", axis=1, tiled=True),
        )
        residual = scatter_columns(node_source.astype(jnp.float32), left_map, left_whole)
        residual = scatter_columns(residual, right_map, right_whole).astype(jnp.bfloat16)
        is_owner = own_height == height
        new_solved, new_update = front_forward(residual, inverse_blocks[1], update_blocks[1])
        node_solved = jnp.where(is_owner, new_solved, node_solved)
        sent_update = jnp.where(is_owner, new_update, sent_update)
        kept_left = jnp.where(is_owner, left_map, kept_left)
        kept_right = jnp.where(is_owner, right_map, kept_right)
        sent_map = node_map
    node_parent = jnp.zeros_like(node_solved)
    leaf_parent = node_parent
    node_whole = jnp.zeros(leaf_source.shape, jnp.bfloat16)
    node_cols = lax.dynamic_slice_in_dim(node_map, row_start, block_rows)
    leaf_cols = lax.dynamic_slice_in_dim(leaf_map, row_start, block_rows)
    for height in range(height_top, 0, -1):
        is_owner = own_height == height
        partial_sum = front_backward(node_solved, node_parent, inverse_blocks[1], update_blocks[1])
        on_left = group_id // 2 ** (height - 1) % 2 == 0
        offset = 2 ** max(height - 2, 0)
        solved = assemble(partial_sum)
        node_whole = jnp.where(is_owner, solved, node_whole)
        if height == 1:
            parent_whole = jnp.where(on_left, send_down(solved, -1), solved)
            from_parent = jnp.take(parent_whole, leaf_cols, axis=1)
        else:
            parent_whole = jnp.where(on_left, send_down(solved, -offset), send_down(solved, offset))
            from_parent = jnp.take(parent_whole, node_cols, axis=1)
        if height == 1:
            leaf_parent = from_parent
        else:
            node_parent = jnp.where(own_height == height - 1, from_parent, node_parent)
    final_rows = lax.dynamic_slice_in_dim(node_whole, row_start, block_rows, 1)
    leaf_whole = assemble(
        front_backward(leaf_solved, leaf_parent, inverse_blocks[0], update_blocks[0])
    )
    return (leaf_whole, final_rows)


def per_device(fields, direction, inverse_blocks, update_blocks, row_map, receivers, weights):
    height_top = lax.axis_size("leaf").bit_length() - 1
    group_id = lax.axis_index("leaf")
    block_rows = inverse_blocks.shape[1]
    row_start = lax.axis_index("front") * block_rows
    trailing = jnp.zeros((), jnp.int32)
    for bit_pos in range(height_top):
        trailing = trailing + (group_id % 2 ** (bit_pos + 1) == 0).astype(jnp.int32)
    own_height = trailing + 1
    leaf_map = row_map[0, 0]
    node_map = row_map[1, 0]
    source_terms = (direction[:, None, :] * fields.astype(jnp.float32)).astype(jnp.bfloat16)
    source_whole = lax.all_gather(source_terms, "front", axis=2, tiled=True)
    delta_leaf, delta_node = solve(
        source_whole[0],
        source_whole[1],
        inverse_blocks,
        update_blocks,
        leaf_map,
        node_map,
        group_id,
        own_height,
        height_top,
        row_start,
    )
    station_values = jnp.take(delta_leaf, receivers[0], axis=1)
    injected = jnp.zeros(delta_leaf.shape, jnp.float32)
    injected = injected.at[:, receivers[0]].add(
        weights[0][None, :] * station_values.astype(jnp.float32)
    )
    injected = injected.astype(jnp.bfloat16)
    adjoint_leaf, adjoint_node_rows = solve(
        injected,
        jnp.zeros_like(injected),
        inverse_blocks,
        update_blocks,
        leaf_map,
        node_map,
        group_id,
        own_height,
        height_top,
        row_start,
    )
    leaf_rows = lax.dynamic_slice_in_dim(adjoint_leaf, row_start, block_rows, 1)
    curve_leaf = jnp.sum(fields[0].astype(jnp.float32) * leaf_rows.astype(jnp.float32), axis=0)
    curve_node = jnp.sum(
        fields[1].astype(jnp.float32) * adjoint_node_rows.astype(jnp.float32), axis=0
    )
    return (station_values, jnp.stack([curve_leaf, curve_node]))


def solution(mesh):
    in_specs = (
        P(None, None, ("leaf", "front")),
        P(None, ("leaf", "front")),
        P(None, ("leaf", "front"), None),
        P(None, ("leaf", "front"), None),
        P(None, "leaf", None),
        P("leaf", None),
        P("leaf", None),
    )
    out_specs = (P(None, "leaf"), P(None, ("leaf", "front")))
    return jax.shard_map(
        per_device, mesh=mesh, in_specs=in_specs, out_specs=out_specs, check_vma=False
    )
```

profile of v0, /device:TPU:1, one launch (start us, length us, event | category | flops | bytes accessed | tf_op | source)
XLA Modules:
  0.0 1826.2 jit_solution(10678629854170555780)
XLA Ops:
  23.6 14.0 all_gather.75
  45.0 12.3 all_gather.77
  72.2 6.6 collective-permute-start.1
  81.9 11.5 collective-permute-start
  97.7 6.4 collective-permute-done.20
  104.6 14.3 all_gather.76
  121.6 8.2 scatter_fusion
  129.8 6.6 scatter_fusion.1
  140.8 11.2 all_gather.78
  153.8 11.3 all_gather.79
  167.7 7.8 scatter_fusion.2
  175.6 6.9 scatter_fusion.3
  186.9 11.2 all_gather.80
  200.0 11.5 all_gather.81
  214.1 8.0 scatter_fusion.4
  222.0 6.6 scatter_fusion.5
  229.0 7.5 collective-permute-start.13
  238.1 11.5 all_gather.82
  249.8 11.3 all_gather.83
  262.9 8.0 scatter_fusion.6
  270.9 6.4 scatter_fusion.7
  284.4 11.5 all_gather.84
  296.2 11.3 all_gather.85
  308.1 8.2 scatter_fusion.8
  316.4 6.2 scatter_fusion.9
  322.9 12.0 collective-permute-start.19
  336.4 11.5 all_gather.86
  348.2 11.3 all_gather.87
  360.5 7.8 scatter_fusion.10
  376.4 64.8 %all-reduce.15.cloned.1.call-done = bf16[48,1024]{1,0:T(8,128)(2,1)} async-done(((bf16[48,1024]{1,0:T(8,128)(2,1)}), bf16[48,1024]{1,0:T(8,128)(2,1)}) %all-reduce.15.cloned.1.call-update) | async-done | bytes 98320 | tf_op jit(solution)/shard_map/psum | solution.py:39
  442.4 7.9 collective-permute-start.23
  458.0 75.7 %all-reduce.17.cloned.1.call-done = bf16[48,1024]{1,0:T(8,128)(2,1)} async-done(((bf16[48,1024]{1,0:T(8,128)(2,1)}), bf16[48,1024]{1,0:T(8,128)(2,1)}) %all-reduce.17.cloned.1.call-update) | async-done | bytes 98320 | tf_op jit(solution)/shard_map/psum | solution.py:39
  543.8 76.6 %all-reduce.19.cloned.1.call-done = bf16[48,1024]{1,0:T(8,128)(2,1)} async-done(((bf16[48,1024]{1,0:T(8,128)(2,1)}), bf16[48,1024]{1,0:T(8,128)(2,1)}) %all-reduce.19.cloned.1.call-update) | async-done | bytes 98320 | tf_op jit(solution)/shard_map/psum | solution.py:39
  629.9 74.4 %all-reduce.21.cloned.1.call-done = bf16[48,1024]{1,0:T(8,128)(2,1)} async-done(((bf16[48,1024]{1,0:T(8,128)(2,1)}), bf16[48,1024]{1,0:T(8,128)(2,1)}) %all-reduce.21.cloned.1.call-update) | async-done | bytes 98320 | tf_op jit(solution)/shard_map/psum | solution.py:39
  714.9 75.8 %all-reduce.23.cloned.1.call-done = bf16[48,1024]{1,0:T(8,128)(2,1)} async-done(((bf16[48,1024]{1,0:T(8,128)(2,1)}), bf16[48,1024]{1,0:T(8,128)(2,1)}) %all-reduce.23.cloned.1.call-update) | async-done | bytes 98320 | tf_op jit(solution)/shard_map/psum | solution.py:39
  800.5 75.9 %all-reduce.25.cloned.1.call-done = bf16[48,1024]{1,0:T(8,128)(2,1)} async-done(((bf16[48,1024]{1,0:T(8,128)(2,1)}), bf16[48,1024]{1,0:T(8,128)(2,1)}) %all-reduce.25.cloned.1.call-update) | async-done | bytes 98320 | tf_op jit(solution)/shard_map/psum | solution.py:39
  883.9 75.6 %all-reduce.27.cloned.1.call-done = bf16[48,1024]{1,0:T(8,128)(2,1)} async-done(((bf16[48,1024]{1,0:T(8,128)(2,1)}), bf16[48,1024]{1,0:T(8,128)(2,1)}) %all-reduce.27.cloned.1.call-update) | async-done | bytes 98320 | tf_op jit(solution)/shard_map/psum | solution.py:39
  965.8 13.9 all_gather.89
  979.9 11.3 all_gather.88
  991.4 7.9 scatter_custom_fusion.13
  1008.8 11.5 all_gather.90
  1020.6 7.9 scatter_custom_fusion.15
  1028.5 11.3 all_gather.91
  1052.8 11.5 all_gather.92
  1064.5 7.9 scatter_custom_fusion.17
  1072.4 11.3 all_gather.93
  1098.5 11.5 all_gather.94
  1110.2 7.9 scatter_custom_fusion.19
  1118.1 11.3 all_gather.95
  1141.8 11.7 all_gather.96
  1153.7 7.9 scatter_custom_fusion.21
  1161.6 11.3 all_gather.97
  1179.6 11.6 collective-permute-start.42
  1192.7 11.5 all_gather.98
  1204.5 7.9 scatter_custom_fusion.23
  1212.4 11.3 all_gather.99
  1231.3 68.8 %all-reduce.29.cloned.1.call-done = bf16[48,1024]{1,0:T(8,128)(2,1)} async-done(((bf16[48,1024]{1,0:T(8,128)(2,1)}), bf16[48,1024]{1,0:T(8,128)(2,1)}) %all-reduce.29.cloned.1.call-update) | async-done | bytes 98320 | tf_op jit(solution)/shard_map/psum | solution.py:39
  1301.3 7.9 collective-permute-start.45
  1317.4 75.7 %all-reduce.31.cloned.1.call-done = bf16[48,1024]{1,0:T(8,128)(2,1)} async-done(((bf16[48,1024]{1,0:T(8,128)(2,1)}), bf16[48,1024]{1,0:T(8,128)(2,1)}) %all-reduce.31.cloned.1.call-update) | async-done | bytes 98320 | tf_op jit(solution)/shard_map/psum | solution.py:39
  1403.2 76.6 %all-reduce.33.cloned.1.call-done = bf16[48,1024]{1,0:T(8,128)(2,1)} async-done(((bf16[48,1024]{1,0:T(8,128)(2,1)}), bf16[48,1024]{1,0:T(8,128)(2,1)}) %all-reduce.33.cloned.1.call-update) | async-done | bytes 98320 | tf_op jit(solution)/shard_map/psum | solution.py:39
  1488.8 74.8 %all-reduce.35.cloned.1.call-done = bf16[48,1024]{1,0:T(8,128)(2,1)} async-done(((bf16[48,1024]{1,0:T(8,128)(2,1)}), bf16[48,1024]{1,0:T(8,128)(2,1)}) %all-reduce.35.cloned.1.call-update) | async-done | bytes 98320 | tf_op jit(solution)/shard_map/psum | solution.py:39
  1574.3 75.8 %all-reduce.37.cloned.1.call-done = bf16[48,1024]{1,0:T(8,128)(2,1)} async-done(((bf16[48,1024]{1,0:T(8,128)(2,1)}), bf16[48,1024]{1,0:T(8,128)(2,1)}) %all-reduce.37.cloned.1.call-update) | async-done | bytes 98320 | tf_op jit(solution)/shard_map/psum | solution.py:39
  1659.1 76.6 %all-reduce.39.cloned.1.call-done = bf16[48,1024]{1,0:T(8,128)(2,1)} async-done(((bf16[48,1024]{1,0:T(8,128)(2,1)}), bf16[48,1024]{1,0:T(8,128)(2,1)}) %all-reduce.39.cloned.1.call-update) | async-done | bytes 98320 | tf_op jit(solution)/shard_map/psum | solution.py:39
  1744.1 74.0 %all-reduce.41.cloned.1.call-done = bf16[48,1024]{1,0:T(8,128)(2,1)} async-done(((bf16[48,1024]{1,0:T(8,128)(2,1)}), bf16[48,1024]{1,0:T(8,128)(2,1)}) %all-reduce.41.cloned.1.call-update) | async-done | bytes 98320 | tf_op jit(solution)/shard_map/psum | solution.py:39
  (358 shorter events, 276.4 us)
Async XLA Ops:
  7.2 434.0 %all-reduce.15.cloned.1.call-start = ((), (), s32[]{:S(2)}) async-start(), calls=%async_computation | async-start | bytes 196608 | tf_op jit(solution)/shard_map/psum | solution.py:39
  8.6 54.8 %collective-permute-start.4 = (s32[1024]{0:T(1024)}, s32[1024]{0:T(1024)}, u32[]{:S(2)}, u32[]{:S(2)}) collective-permute-start(s32[1024]{0:T(1024)} %bitcast.5), channel_id=1, source_target_pairs={{0,8},{8,16},{16,24},{24,32},{32,40},{40,48},{48,56},{56,64},{64,7... | collective-permute-start | bytes 12296 | tf_op jit(solution)/shard_map/ppermute | solution.py:12
  13.1 56.5 %collective-permute-start.8 = (s32[1024]{0:T(1024)}, s32[1024]{0:T(1024)}, u32[]{:S(2)}, u32[]{:S(2)}) collective-permute-start(s32[1024]{0:T(1024)} %bitcast.5), channel_id=1, source_target_pairs={{8,0},{16,8},{24,16},{32,24},{40,32},{48,40},{56,48},{64,56},{72,6... | collective-permute-start | bytes 12296 | tf_op jit(solution)/shard_map/ppermute | solution.py:12
  14.4 57.8 %collective-permute-start.3 = (s32[1024]{0:T(1024)}, s32[1024]{0:T(1024)}, u32[]{:S(2)}, u32[]{:S(2)}) collective-permute-start(s32[1024]{0:T(1024)} %bitcast.5), channel_id=1, source_target_pairs={{0,16},{8,24},{16,32},{24,40},{32,48},{40,56},{48,64},{56,72},{64,... | collective-permute-start | bytes 12296 | tf_op jit(solution)/shard_map/ppermute | solution.py:12
  19.9 40.9 %collective-permute-start.5 = (s32[1024]{0:T(1024)}, s32[1024]{0:T(1024)}, u32[]{:S(2)}, u32[]{:S(2)}) collective-permute-start(s32[1024]{0:T(1024)} %bitcast.7), channel_id=1, source_target_pairs={{0,8},{8,16},{16,24},{24,32},{32,40},{40,48},{48,56},{56,64},{64,7... | collective-permute-start | bytes 12296 | tf_op jit(solution)/shard_map/ppermute | solution.py:12
  38.8 65.9 %collective-permute-start.6 = (bf16[48,128]{1,0:T(8,128)(2,1)S(1)}, bf16[48,128]{1,0:T(8,128)(2,1)}, u32[]{:S(2)}, u32[]{:S(2)}) collective-permute-start(bf16[48,128]{1,0:T(8,128)(2,1)S(1)} %convolution_convert_fusion), channel_id=1, source_target_pairs={{0,8},{8,16},{16,24},{24,32},{32,40},{40,48},{48,56},{56,64},{64,7... | collective-permute-start | bytes 36872 | tf_op jit(solution)/shard_map/ppermute | solution.py:12
  60.8 19.2 %collective-permute-start.11 = (s32[1024]{0:T(1024)}, s32[1024]{0:T(1024)S(1)}, u32[]{:S(2)}, u32[]{:S(2)}) collective-permute-start(s32[1024]{0:T(1024)} %bitcast.5), channel_id=1, source_target_pairs={{16,0},{24,8},{32,16},{40,24},{48,32},{56,40},{64,48},{72,56},{80,... | collective-permute-start | bytes 12296 | tf_op jit(solution)/shard_map/ppermute | solution.py:12
  63.4 18.5 %collective-permute-start.2 = (s32[1024]{0:T(1024)}, s32[1024]{0:T(1024)S(1)}, u32[]{:S(2)}, u32[]{:S(2)}) collective-permute-start(s32[1024]{0:T(1024)} %bitcast.5), channel_id=1, source_target_pairs={{0,32},{8,40},{16,48},{24,56},{32,64},{40,72},{48,80},{56,88},{64,... | collective-permute-start | bytes 12296 | tf_op jit(solution)/shard_map/ppermute | solution.py:12
  69.6 24.4 %collective-permute-start.14 = (s32[1024]{0:T(1024)}, s32[1024]{0:T(1024)S(1)}, u32[]{:S(2)}, u32[]{:S(2)}) collective-permute-start(s32[1024]{0:T(1024)} %bitcast.5), channel_id=1, source_target_pairs={{32,0},{40,8},{48,16},{56,24},{64,32},{72,40},{80,48},{88,56},{96,... | collective-permute-start | bytes 12296 | tf_op jit(solution)/shard_map/ppermute | solution.py:12
  72.2 23.7 %collective-permute-start.1 = (s32[1024]{0:T(1024)}, s32[1024]{0:T(1024)S(1)}, u32[]{:S(2)}, u32[]{:S(2)}) collective-permute-start(s32[1024]{0:T(1024)} %bitcast.5), channel_id=1, source_target_pairs={{0,64},{8,72},{16,80},{24,88},{32,96},{40,104},{48,112},{56,120},{... | collective-permute-start | bytes 12296 | tf_op jit(solution)/shard_map/ppermute | solution.py:12
  80.0 16.5 collective-permute-start.17
  81.9 15.2 collective-permute-start
  94.0 10.0 collective-permute-start.20
  138.6 15.2 collective-permute-start.9
  184.8 15.2 collective-permute-start.12
  229.0 9.1 collective-permute-start.13
  236.5 13.3 collective-permute-start.15
  277.5 6.9 collective-permute-start.16
  282.9 13.3 collective-permute-start.18
  322.9 13.5 collective-permute-start.19
  334.9 13.3 collective-permute-start.21
  375.7 158.1 %all-reduce.17.cloned.1.call-start = ((), (), s32[]{:S(2)}) async-start(), calls=%async_computation.1 | async-start | bytes 196608 | tf_op jit(solution)/shard_map/psum | solution.py:39
  441.2 15.0 collective-permute-start.22
  442.4 13.7 collective-permute-start.23
  458.0 162.3 %all-reduce.19.cloned.1.call-start = ((), (), s32[]{:S(2)}) async-start(), calls=%async_computation.2 | async-start | bytes 196608 | tf_op jit(solution)/shard_map/psum | solution.py:39
  533.7 7.5 collective-permute-start.24
  535.0 6.8 collective-permute-start.25
  543.7 160.5 %all-reduce.21.cloned.1.call-start = ((), (), s32[]{:S(2)}) async-start(), calls=%async_computation.3 | async-start | bytes 196608 | tf_op jit(solution)/shard_map/psum | solution.py:39
  620.3 5.6 collective-permute-start.26
  621.6 5.9 collective-permute-start.27
  629.4 161.3 %all-reduce.23.cloned.1.call-start = ((), (), s32[]{:S(2)}) async-start(), calls=%async_computation.4 | async-start | bytes 196608 | tf_op jit(solution)/shard_map/psum | solution.py:39
  704.3 7.1 collective-permute-start.28
  705.5 7.4 collective-permute-start.29
  714.8 161.6 %all-reduce.25.cloned.1.call-start = ((), (), s32[]{:S(2)}) async-start(), calls=%async_computation.5 | async-start | bytes 196608 | tf_op jit(solution)/shard_map/psum | solution.py:39
  790.7 5.6 collective-permute-start.30
  792.0 5.9 collective-permute-start.31
  799.7 159.7 %all-reduce.27.cloned.1.call-start = ((), (), s32[]{:S(2)}) async-start(), calls=%async_computation.6 | async-start | bytes 196608 | tf_op jit(solution)/shard_map/psum | solution.py:39
  876.4 5.6 collective-permute-start.32
  883.8 416.2 %all-reduce.29.cloned.1.call-start = ((), (), s32[]{:S(2)}) async-start(), calls=%async_computation.7 | async-start | bytes 196608 | tf_op jit(solution)/shard_map/psum | solution.py:39
  963.4 16.5 collective-permute-start.33
  1007.5 20.9 %collective-permute-start.35 = (bf16[48,128]{1,0:T(8,128)(2,1)S(1)}, bf16[48,128]{1,0:T(8,128)(2,1)S(1)}, u32[]{:S(2)}, u32[]{:S(2)}) collective-permute-start(bf16[48,128]{1,0:T(8,128)(2,1)S(1)} %fusion.23), channel_id=1, source_target_pairs={{8,0},{16,8},{24,16},{32,24},{40,32},{48,40},{56,48},{64,56},{72,6... | collective-permute-start | bytes 36872 | tf_op jit(solution)/shard_map/ppermute | solution.py:12
  1046.9 5.8 collective-permute-start.36
  1050.8 21.6 %collective-permute-start.37 = (bf16[48,128]{1,0:T(8,128)(2,1)S(1)}, bf16[48,128]{1,0:T(8,128)(2,1)S(1)}, u32[]{:S(2)}, u32[]{:S(2)}) collective-permute-start(bf16[48,128]{1,0:T(8,128)(2,1)S(1)} %fusion.24), channel_id=1, source_target_pairs={{16,0},{24,8},{32,16},{40,24},{48,32},{56,40},{64,48},{72,56},{80,... | collective-permute-start | bytes 36872 | tf_op jit(solution)/shard_map/ppermute | solution.py:12
  1090.9 7.6 collective-permute-start.38
  1096.9 21.2 %collective-permute-start.39 = (bf16[48,128]{1,0:T(8,128)(2,1)S(1)}, bf16[48,128]{1,0:T(8,128)(2,1)S(1)}, u32[]{:S(2)}, u32[]{:S(2)}) collective-permute-start(bf16[48,128]{1,0:T(8,128)(2,1)S(1)} %fusion.25), channel_id=1, source_target_pairs={{32,0},{40,8},{48,16},{56,24},{64,32},{72,40},{80,48},{88,56},{96,... | collective-permute-start | bytes 36872 | tf_op jit(solution)/shard_map/ppermute | solution.py:12
  1140.2 21.4 %collective-permute-start.41 = (bf16[48,128]{1,0:T(8,128)(2,1)S(1)}, bf16[48,128]{1,0:T(8,128)(2,1)S(1)}, u32[]{:S(2)}, u32[]{:S(2)}) collective-permute-start(bf16[48,128]{1,0:T(8,128)(2,1)S(1)} %fusion.26), channel_id=1, source_target_pairs={{64,0},{72,8},{80,16},{88,24},{96,32},{104,40},{112,48},{120,56},{... | collective-permute-start | bytes 36872 | tf_op jit(solution)/shard_map/ppermute | solution.py:12
  1179.6 13.1 collective-permute-start.42
  1191.2 21.2 %collective-permute-start.43 = (bf16[48,128]{1,0:T(8,128)(2,1)S(1)}, bf16[48,128]{1,0:T(8,128)(2,1)S(1)}, u32[]{:S(2)}, u32[]{:S(2)}) collective-permute-start(bf16[48,128]{1,0:T(8,128)(2,1)S(1)} %fusion.27), channel_id=1, source_target_pairs={{128,0},{136,8},{144,16},{152,24},{160,32},{168,40},{176,48},{184,... | collective-permute-start | bytes 36872 | tf_op jit(solution)/shard_map/ppermute | solution.py:12
  1231.2 161.9 %all-reduce.31.cloned.1.call-start = ((), (), s32[]{:S(2)}) async-start(), calls=%async_computation.8 | async-start | bytes 196608 | tf_op jit(solution)/shard_map/psum | solution.py:39
  1300.0 15.0 collective-permute-start.44
  1301.3 13.7 collective-permute-start.45
  1317.4 162.3 %all-reduce.33.cloned.1.call-start = ((), (), s32[]{:S(2)}) async-start(), calls=%async_computation.9 | async-start | bytes 196608 | tf_op jit(solution)/shard_map/psum | solution.py:39
  1393.1 7.5 collective-permute-start.46
  1394.4 6.8 collective-permute-start.47
  1403.1 160.5 %all-reduce.35.cloned.1.call-start = ((), (), s32[]{:S(2)}) async-start(), calls=%async_computation.10 | async-start | bytes 196608 | tf_op jit(solution)/shard_map/psum | solution.py:39
  1479.7 5.6 collective-permute-start.48
  1481.0 5.9 collective-permute-start.49
  1488.8 161.2 %all-reduce.37.cloned.1.call-start = ((), (), s32[]{:S(2)}) async-start(), calls=%async_computation.11 | async-start | bytes 196608 | tf_op jit(solution)/shard_map/psum | solution.py:39
  1563.6 7.1 collective-permute-start.50
  1564.9 7.4 collective-permute-start.51
  1574.2 161.6 %all-reduce.39.cloned.1.call-start = ((), (), s32[]{:S(2)}) async-start(), calls=%async_computation.12 | async-start | bytes 196608 | tf_op jit(solution)/shard_map/psum | solution.py:39
  1651.3 5.9 collective-permute-start.53
  1659.1 159.0 %all-reduce.41.cloned.1.call-start = ((), (), s32[]{:S(2)}) async-start(), calls=%async_computation.13 | async-start | bytes 196608 | tf_op jit(solution)/shard_map/psum | solution.py:39
  1735.8 5.7 collective-permute-start.54
  (29 other events, 634.3 us)
Sparse Core Ops, SparseCore 0:
  375.8 65.3 all-reduce.14
  458.1 75.5 all-reduce.16
  543.8 76.4 all-reduce.18
  629.5 74.7 all-reduce.20
  715.0 75.6 all-reduce.22
  799.9 76.4 all-reduce.24
  883.9 75.5 all-reduce.26
  1231.3 68.6 all-reduce.28
  1317.5 75.5 all-reduce.30
  1403.2 76.4 all-reduce.32
  1488.9 74.6 all-reduce.34
  1574.3 75.6 all-reduce.36
  1659.2 76.5 all-reduce.38
  1743.4 74.6 all-reduce.40
where the time goes:
time: 1840 us; the launch traced here: 1830 us
  waiting for transfers between devices  1080 us (59%)
  blocking collectives  293 us (16%)
  other arithmetic  192 us (10%)
  starting transfers between devices  185 us (10%)
  local copies, waits for them, and re-layouts  35.2 us (2%)
  matrix products  21.9 us (1%)
    psum x14, waiting for transfers between devices, assemble(): return lax.psum(partial_sum.astype(jnp.bfloat16), 'front')  1040 us
    ppermute x55, starting transfers between devices, passed_along(): lax.ppermute(value, axis, [(source, source + steps) for source in range(i...  185 us
    scatter-add x24, other arithmetic, scatter_columns(): return base.at[:, columns].add(-values.astype(jnp.float32))  172 us
    all_gather x12, blocking collectives, solve(): lax.all_gather(left_update, 'front', axis=1, tiled=True)  140 us
    all_gather x12, blocking collectives, solve(): lax.all_gather(right_update, 'front', axis=1, tiled=True)  139 us
    ppermute x55, waiting for transfers between devices, passed_along(): lax.ppermute(value, axis, [(source, source + steps) for source in range(i...  41.2 us
  transfers between devices with their start and end apart: 69, of which 35 were waited for; matrix products, arithmetic and copies ran while one was open for 4% of the time, Pallas kernels for 0%

commit v1 on v0

v1 whole, which is shorter than its diff:
```python
import jax
import jax.numpy as jnp
from jax import lax
from jax.sharding import PartitionSpec as P

CONTRACT_LAST = (((1,), (1,)), ((), ()))


def times_transposed(vectors, matrix):
    return lax.dot_general(vectors, matrix, CONTRACT_LAST, preferred_element_type=jnp.float32)


def times(vectors, matrix):
    return jnp.dot(vectors, matrix, preferred_element_type=jnp.float32)


def owners_at(height, groups):
    return [g for g in range(1, groups) if (g & -g) == 1 << (height - 1)]


def links(height, groups):
    owners = owners_at(height, groups)
    if height == 1:
        return [(g - 1, g) for g in owners], []
    offset = 2 ** (height - 2)
    return [(g - offset, g) for g in owners], [(g + offset, g) for g in owners]


def send(value, pairs):
    return lax.ppermute(value, "leaf", pairs)


def reverse(pairs):
    return [(b, a) for a, b in pairs]


def forward(leaf_r, node_r, leaf_up, node_up, is_first, levels, groups):
    update = times_transposed(leaf_r, leaf_up).astype(jnp.bfloat16)
    node_r = node_r.astype(jnp.float32)
    for height in range(1, levels + 1):
        left, right = links(height, groups)
        from_left = send(update, left).astype(jnp.float32)
        if height == 1:
            from_right = jnp.where(is_first, update.astype(jnp.float32), 0.0)
        else:
            from_right = send(update, right).astype(jnp.float32)
        node_r = node_r - from_left - from_right
        if height < levels:
            update = times_transposed(node_r.astype(jnp.bfloat16), node_up).astype(jnp.bfloat16)
    return node_r.astype(jnp.bfloat16)


def backward(leaf_t, node_t, leaf_up, node_up, is_first, levels, groups):
    node_x = node_t.astype(jnp.bfloat16)
    for height in range(levels, 1, -1):
        left, right = links(height, groups)
        z = send(node_x, reverse(left)) + send(node_x, reverse(right))
        new_x = (node_t - times(z, node_up)).astype(jnp.bfloat16)
        group = lax.axis_index("leaf")
        mine = (group & -group) == 1 << (height - 2)
        node_x = jnp.where(mine, new_x, node_x)
    left, _ = links(1, groups)
    z = jnp.where(is_first, node_x, send(node_x, reverse(left)))
    leaf_x = (leaf_t - times(z, leaf_up)).astype(jnp.bfloat16)
    return leaf_x, node_x


def solve(leaf_r, node_r, mats, is_first, levels, groups):
    leaf_up, node_up, leaf_inv, node_inv = mats
    node_r = forward(leaf_r, node_r, leaf_up, node_up, is_first, levels, groups)
    leaf_t = times(times_transposed(leaf_r, leaf_inv).astype(jnp.bfloat16), leaf_inv)
    node_t = times(times_transposed(node_r, node_inv).astype(jnp.bfloat16), node_inv)
    return backward(leaf_t, node_t, leaf_up, node_up, is_first, levels, groups)


def per_device(fields, direction, inverse_blocks, update_blocks, row_map, receivers, weights):
    groups = lax.axis_size("leaf")
    width = lax.axis_size("front")
    levels = groups.bit_length() - 1
    is_first = lax.axis_index("leaf") % 2 == 1
    sources, rows = fields.shape[1], fields.shape[2]
    share = sources // width
    whole = rows * width

    terms = (direction[:, None, :] * fields.astype(jnp.float32)).astype(jnp.bfloat16)
    packed = jnp.concatenate([fields, terms], 0).reshape(4, width, share, rows).transpose(1, 0, 2, 3)
    packed = lax.all_to_all(packed, "front", 0, 0, tiled=True)
    packed = packed.transpose(1, 2, 0, 3).reshape(4, share, whole)
    field_leaf, field_node, term_leaf, term_node = packed[0], packed[1], packed[2], packed[3]

    def gather(block):
        return lax.all_gather(block, "front", axis=0, tiled=True)

    def placed(matrix, columns):
        spots = (jnp.arange(whole)[:, None] == columns[None, :]).astype(jnp.bfloat16)
        return times(spots, matrix).astype(jnp.bfloat16)

    leaf_up = placed(gather(update_blocks[0]), row_map[0, 0])
    node_up = placed(gather(update_blocks[1]), row_map[1, 0])
    leaf_inv = gather(inverse_blocks[0])
    node_inv = gather(inverse_blocks[1])
    mats = (leaf_up, node_up, leaf_inv, node_inv)

    at_station = receivers[0][:, None] == jnp.arange(whole)[None, :]
    station_weight = jnp.sum(jnp.where(at_station, weights[0][:, None], 0.0), axis=0)

    delta_leaf, _ = solve(term_leaf, term_node, mats, is_first, levels, groups)
    injected = (delta_leaf.astype(jnp.float32) * station_weight[None, :]).astype(jnp.bfloat16)
    station = times_transposed(delta_leaf, at_station.astype(jnp.bfloat16))
    adj_leaf, adj_node = solve(injected, jnp.zeros_like(term_node), mats, is_first, levels, groups)
    curve_leaf = jnp.sum(field_leaf.astype(jnp.float32) * adj_leaf.astype(jnp.float32), axis=0)
    curve_node = jnp.sum(field_node.astype(jnp.float32) * adj_node.astype(jnp.float32), axis=0)

    curve = jnp.stack([curve_leaf, curve_node]).reshape(2, width, rows).transpose(1, 0, 2)
    out = jnp.concatenate([curve, jnp.broadcast_to(station[None], (width,) + station.shape)], axis=1)
    out = lax.all_to_all(out, "front", 0, 0, tiled=True)
    curvature = jnp.sum(out[:, :2], axis=0)
    data_change = out[:, 2:].reshape(sources, station.shape[1]).astype(jnp.bfloat16)
    return data_change, curvature


def solution(mesh):
    in_specs = (
        P(None, None, ("leaf", "front")),
        P(None, ("leaf", "front")),
        P(None, ("leaf", "front"), None),
        P(None, ("leaf", "front"), None),
        P(None, "leaf", None),
        P("leaf", None),
        P("leaf", None),
    )
    out_specs = (P(None, "leaf"), P(None, ("leaf", "front")))
    return jax.shard_map(
        per_device, mesh=mesh, in_specs=in_specs, out_specs=out_specs, check_vma=False
    )
```

time: 1840 us -> 257 us (0.14)
  waiting for transfers between devices: 1080 us -> 133 us
  blocking collectives: 293 us -> 20.6 us
  other arithmetic: 192 us -> 0.81 us
  starting transfers between devices: 185 us -> 45.8 us
  local copies, waits for them, and re-layouts: 35.2 us -> 5.12 us
    psum x14 -> x0, waiting for transfers between devices: 1040 us -> none  [assemble(): return lax.psum(partial_sum.astype(jnp.bfloat16), 'front')]
    all_gather x25 -> x0, blocking collectives: 293 us -> none  [the longest x12 140 us: solve(): lax.all_gather(left_update, 'front', axis=1, tiled=True)]
    scatter-add x25 -> x0, other arithmetic: 173 us -> none  [the longest x24 172 us: scatter_columns(): return base.at[:, columns].add(-values.astype(jnp.float32))]
    ppermute x55 -> x44, starting transfers between devices: 185 us -> 35.6 us  [send(): return lax.ppermute(value, 'leaf', pairs)]
    all_gather x0 -> x4, waiting for transfers between devices: none -> 92.2 us  [gather(): return lax.all_gather(block, 'front', axis=0, tiled=True)]
    all_to_all x0 -> x1, blocking collectives: none -> 20.6 us  [per_device(): out = lax.all_to_all(out, 'front', 0, 0, tiled=True)]
    ppermute x55 -> x44, waiting for transfers between devices: 41.2 us -> 34.9 us  [send(): return lax.ppermute(value, 'leaf', pairs)]
  transfers between devices with their start and end apart: 69 -> 49, of which waited for: 35 -> 7; matrix products, arithmetic and copies ran while one was open for 4% -> 10% of each run, Pallas kernels for 0% -> 0%
where the time goes in v1:
time: 257 us; the launch traced here: 254 us
  waiting for transfers between devices  133 us (52%)
  starting transfers between devices  45.8 us (18%)
  matrix products  34.8 us (14%)
  blocking collectives  20.6 us (8%)
  between operations  14.7 us (6%)
  local copies, waits for them, and re-layouts  5.12 us (2%)
    all_gather x4, waiting for transfers between devices, gather(): return lax.all_gather(block, 'front', axis=0, tiled=True)  92.2 us
    ppermute x44, starting transfers between devices, send(): return lax.ppermute(value, 'leaf', pairs)  35.6 us
    ppermute x44, waiting for transfers between devices, send(): return lax.ppermute(value, 'leaf', pairs)  34.9 us
    dot_general x18, matrix products, times(): return jnp.dot(vectors, matrix, preferred_element_type=jnp.float32)  26.9 us
    all_to_all x1, blocking collectives, per_device(): out = lax.all_to_all(out, 'front', 0, 0, tiled=True)  20.6 us
    all_to_all x1, starting transfers between devices, per_device(): packed = lax.all_to_all(packed, 'front', 0, 0, tiled=True)  10.1 us
    dot_general x13, matrix products, times_transposed(): lax.dot_general(vectors, matrix, CONTRACT_LAST, preferred_element_type=jn...  7.97 us
  transfers between devices with their start and end apart: 49, of which 7 were waited for; matrix products, arithmetic and copies ran while one was open for 10% of the time, Pallas kernels for 0%

profile of v1, /device:TPU:1, one launch (start us, length us, event | category | flops | bytes accessed | tf_op | source)
XLA Modules:
  0.0 254.4 jit_solution(5102660309153354956)
XLA Ops:
  7.2 1.9 fusion.113
  9.2 0.7 all-gather.13.cloned.1.call-update
  9.9 1.9 fusion.114
  12.5 10.1 %all-to-all-start = ((bf16[8,4,6,128]{3,1,2,0:T(4,128)(2,1)}), bf16[8,4,6,128]{3,1,2,0:T(4,128)(2,1)S(1)}, u32[]{:S(2)}, u32[]{:S(2)}) async-start(bf16[8,4,6,128]{3,1,2,0:T(4,128)(2,1)} %bitcast.1), calls=%async_computation | async-start | bytes 98304 | tf_op jit(solution)/shard_map/all_to_all | solution.py:87
  23.2 4.2 %all-to-all-done = bf16[8,4,6,128]{3,1,2,0:T(4,128)(2,1)S(1)} async-done(((bf16[8,4,6,128]{3,1,2,0:T(4,128)(2,1)}), bf16[8,4,6,128]{3,1,2,0:T(4,128)(2,1)S(1)}, u32[]{:S(2)}, u32[]{:S(2)}) %all-to-all-start) | async-done | bytes 49184 | tf_op jit(solution)/shard_map/all_to_all | solution.py:87
  27.5 21.3 %all-gather.11.cloned.1.call-done = bf16[1,1024,1024]{2,1,0:T(8,128)(2,1)} async-done(((bf16[1,128,1024]{2,1,0:T(8,128)(2,1)}), bf16[1,1024,1024]{2,1,0:T(8,128)(2,1)}) %all-gather.11.cloned.1.call-update) | async-done | bytes 2097168 | tf_op jit(solution)/shard_map/all_gather | solution.py:92
  48.8 3.9 %fusion.25 = bf16[1024,1024]{1,0:T(8,128)(2,1)S(1)} fusion(bf16[1,1024,1024]{2,1,0:T(8,128)(2,1)} %all-gather.11.cloned.1.call-done, s32[1024]{0:T(1024)S(1)} %bitcast.131), kind=kOutput, calls=%fused_computation.25 | convolution fusion | flops 2149580800 | bytes 4198400 | tf_op jit(solution)/shard_map/dot_general | solution.py:14
  53.4 3.1 %collective-permute-start = (bf16[6,1024]{1,0:T(8,128)(2,1)S(1)}, bf16[6,1024]{1,0:T(8,128)(2,1)S(1)}, u32[]{:S(2)}, u32[]{:S(2)}) collective-permute-start(bf16[6,1024]{1,0:T(8,128)(2,1)S(1)} %convolution_convert_fusion.11), channel_id=1, source_target_pairs={{0,8},{16,24},{32,40},{48,56},{64,72},{80,88},{96,104},{112,120},{... | collective-permute-start | bytes 36872 | tf_op jit(solution)/shard_map/ppermute | solution.py:30
  56.5 27.7 %all-gather.13.cloned.1.call-done = bf16[1,1024,1024]{2,1,0:T(8,128)(2,1)} async-done(((bf16[1,128,1024]{2,1,0:T(8,128)(2,1)}), bf16[1,1024,1024]{2,1,0:T(8,128)(2,1)}) %all-gather.13.cloned.1.call-update) | async-done | bytes 2097168 | tf_op jit(solution)/shard_map/all_gather | solution.py:92
  84.2 3.9 %fusion.22 = bf16[1024,1024]{1,0:T(8,128)(2,1)S(1)} fusion(bf16[1,1024,1024]{2,1,0:T(8,128)(2,1)} %all-gather.13.cloned.1.call-done, s32[1024]{0:T(1024)S(1)} %bitcast.130), kind=kOutput, calls=%fused_computation.24 | convolution fusion | flops 2149580800 | bytes 4198400 | tf_op jit(solution)/shard_map/dot_general | solution.py:14
  88.8 0.7 collective-permute-start.1
  89.5 0.7 collective-permute-start.2
  90.8 0.7 collective-permute-start.3
  91.5 0.7 collective-permute-start.4
  92.8 0.7 collective-permute-start.5
  93.5 0.7 collective-permute-start.6
  94.8 0.7 collective-permute-start.7
  95.5 0.7 collective-permute-start.8
  96.2 0.6 convolution_convert_fusion.6
  96.8 0.7 collective-permute-start.10
  97.5 0.7 collective-permute-start.9
  98.2 21.4 %all-gather.15.cloned.1.call-done = bf16[1,1024,1024]{2,1,0:T(8,128)(2,1)} async-done(((bf16[1,128,1024]{2,1,0:T(8,128)(2,1)}), bf16[1,1024,1024]{2,1,0:T(8,128)(2,1)}) %all-gather.15.cloned.1.call-update) | async-done | bytes 2097168 | tf_op jit(solution)/shard_map/all_gather | solution.py:92
  119.6 3.2 %fusion.116 = (bf16[6,1024]{1,0:T(8,128)(2,1)S(1)}, f32[6,1024]{1,0:T(8,128)S(1)}) fusion(bf16[1,1024,1024]{2,1,0:T(8,128)(2,1)} %all-gather.15.cloned.1.call-done, bf16[6,1024]{1,0:T(8,128)(2,1)S(1)} %collective-permute-done.10, bf16[6,1024]{1,0:T(8,128)(2,1)S(1)} %collective-permute-done.9, bf16[6,1024]{1,0:T(8,128)(2,1)S(1)} %collective-permute-done.8, ...), kind=kOutput, calls=%fused_computation.144 | convolution fusion | flops 25257984 | bytes 2232320 | tf_op jit(solution)/shard_map/dot_general | solution.py:14
  122.8 0.7 collective-permute-start.11
  123.4 0.7 collective-permute-start.12
  124.5 0.7 collective-permute-start.13
  125.2 0.7 collective-permute-start.14
  126.3 0.7 collective-permute-start.15
  126.9 0.7 collective-permute-start.16
  128.0 0.7 collective-permute-start.17
  128.7 0.7 collective-permute-start.18
  129.8 0.7 collective-permute-start.19
  130.4 0.7 collective-permute-start.20
  131.7 1.5 collective-permute-start.21
  133.2 21.7 %all-gather.9.cloned.1.call-done = bf16[1,1024,1024]{2,1,0:T(8,128)(2,1)} async-done(((bf16[1,128,1024]{2,1,0:T(8,128)(2,1)}), bf16[1,1024,1024]{2,1,0:T(8,128)(2,1)}) %all-gather.9.cloned.1.call-update) | async-done | bytes 2097168 | tf_op jit(solution)/shard_map/all_gather | solution.py:92
  154.8 3.2 %fusion.16 = f32[6,1024]{1,0:T(8,128)S(1)} fusion(bf16[1,1024,1024]{2,1,0:T(8,128)(2,1)} %all-gather.9.cloned.1.call-done, bf16[1,6,8,128]{3,2,1,0:T(8,128)(2,1)S(1)} %get-tuple-element.9), kind=kOutput, calls=%fused_computation.18 | convolution fusion | flops 25171968 | bytes 2134016 | tf_op jit(solution)/shard_map/dot_general | solution.py:14
  158.0 2.1 fusion.33
  160.9 3.1 %collective-permute-start.22 = (bf16[6,1024]{1,0:T(8,128)(2,1)S(1)}, bf16[6,1024]{1,0:T(8,128)(2,1)S(1)}, u32[]{:S(2)}, u32[]{:S(2)}) collective-permute-start(bf16[6,1024]{1,0:T(8,128)(2,1)S(1)} %convolution_convert_fusion.5), channel_id=1, source_target_pairs={{0,8},{16,24},{32,40},{48,56},{64,72},{80,88},{96,104},{112,120},{... | collective-permute-start | bytes 36872 | tf_op jit(solution)/shard_map/ppermute | solution.py:30
  164.0 0.9 collective-permute-done.22
  165.5 0.7 collective-permute-start.23
  166.1 0.7 collective-permute-start.24
  167.5 0.7 collective-permute-start.25
  168.2 0.7 collective-permute-start.26
  169.5 0.7 collective-permute-start.27
  170.2 0.7 collective-permute-start.28
  171.5 0.7 collective-permute-start.29
  172.2 0.7 collective-permute-start.30
  173.6 0.7 collective-permute-start.31
  174.2 0.7 collective-permute-start.32
  174.9 3.2 %fusion.119 = (bf16[6,1024]{1,0:T(8,128)(2,1)S(1)}, f32[6,1024]{1,0:T(8,128)S(1)}) fusion(bf16[1,1024,1024]{2,1,0:T(8,128)(2,1)} %all-gather.15.cloned.1.call-done, bf16[6,1024]{1,0:T(8,128)(2,1)S(1)} %collective-permute-done.32, bf16[6,1024]{1,0:T(8,128)(2,1)S(1)} %collective-permute-done.31, bf16[6,1024]{1,0:T(8,128)(2,1)S(1)} %collective-permute-done.30, ...), kind=kOutput, calls=%fused_computation.145 | convolution fusion | flops 25233408 | bytes 2207744 | tf_op jit(solution)/shard_map/dot_general | solution.py:14
  178.1 0.7 collective-permute-start.33
  178.7 0.7 collective-permute-start.34
  179.8 0.7 collective-permute-start.35
  180.5 0.7 collective-permute-start.36
  181.6 0.7 collective-permute-start.37
  182.2 0.7 collective-permute-start.38
  183.3 0.7 collective-permute-start.39
  184.0 0.7 collective-permute-start.40
  185.0 0.7 collective-permute-start.41
  185.7 0.7 collective-permute-start.42
  186.4 3.2 %fusion.12 = f32[6,1024]{1,0:T(8,128)S(1)} fusion(bf16[1,1024,1024]{2,1,0:T(8,128)(2,1)} %all-gather.9.cloned.1.call-done, bf16[6,1024]{1,0:T(8,128)(2,1)S(1)} %fusion.33, f32[1024]{0:T(1024)S(1)} %select_reduce_fusion), kind=kOutput, calls=%fused_computation.14 | convolution fusion | flops 25190400 | bytes 2138112 | tf_op jit(solution)/shard_map/dot_general | solution.py:14
  190.0 1.4 collective-permute-start.43
  191.7 34.0 %collective-permute-done.43 = bf16[6,1024]{1,0:T(8,128)(2,1)S(1)} collective-permute-done((bf16[6,1024]{1,0:T(8,128)(2,1)S(1)}, bf16[6,1024]{1,0:T(8,128)(2,1)S(1)}, u32[]{:S(2)}, u32[]{:S(2)}) %collective-permute-start.43) | collective-permute-done | bytes 12320 | tf_op jit(solution)/shard_map/ppermute | solution.py:30
  226.1 20.6 %all_to_all.10 = f32[8,8,128]{2,1,0:T(8,128)S(1)} all-to-all(f32[8,8,128]{2,1,0:T(8,128)S(1)} %pad_maximum_fusion.1), channel_id=1, replica_groups=mesh['leaf'=64,'front'=8] {'front'}, dimensions={0} | all-to-all | bytes 65536 | tf_op jit(solution)/shard_map/all_to_all | solution.py:116
  (104 shorter events, 14.6 us)
Async XLA Ops:
  7.2 4.7 %copy-start.3 = (bf16[2,48,128]{2,1,0:T(8,128)(2,1)S(1)}, bf16[2,48,128]{2,1,0:T(8,128)(2,1)}, u32[]{:S(2)}) copy-start(bf16[2,48,128]{2,1,0:T(8,128)(2,1)} %param.7) | copy-start | bytes 73732
  7.2 4.7 %copy-start.5 = (f32[2,128]{1,0:T(2,128)S(1)}, f32[2,128]{1,0:T(2,128)}, u32[]{:S(2)}) copy-start(f32[2,128]{1,0:T(2,128)} %param.8) | copy-start | bytes 3076
  7.2 16.0 %copy-start.4 = (s32[2,1,1024]{2,1,0:T(1,128)S(1)}, s32[2,1,1024]{2,1,0:T(1,128)}, u32[]{:S(2)}) copy-start(s32[2,1,1024]{2,1,0:T(1,128)} %param.11) | copy-start | bytes 24580
  7.2 41.6 %all-gather.11.cloned.1.call-start = ((), (), s32[]{:S(2)}) async-start(), calls=%async_computation.3 | async-start | bytes 2359296 | tf_op jit(solution)/shard_map/all_gather | solution.py:92
  9.1 75.1 %all-gather.13.cloned.1.call-start = ((), (), s32[]{:S(2)}) async-start(), calls=%async_computation.4 | async-start | bytes 2359296 | tf_op jit(solution)/shard_map/all_gather | solution.py:92
  9.9 109.7 %all-gather.15.cloned.1.call-start = ((), (), s32[]{:S(2)}) async-start(), calls=%async_computation.5 | async-start | bytes 2359296 | tf_op jit(solution)/shard_map/all_gather | solution.py:92
  12.5 14.9 %all-to-all-start = ((bf16[8,4,6,128]{3,1,2,0:T(4,128)(2,1)}), bf16[8,4,6,128]{3,1,2,0:T(4,128)(2,1)S(1)}, u32[]{:S(2)}, u32[]{:S(2)}) async-start(bf16[8,4,6,128]{3,1,2,0:T(4,128)(2,1)} %bitcast.1), calls=%async_computation | async-start | bytes 98304 | tf_op jit(solution)/shard_map/all_to_all | solution.py:87
  22.6 132.2 %all-gather.9.cloned.1.call-start = ((), (), s32[]{:S(2)}) async-start(), calls=%async_computation.2 | async-start | bytes 2359296 | tf_op jit(solution)/shard_map/all_gather | solution.py:92
  52.7 31.5 %copy-start = (bf16[1024,1024]{1,0:T(8,128)(2,1)}, bf16[1024,1024]{1,0:T(8,128)(2,1)S(1)}, u32[]{:S(2)}) copy-start(bf16[1024,1024]{1,0:T(8,128)(2,1)S(1)} %fusion.25) | copy-start | bytes 6291460
  53.4 34.8 %collective-permute-start = (bf16[6,1024]{1,0:T(8,128)(2,1)S(1)}, bf16[6,1024]{1,0:T(8,128)(2,1)S(1)}, u32[]{:S(2)}, u32[]{:S(2)}) collective-permute-start(bf16[6,1024]{1,0:T(8,128)(2,1)S(1)} %convolution_convert_fusion.11), channel_id=1, source_target_pairs={{0,8},{16,24},{32,40},{48,56},{64,72},{80,88},{96,104},{112,120},{... | collective-permute-start | bytes 36872 | tf_op jit(solution)/shard_map/ppermute | solution.py:30
  88.8 1.3 collective-permute-start.1
  89.5 0.7 collective-permute-start.2
  90.8 1.3 collective-permute-start.3
  91.5 0.7 collective-permute-start.4
  92.8 1.3 collective-permute-start.5
  93.5 0.7 collective-permute-start.6
  94.8 1.3 collective-permute-start.7
  95.5 0.7 collective-permute-start.8
  96.8 22.8 %collective-permute-start.10 = (bf16[6,1024]{1,0:T(8,128)(2,1)S(1)}, bf16[6,1024]{1,0:T(8,128)(2,1)S(1)}, u32[]{:S(2)}, u32[]{:S(2)}) collective-permute-start(bf16[6,1024]{1,0:T(8,128)(2,1)S(1)} %convolution_convert_fusion.6), channel_id=1, source_target_pairs={{384,256},{385,257},{386,258},{387,259},{388,260},{389,261},{390,2... | collective-permute-start | bytes 36872 | tf_op jit(solution)/shard_map/ppermute | solution.py:30
  97.5 22.1 %collective-permute-start.9 = (bf16[6,1024]{1,0:T(8,128)(2,1)S(1)}, bf16[6,1024]{1,0:T(8,128)(2,1)S(1)}, u32[]{:S(2)}, u32[]{:S(2)}) collective-permute-start(bf16[6,1024]{1,0:T(8,128)(2,1)S(1)} %convolution_convert_fusion.6), channel_id=1, source_target_pairs={{128,256},{129,257},{130,258},{131,259},{132,260},{133,261},{134,2... | collective-permute-start | bytes 36872 | tf_op jit(solution)/shard_map/ppermute | solution.py:30
  122.8 1.3 collective-permute-start.11
  123.4 0.7 collective-permute-start.12
  124.5 1.3 collective-permute-start.13
  125.2 0.7 collective-permute-start.14
  126.3 1.4 collective-permute-start.15
  126.9 0.7 collective-permute-start.16
  127.6 3.5 %copy-start.6 = (f32[1,128]{1,0:T(1,128)S(1)}, f32[1,128]{1,0:T(1,128)}, u32[]{:S(2)}) copy-start(f32[1,128]{1,0:T(1,128)} %param.13) | copy-start | bytes 1540
  127.6 3.5 %copy-start.7 = (s32[1,128]{1,0:T(1,128)S(1)}, s32[1,128]{1,0:T(1,128)}, u32[]{:S(2)}) copy-start(s32[1,128]{1,0:T(1,128)} %param.12) | copy-start | bytes 1540
  128.0 1.3 collective-permute-start.17
  128.7 0.7 collective-permute-start.18
  129.8 1.5 collective-permute-start.19
  130.4 0.8 collective-permute-start.20
  131.7 26.3 %collective-permute-start.21 = (bf16[6,1024]{1,0:T(8,128)(2,1)S(1)}, bf16[6,1024]{1,0:T(8,128)(2,1)S(1)}, u32[]{:S(2)}, u32[]{:S(2)}) collective-permute-start(bf16[6,1024]{1,0:T(8,128)(2,1)S(1)} %fusion.68), channel_id=1, source_target_pairs={{8,0},{24,16},{40,32},{56,48},{72,64},{88,80},{104,96},{120,112},{... | collective-permute-start | bytes 36872 | tf_op jit(solution)/shard_map/ppermute | solution.py:30
  158.0 2.2 copy-start.1
  160.9 4.0 %collective-permute-start.22 = (bf16[6,1024]{1,0:T(8,128)(2,1)S(1)}, bf16[6,1024]{1,0:T(8,128)(2,1)S(1)}, u32[]{:S(2)}, u32[]{:S(2)}) collective-permute-start(bf16[6,1024]{1,0:T(8,128)(2,1)S(1)} %convolution_convert_fusion.5), channel_id=1, source_target_pairs={{0,8},{16,24},{32,40},{48,56},{64,72},{80,88},{96,104},{112,120},{... | collective-permute-start | bytes 36872 | tf_op jit(solution)/shard_map/ppermute | solution.py:30
  165.5 1.3 collective-permute-start.23
  166.1 0.7 collective-permute-start.24
  167.5 1.3 collective-permute-start.25
  168.2 0.7 collective-permute-start.26
  169.5 1.3 collective-permute-start.27
  170.2 0.7 collective-permute-start.28
  171.5 1.3 collective-permute-start.29
  172.2 0.7 collective-permute-start.30
  173.6 1.3 collective-permute-start.31
  174.2 0.7 collective-permute-start.32
  178.1 1.3 collective-permute-start.33
  178.7 0.7 collective-permute-start.34
  179.8 1.3 collective-permute-start.35
  180.5 0.7 collective-permute-start.36
  181.6 1.3 collective-permute-start.37
  182.2 0.7 collective-permute-start.38
  183.3 1.3 collective-permute-start.39
  184.0 0.7 collective-permute-start.40
  185.0 4.5 %collective-permute-start.41 = (bf16[6,1024]{1,0:T(8,128)(2,1)S(1)}, bf16[6,1024]{1,0:T(8,128)(2,1)S(1)}, u32[]{:S(2)}, u32[]{:S(2)}) collective-permute-start(bf16[6,1024]{1,0:T(8,128)(2,1)S(1)} %fusion.64), channel_id=1, source_target_pairs={{16,8},{48,40},{80,72},{112,104},{144,136},{176,168},{208,200},{24... | collective-permute-start | bytes 36872 | tf_op jit(solution)/shard_map/ppermute | solution.py:30
  185.7 3.8 %collective-permute-start.42 = (bf16[6,1024]{1,0:T(8,128)(2,1)S(1)}, bf16[6,1024]{1,0:T(8,128)(2,1)S(1)}, u32[]{:S(2)}, u32[]{:S(2)}) collective-permute-start(bf16[6,1024]{1,0:T(8,128)(2,1)S(1)} %fusion.64), channel_id=1, source_target_pairs={{16,24},{48,56},{80,88},{112,120},{144,152},{176,184},{208,216},{2... | collective-permute-start | bytes 36872 | tf_op jit(solution)/shard_map/ppermute | solution.py:30
  189.5 36.1 %copy-start.2 = (bf16[1024,1024]{1,0:T(8,128)(2,1)S(1)}, bf16[1024,1024]{1,0:T(8,128)(2,1)}, u32[]{:S(2)}) copy-start(bf16[1024,1024]{1,0:T(8,128)(2,1)} %copy-done) | copy-start | bytes 6291460
  190.0 35.7 %collective-permute-start.43 = (bf16[6,1024]{1,0:T(8,128)(2,1)S(1)}, bf16[6,1024]{1,0:T(8,128)(2,1)S(1)}, u32[]{:S(2)}, u32[]{:S(2)}) collective-permute-start(bf16[6,1024]{1,0:T(8,128)(2,1)S(1)} %get-tuple-element.17), channel_id=1, source_target_pairs={{8,0},{24,16},{40,32},{56,48},{72,64},{88,80},{104,96},{120,112},{... | collective-permute-start | bytes 36872 | tf_op jit(solution)/shard_map/ppermute | solution.py:30
Sparse Core Ops, SparseCore 0:
  10.2 38.5 all-gather.10
  50.9 33.2 all-gather.12
  86.4 33.2 all-gather.14
  121.6 33.1 all-gather.8

commit v2 on v1

--- a/solution.py
+++ b/solution.py
@@ -34,8 +34,7 @@
     return [(b, a) for a, b in pairs]
 
 
-def forward(leaf_r, node_r, leaf_up, node_up, is_first, levels, groups):
-    update = times_transposed(leaf_r, leaf_up).astype(jnp.bfloat16)
+def forward(update, node_r, node_up, is_first, levels, groups):
     node_r = node_r.astype(jnp.float32)
     for height in range(1, levels + 1):
         left, right = links(height, groups)
@@ -65,12 +64,25 @@
     return leaf_x, node_x
 
 
-def solve(leaf_r, node_r, mats, is_first, levels, groups):
-    leaf_up, node_up, leaf_inv, node_inv = mats
-    node_r = forward(leaf_r, node_r, leaf_up, node_up, is_first, levels, groups)
-    leaf_t = times(times_transposed(leaf_r, leaf_inv).astype(jnp.bfloat16), leaf_inv)
-    node_t = times(times_transposed(node_r, node_inv).astype(jnp.bfloat16), node_inv)
-    return backward(leaf_t, node_t, leaf_up, node_up, is_first, levels, groups)
+def gather_rows(block):
+    count = lax.axis_size("front")
+
+    def shifted(by):
+        return lax.ppermute(block, "front", [(f, (f + by) % count) for f in range(count)])
+
+    near = [block, shifted(2), shifted(-2), shifted(4)] if count == 8 else [block]
+    near = jnp.concatenate(near, 0)
+    far = lax.ppermute(near, "front", [(f, f ^ 1) for f in range(count)])
+    return jnp.concatenate([near, far], 0)
+
+
+def gathered_order(columns):
+    count = lax.axis_size("front")
+    here = lax.axis_index("front")
+    steps = jnp.array([0, -2, 2, 4] if count == 8 else [0])
+    near = (here + steps) % count
+    order = jnp.concatenate([near, near ^ 1])
+    return columns.reshape(count, -1)[order].reshape(-1)
 
 
 def per_device(fields, direction, inverse_blocks, update_blocks, row_map, receivers, weights):
@@ -82,32 +94,55 @@
     share = sources // width
     whole = rows * width
 
+    def own(axis_rows):
+        return axis_rows.transpose(1, 0, 2).reshape(axis_rows.shape[1], whole)
+
     terms = (direction[:, None, :] * fields.astype(jnp.float32)).astype(jnp.bfloat16)
     packed = jnp.concatenate([fields, terms], 0).reshape(4, width, share, rows).transpose(1, 0, 2, 3)
+    packed = packed.reshape(width, 4 * share, rows)
+    packed = jnp.concatenate([packed, jnp.broadcast_to(terms[:1], (width, sources, rows))], 1)
     packed = lax.all_to_all(packed, "front", 0, 0, tiled=True)
-    packed = packed.transpose(1, 2, 0, 3).reshape(4, share, whole)
-    field_leaf, field_node, term_leaf, term_node = packed[0], packed[1], packed[2], packed[3]
+    leaf_all = own(packed[:, 4 * share :])
+    field_leaf, field_node, term_leaf, term_node = [
+        own(packed[:, k * share : (k + 1) * share]) for k in range(4)
+    ]
 
-    def gather(block):
-        return lax.all_gather(block, "front", axis=0, tiled=True)
+    node_rows = gather_rows(update_blocks[1])
+    later = jnp.stack([inverse_blocks[1], inverse_blocks[0], update_blocks[0]])
+    later = lax.all_gather(later, "front", axis=0)
 
-    def placed(matrix, columns):
-        spots = (jnp.arange(whole)[:, None] == columns[None, :]).astype(jnp.bfloat16)
-        return times(spots, matrix).astype(jnp.bfloat16)
+    def spots(columns):
+        return (jnp.arange(whole)[:, None] == columns[None, :]).astype(jnp.bfloat16)
 
-    leaf_up = placed(gather(update_blocks[0]), row_map[0, 0])
-    node_up = placed(gather(update_blocks[1]), row_map[1, 0])
-    leaf_inv = gather(inverse_blocks[0])
-    node_inv = gather(inverse_blocks[1])
-    mats = (leaf_up, node_up, leaf_inv, node_inv)
+    def squared(blocks):
+        return lax.dot_general(
+            blocks, blocks, (((0, 1), (0, 1)), ((), ())), preferred_element_type=jnp.float32
+        ).astype(jnp.bfloat16)
+
+    leaf_spots = spots(row_map[0, 0])
+    node_up = times(spots(gathered_order(row_map[1, 0])), node_rows).astype(jnp.bfloat16)
 
     at_station = receivers[0][:, None] == jnp.arange(whole)[None, :]
     station_weight = jnp.sum(jnp.where(at_station, weights[0][:, None], 0.0), axis=0)
 
-    delta_leaf, _ = solve(term_leaf, term_node, mats, is_first, levels, groups)
+    update = times_transposed(leaf_all, update_blocks[0]).astype(jnp.bfloat16)
+    update = lax.all_to_all(update.reshape(width, share, rows), "front", 0, 0, tiled=True)
+    update = times_transposed(own(update), leaf_spots).astype(jnp.bfloat16)
+    node_r = forward(update, term_node, node_up, is_first, levels, groups)
+    node_inv = squared(later[:, 0])
+    leaf_inv = squared(later[:, 1])
+    leaf_up = times(leaf_spots, later[:, 2].reshape(whole, whole)).astype(jnp.bfloat16)
+    node_t = times(node_r, node_inv)
+    leaf_t = times(term_leaf, leaf_inv)
+    delta_leaf, _ = backward(leaf_t, node_t, leaf_up, node_up, is_first, levels, groups)
     injected = (delta_leaf.astype(jnp.float32) * station_weight[None, :]).astype(jnp.bfloat16)
     station = times_transposed(delta_leaf, at_station.astype(jnp.bfloat16))
-    adj_leaf, adj_node = solve(injected, jnp.zeros_like(term_node), mats, is_first, levels, groups)
+
+    update = times_transposed(injected, leaf_up).astype(jnp.bfloat16)
+    node_r = forward(update, jnp.zeros_like(term_node), node_up, is_first, levels, groups)
+    node_t = times(node_r, node_inv)
+    leaf_t = times(injected, leaf_inv)
+    adj_leaf, adj_node = backward(leaf_t, node_t, leaf_up, node_up, is_first, levels, groups)
     curve_leaf = jnp.sum(field_leaf.astype(jnp.float32) * adj_leaf.astype(jnp.float32), axis=0)
     curve_node = jnp.sum(field_node.astype(jnp.float32) * adj_node.astype(jnp.float32), axis=0)
 

time: 257 us -> 226 us (0.88)
  waiting for transfers between devices: 133 us -> 73.4 us
  starting transfers between devices: 45.8 us -> 59.8 us
  local copies, waits for them, and re-layouts: 5.12 us -> 13.8 us
  blocking collectives: 20.6 us -> 27.2 us
  other arithmetic: 0.81 us -> 4.46 us
  matrix products: 34.8 us -> 31.4 us
    all_gather x4 -> x1, waiting for transfers between devices: 92.2 us -> 0.02 us  [per_device(): later = lax.all_gather(later, 'front', axis=0)]
    ppermute x44, waiting for transfers between devices: 34.9 us -> 71 us  [send(): return lax.ppermute(value, 'leaf', pairs)]
    dot_general x18, matrix products: 26.9 us -> 12.5 us  [times(): return jnp.dot(vectors, matrix, preferred_element_type=jnp.float32)]
    ppermute x0 -> x4, starting transfers between devices: none -> 13.7 us  [the longest x3 10.9 us: shifted(): lax.ppermute(block, 'front', [(f, (f + by) % count) for f in range(count)])]
    dot_general x0 -> x2, matrix products: none -> 9.23 us  [squared(): lax.dot_general(blocks, blocks, (((0, 1), (0, 1)), ((), ())), preferred_e...]
    all_to_all x1, blocking collectives: 20.6 us -> 27.2 us  [per_device(): out = lax.all_to_all(out, 'front', 0, 0, tiled=True)]
    all_to_all x1, waiting for transfers between devices: 4.21 us -> 0.01 us  [per_device(): packed = lax.all_to_all(packed, 'front', 0, 0, tiled=True)]
    unnamed x16 -> x24, local copies, waits for them, and re-layouts: 0.13 us -> 4.28 us
  transfers between devices with their start and end apart: 49 -> 51, of which waited for: 7 -> 4; matrix products, arithmetic and copies ran while one was open for 10% -> 15% of each run, Pallas kernels for 0% -> 0%
where the time goes in v2:
time: 226 us; the launch traced here: 225 us
  waiting for transfers between devices  73.4 us (32%)
  starting transfers between devices  59.8 us (26%)
  matrix products  31.4 us (14%)
  blocking collectives  27.2 us (12%)
  between operations  15.1 us (7%)
  local copies, waits for them, and re-layouts  13.8 us (6%)
  other arithmetic  4.46 us (2%)
    ppermute x44, waiting for transfers between devices, send(): return lax.ppermute(value, 'leaf', pairs)  71 us
    ppermute x44, starting transfers between devices, send(): return lax.ppermute(value, 'leaf', pairs)  32.3 us
    all_to_all x1, blocking collectives, per_device(): out = lax.all_to_all(out, 'front', 0, 0, tiled=True)  27.2 us
    dot_general x18, matrix products, times(): return jnp.dot(vectors, matrix, preferred_element_type=jnp.float32)  12.5 us
    ppermute x3, starting transfers between devices, shifted(): lax.ppermute(block, 'front', [(f, (f + by) % count) for f in range(count)])  10.9 us
    all_to_all x1, starting transfers between devices, per_device(): packed = lax.all_to_all(packed, 'front', 0, 0, tiled=True)  9.71 us
    dot_general x14, matrix products, times_transposed(): lax.dot_general(vectors, matrix, CONTRACT_LAST, preferred_element_type=jn...  9.61 us
    dot_general x2, matrix products, squared(): lax.dot_general(blocks, blocks, (((0, 1), (0, 1)), ((), ())), preferred_e...  9.23 us
  transfers between devices with their start and end apart: 51, of which 4 were waited for; matrix products, arithmetic and copies ran while one was open for 15% of the time, Pallas kernels for 0%

profile of v2, /device:TPU:1, one launch (start us, length us, event | category | flops | bytes accessed | tf_op | source)
XLA Modules:
  0.0 225.1 jit_solution(687623303916798383)
XLA Ops:
  7.2 1.1 slice_bitcast_fusion.4
  8.3 1.1 fusion.82
  9.5 1.0 pad_maximum_fusion.1
  10.5 4.1 %collective-permute-start.1 = (bf16[128,1024]{1,0:T(8,128)(2,1)S(1)}, bf16[128,1024]{1,0:T(8,128)(2,1)S(1)}, u32[]{:S(2)}, u32[]{:S(2)}) collective-permute-start(bf16[128,1024]{1,0:T(8,128)(2,1)S(1)} %get-tuple-element.4), channel_id=1, source_target_pairs={{0,2},{1,3},{2,4},{3,5},{4,6},{5,7},{6,0},{7,1},{8,10},{9,11},{10,... | collective-permute-start | bytes 786440 | tf_op jit(solution)/shard_map/ppermute | solution.py:71
  14.5 3.3 %collective-permute-start.2 = (bf16[128,1024]{1,0:T(8,128)(2,1)S(1)}, bf16[128,1024]{1,0:T(8,128)(2,1)S(1)}, u32[]{:S(2)}, u32[]{:S(2)}) collective-permute-start(bf16[128,1024]{1,0:T(8,128)(2,1)S(1)} %get-tuple-element.4), channel_id=1, source_target_pairs={{0,6},{1,7},{2,0},{3,1},{4,2},{5,3},{6,4},{7,5},{8,14},{9,15},{10,... | collective-permute-start | bytes 786440 | tf_op jit(solution)/shard_map/ppermute | solution.py:71
  17.9 3.5 %collective-permute-start.3 = (bf16[128,1024]{1,0:T(8,128)(2,1)S(1)}, bf16[128,1024]{1,0:T(8,128)(2,1)S(1)}, u32[]{:S(2)}, u32[]{:S(2)}) collective-permute-start(bf16[128,1024]{1,0:T(8,128)(2,1)S(1)} %get-tuple-element.4), channel_id=1, source_target_pairs={{0,4},{1,5},{2,6},{3,7},{4,0},{5,1},{6,2},{7,3},{8,12},{9,13},{10,... | collective-permute-start | bytes 786440 | tf_op jit(solution)/shard_map/ppermute | solution.py:71
  21.6 0.7 pad_maximum_fusion.2
  22.2 9.7 %all-to-all-start = ((bf16[8,72,128]{2,1,0:T(8,128)(2,1)}), bf16[8,72,128]{2,1,0:T(8,128)(2,1)S(1)}, u32[]{:S(2)}, u32[]{:S(2)}) async-start(bf16[8,72,128]{2,1,0:T(8,128)(2,1)} %pad_maximum_fusion.2), calls=%async_computation | async-start | bytes 294912 | tf_op jit(solution)/shard_map/all_to_all | solution.py:104
  32.6 0.7 constant_dynamic-update-slice_fusion.4
  33.4 2.8 %collective-permute-start.4 = (bf16[512,1024]{1,0:T(8,128)(2,1)S(1)}, bf16[512,1024]{1,0:T(8,128)(2,1)S(1)}, u32[]{:S(2)}, u32[]{:S(2)}) collective-permute-start(bf16[512,1024]{1,0:T(8,128)(2,1)S(1)} %pad_maximum_fusion), channel_id=1, source_target_pairs={{0,1},{1,0},{2,3},{3,2},{4,5},{5,4},{6,7},{7,6},{8,9},{9,8},{10,11... | collective-permute-start | bytes 3145736 | tf_op jit(solution)/shard_map/ppermute | solution.py:75
  36.2 0.7 xor_bitcast_fusion
  37.4 0.8 convolution_convert_fusion.11
  38.2 1.3 reshape.132
  39.6 4.1 %all-to-all-start.1 = ((bf16[8,6,128]{2,1,0:T(8,128)(2,1)}), bf16[8,6,128]{2,1,0:T(8,128)(2,1)S(1)}, u32[]{:S(2)}, u32[]{:S(2)}) async-start(bf16[8,6,128]{2,1,0:T(8,128)(2,1)} %reshape.132), calls=%async_computation.1 | async-start | bytes 32768 | tf_op jit(solution)/shard_map/all_to_all | solution.py:129
  44.3 1.8 gather_fusion
  46.1 2.3 %all-to-all-done.1 = bf16[8,6,128]{2,1,0:T(8,128)(2,1)S(1)} async-done(((bf16[8,6,128]{2,1,0:T(8,128)(2,1)}), bf16[8,6,128]{2,1,0:T(8,128)(2,1)S(1)}, u32[]{:S(2)}, u32[]{:S(2)}) %all-to-all-start.1) | async-done | bytes 12320 | tf_op jit(solution)/shard_map/all_to_all | solution.py:129
  48.4 1.5 fusion.22
  49.9 1.4 collective-permute-start
  51.3 0.7 constant_dynamic-update-slice_fusion.3
  52.0 0.7 constant_dynamic-update-slice_fusion.2
  52.7 0.7 constant_dynamic-update-slice_fusion.1
  53.5 1.1 constant_dynamic-update-slice_fusion
  54.6 4.0 %fusion.6 = bf16[1024,1024]{1,0:T(8,128)(2,1)S(1)} fusion(bf16[1024,1024]{1,0:T(8,128)(2,1)} %constant_dynamic-update-slice_fusion, s32[1024]{0:T(1024)S(1)} %bitcast.121), kind=kOutput, calls=%fused_computation.13 | convolution fusion | flops 2149580800 | bytes 4198400 | tf_op jit(solution)/shard_map/dot_general | solution.py:14
  59.2 0.7 collective-permute-start.6
  59.9 0.7 collective-permute-start.5
  61.9 0.7 collective-permute-start.7
  63.3 0.7 collective-permute-start.10
  63.9 0.7 collective-permute-start.9
  65.3 0.7 collective-permute-start.12
  66.0 0.7 collective-permute-start.11
  67.3 0.7 collective-permute-start.14
  68.0 0.7 collective-permute-start.13
  68.7 4.6 %bitcast_convert_fusion = bf16[1024,1024]{1,0:T(8,128)(2,1)S(1)} fusion(bf16[8,3,128,1024]{3,2,1,0:T(8,128)(2,1)} %bitcast.113), kind=kOutput, calls=%fused_computation.1 | convolution fusion | flops 2148532224 | bytes 4194304 | tf_op jit(solution)/shard_map/dot_general | solution.py:118
  73.3 1.3 copy-done
  75.7 0.7 collective-permute-start.16
  77.5 0.7 collective-permute-start.18
  79.2 0.7 collective-permute-start.20
  80.1 1.8 slice.79
  82.9 0.8 collective-permute-start.22
  83.8 2.4 %fusion.7 = bf16[1024,1024]{1,0:T(8,128)(2,1)S(1)} fusion(bf16[1024,1024]{1,0:T(8,128)(2,1)S(1)} %bitcast.112, s32[1024]{0:T(1024)S(1)} %bitcast.123), kind=kOutput, calls=%fused_computation.14 | convolution fusion | flops 2149580800 | bytes 4198400 | tf_op jit(solution)/shard_map/dot_general | solution.py:14
  87.2 0.7 collective-permute-start.24
  87.9 4.6 %bitcast_convert_fusion.1 = bf16[1024,1024]{1,0:T(8,128)(2,1)S(1)} fusion(bf16[8,3,128,1024]{3,2,1,0:T(8,128)(2,1)} %bitcast.115), kind=kOutput, calls=%fused_computation.2 | convolution fusion | flops 2148532224 | bytes 4194304 | tf_op jit(solution)/shard_map/dot_general | solution.py:118
  92.9 1.3 collective-permute-start.25
  94.6 27.0 %collective-permute-done.25 = bf16[6,1024]{1,0:T(8,128)(2,1)S(1)} collective-permute-done((bf16[6,1024]{1,0:T(8,128)(2,1)S(1)}, bf16[6,1024]{1,0:T(8,128)(2,1)S(1)}, u32[]{:S(2)}, u32[]{:S(2)}) %collective-permute-start.25) | collective-permute-done | bytes 12320 | tf_op jit(solution)/shard_map/ppermute | solution.py:30
  122.6 1.7 collective-permute-start.26
  124.3 0.9 collective-permute-done.26
  125.8 0.7 collective-permute-start.28
  126.4 0.7 collective-permute-start.27
  127.8 0.7 collective-permute-start.30
  128.5 0.7 collective-permute-start.29
  129.8 0.7 collective-permute-start.32
  130.5 0.7 collective-permute-start.31
  131.9 0.7 collective-permute-start.34
  132.5 0.7 collective-permute-start.33
  133.9 0.7 collective-permute-start.36
  134.5 0.7 collective-permute-start.35
  136.3 0.7 collective-permute-start.38
  138.0 0.7 collective-permute-start.40
  139.8 0.7 collective-permute-start.42
  141.5 0.7 collective-permute-start.44
  143.3 0.7 collective-permute-start.46
  144.7 1.3 collective-permute-start.47
  146.3 43.1 %collective-permute-done.47 = bf16[6,1024]{1,0:T(8,128)(2,1)S(1)} collective-permute-done((bf16[6,1024]{1,0:T(8,128)(2,1)S(1)}, bf16[6,1024]{1,0:T(8,128)(2,1)S(1)}, u32[]{:S(2)}, u32[]{:S(2)}) %collective-permute-start.47) | collective-permute-done | bytes 12320 | tf_op jit(solution)/shard_map/ppermute | solution.py:30
  189.8 27.2 %all_to_all.15 = f32[8,8,128]{2,1,0:T(8,128)S(1)} all-to-all(f32[8,8,128]{2,1,0:T(8,128)S(1)} %pad_maximum_fusion.4), channel_id=1, replica_groups=mesh['leaf'=64,'front'=8] {'front'}, dimensions={0} | all-to-all | bytes 65536 | tf_op jit(solution)/shard_map/all_to_all | solution.py:151
  (129 shorter events, 24.4 us)
Async XLA Ops:
  7.2 14.3 %copy-start.3 = (bf16[2,48,128]{2,1,0:T(8,128)(2,1)S(1)}, bf16[2,48,128]{2,1,0:T(8,128)(2,1)}, u32[]{:S(2)}) copy-start(bf16[2,48,128]{2,1,0:T(8,128)(2,1)} %param.8) | copy-start | bytes 73732
  7.2 14.3 %copy-start.7 = (f32[2,128]{1,0:T(2,128)S(1)}, f32[2,128]{1,0:T(2,128)}, u32[]{:S(2)}) copy-start(f32[2,128]{1,0:T(2,128)} %param.9) | copy-start | bytes 3076
  7.2 61.5 %all-gather.3.cloned.1.call-start = ((), (), s32[]{:S(2)}) async-start(), calls=%async_computation.3 | async-start | bytes 7077888 | tf_op jit(solution)/shard_map/all_gather | solution.py:112
  8.3 23.7 %copy-start.4 = (s32[2,1,1024]{2,1,0:T(1,128)S(1)}, s32[2,1,1024]{2,1,0:T(1,128)}, u32[]{:S(2)}) copy-start(s32[2,1,1024]{2,1,0:T(1,128)} %param.12) | copy-start | bytes 24580
  8.3 24.2 %copy-start.2 = (bf16[2,128,1024]{2,1,0:T(8,128)(2,1)S(1)}, bf16[2,128,1024]{2,1,0:T(8,128)(2,1)}, u32[]{:S(2)}) copy-start(bf16[2,128,1024]{2,1,0:T(8,128)(2,1)} %param.11) | copy-start | bytes 1572868
  10.5 22.8 %collective-permute-start.1 = (bf16[128,1024]{1,0:T(8,128)(2,1)S(1)}, bf16[128,1024]{1,0:T(8,128)(2,1)S(1)}, u32[]{:S(2)}, u32[]{:S(2)}) collective-permute-start(bf16[128,1024]{1,0:T(8,128)(2,1)S(1)} %get-tuple-element.4), channel_id=1, source_target_pairs={{0,2},{1,3},{2,4},{3,5},{4,6},{5,7},{6,0},{7,1},{8,10},{9,11},{10,... | collective-permute-start | bytes 786440 | tf_op jit(solution)/shard_map/ppermute | solution.py:71
  14.5 18.8 %collective-permute-start.2 = (bf16[128,1024]{1,0:T(8,128)(2,1)S(1)}, bf16[128,1024]{1,0:T(8,128)(2,1)S(1)}, u32[]{:S(2)}, u32[]{:S(2)}) collective-permute-start(bf16[128,1024]{1,0:T(8,128)(2,1)S(1)} %get-tuple-element.4), channel_id=1, source_target_pairs={{0,6},{1,7},{2,0},{3,1},{4,2},{5,3},{6,4},{7,5},{8,14},{9,15},{10,... | collective-permute-start | bytes 786440 | tf_op jit(solution)/shard_map/ppermute | solution.py:71
  17.9 15.4 %collective-permute-start.3 = (bf16[128,1024]{1,0:T(8,128)(2,1)S(1)}, bf16[128,1024]{1,0:T(8,128)(2,1)S(1)}, u32[]{:S(2)}, u32[]{:S(2)}) collective-permute-start(bf16[128,1024]{1,0:T(8,128)(2,1)S(1)} %get-tuple-element.4), channel_id=1, source_target_pairs={{0,4},{1,5},{2,6},{3,7},{4,0},{5,1},{6,2},{7,3},{8,12},{9,13},{10,... | collective-permute-start | bytes 786440 | tf_op jit(solution)/shard_map/ppermute | solution.py:71
  22.2 15.2 %all-to-all-start = ((bf16[8,72,128]{2,1,0:T(8,128)(2,1)}), bf16[8,72,128]{2,1,0:T(8,128)(2,1)S(1)}, u32[]{:S(2)}, u32[]{:S(2)}) async-start(bf16[8,72,128]{2,1,0:T(8,128)(2,1)} %pad_maximum_fusion.2), calls=%async_computation | async-start | bytes 294912 | tf_op jit(solution)/shard_map/all_to_all | solution.py:104
  33.4 20.1 %collective-permute-start.4 = (bf16[512,1024]{1,0:T(8,128)(2,1)S(1)}, bf16[512,1024]{1,0:T(8,128)(2,1)S(1)}, u32[]{:S(2)}, u32[]{:S(2)}) collective-permute-start(bf16[512,1024]{1,0:T(8,128)(2,1)S(1)} %pad_maximum_fusion), channel_id=1, source_target_pairs={{0,1},{1,0},{2,3},{3,2},{4,5},{5,4},{6,7},{7,6},{8,9},{9,8},{10,11... | collective-permute-start | bytes 3145736 | tf_op jit(solution)/shard_map/ppermute | solution.py:75
  39.6 8.8 %all-to-all-start.1 = ((bf16[8,6,128]{2,1,0:T(8,128)(2,1)}), bf16[8,6,128]{2,1,0:T(8,128)(2,1)S(1)}, u32[]{:S(2)}, u32[]{:S(2)}) async-start(bf16[8,6,128]{2,1,0:T(8,128)(2,1)} %reshape.132), calls=%async_computation.1 | async-start | bytes 32768 | tf_op jit(solution)/shard_map/all_to_all | solution.py:129
  49.9 4.7 %copy-start.5 = (s32[8,128]{1,0:T(8,128)S(1)}, s32[8,128]{1,0:T(8,128)}, u32[]{:S(2)}) copy-start(s32[8,128]{1,0:T(8,128)} %gather_fusion) | copy-start | bytes 12292
  49.9 8.7 %collective-permute-start = (bf16[6,1024]{1,0:T(8,128)(2,1)S(1)}, bf16[6,1024]{1,0:T(8,128)(2,1)S(1)}, u32[]{:S(2)}, u32[]{:S(2)}) collective-permute-start(bf16[6,1024]{1,0:T(8,128)(2,1)S(1)} %fusion.22), channel_id=1, source_target_pairs={{0,8},{16,24},{32,40},{48,56},{64,72},{80,88},{96,104},{112,120},{... | collective-permute-start | bytes 36872 | tf_op jit(solution)/shard_map/ppermute | solution.py:30
  59.2 1.3 collective-permute-start.6
  59.9 0.7 collective-permute-start.5
  61.3 1.3 collective-permute-start.8
  61.9 0.7 collective-permute-start.7
  63.3 1.3 collective-permute-start.10
  63.9 0.7 collective-permute-start.9
  65.3 1.3 collective-permute-start.12
  66.0 0.7 collective-permute-start.11
  67.3 6.0 %collective-permute-start.14 = (bf16[6,1024]{1,0:T(8,128)(2,1)S(1)}, bf16[6,1024]{1,0:T(8,128)(2,1)S(1)}, u32[]{:S(2)}, u32[]{:S(2)}) collective-permute-start(bf16[6,1024]{1,0:T(8,128)(2,1)S(1)} %convolution_convert_fusion.6), channel_id=1, source_target_pairs={{384,256},{385,257},{386,258},{387,259},{388,260},{389,261},{390,2... | collective-permute-start | bytes 36872 | tf_op jit(solution)/shard_map/ppermute | solution.py:30
  68.0 5.3 %collective-permute-start.13 = (bf16[6,1024]{1,0:T(8,128)(2,1)S(1)}, bf16[6,1024]{1,0:T(8,128)(2,1)S(1)}, u32[]{:S(2)}, u32[]{:S(2)}) collective-permute-start(bf16[6,1024]{1,0:T(8,128)(2,1)S(1)} %convolution_convert_fusion.6), channel_id=1, source_target_pairs={{128,256},{129,257},{130,258},{131,259},{132,260},{133,261},{134,2... | collective-permute-start | bytes 36872 | tf_op jit(solution)/shard_map/ppermute | solution.py:30
  73.3 1.4 copy-start
  75.0 1.3 collective-permute-start.15
  75.7 0.7 collective-permute-start.16
  76.4 3.5 %copy-start.8 = (f32[1,128]{1,0:T(1,128)S(1)}, f32[1,128]{1,0:T(1,128)}, u32[]{:S(2)}) copy-start(f32[1,128]{1,0:T(1,128)} %param.14) | copy-start | bytes 1540
  76.4 3.5 %copy-start.9 = (s32[1,128]{1,0:T(1,128)S(1)}, s32[1,128]{1,0:T(1,128)}, u32[]{:S(2)}) copy-start(s32[1,128]{1,0:T(1,128)} %param.13) | copy-start | bytes 1540
  76.8 1.3 collective-permute-start.17
  77.5 0.7 collective-permute-start.18
  78.6 3.3 %collective-permute-start.19 = (bf16[6,1024]{1,0:T(8,128)(2,1)S(1)}, bf16[6,1024]{1,0:T(8,128)(2,1)S(1)}, u32[]{:S(2)}, u32[]{:S(2)}) collective-permute-start(bf16[6,1024]{1,0:T(8,128)(2,1)S(1)} %fusion.32), channel_id=1, source_target_pairs={{64,32},{192,160},{320,288},{448,416},{65,33},{193,161},{321,289},... | collective-permute-start | bytes 36872 | tf_op jit(solution)/shard_map/ppermute | solution.py:30
  79.2 2.6 %collective-permute-start.20 = (bf16[6,1024]{1,0:T(8,128)(2,1)S(1)}, bf16[6,1024]{1,0:T(8,128)(2,1)S(1)}, u32[]{:S(2)}, u32[]{:S(2)}) collective-permute-start(bf16[6,1024]{1,0:T(8,128)(2,1)S(1)} %fusion.32), channel_id=1, source_target_pairs={{64,96},{192,224},{320,352},{448,480},{65,97},{193,225},{321,353},... | collective-permute-start | bytes 36872 | tf_op jit(solution)/shard_map/ppermute | solution.py:30
  81.8 1.9 copy-start.6
  82.2 3.9 %collective-permute-start.21 = (bf16[6,1024]{1,0:T(8,128)(2,1)S(1)}, bf16[6,1024]{1,0:T(8,128)(2,1)S(1)}, u32[]{:S(2)}, u32[]{:S(2)}) collective-permute-start(bf16[6,1024]{1,0:T(8,128)(2,1)S(1)} %fusion.31), channel_id=1, source_target_pairs={{32,16},{96,80},{160,144},{224,208},{288,272},{352,336},{416,400},... | collective-permute-start | bytes 36872 | tf_op jit(solution)/shard_map/ppermute | solution.py:30
  82.9 3.2 %collective-permute-start.22 = (bf16[6,1024]{1,0:T(8,128)(2,1)S(1)}, bf16[6,1024]{1,0:T(8,128)(2,1)S(1)}, u32[]{:S(2)}, u32[]{:S(2)}) collective-permute-start(bf16[6,1024]{1,0:T(8,128)(2,1)S(1)} %fusion.31), channel_id=1, source_target_pairs={{32,48},{96,112},{160,176},{224,240},{288,304},{352,368},{416,432}... | collective-permute-start | bytes 36872 | tf_op jit(solution)/shard_map/ppermute | solution.py:30
  86.5 6.0 %collective-permute-start.23 = (bf16[6,1024]{1,0:T(8,128)(2,1)S(1)}, bf16[6,1024]{1,0:T(8,128)(2,1)S(1)}, u32[]{:S(2)}, u32[]{:S(2)}) collective-permute-start(bf16[6,1024]{1,0:T(8,128)(2,1)S(1)} %fusion.30), channel_id=1, source_target_pairs={{16,8},{48,40},{80,72},{112,104},{144,136},{176,168},{208,200},{24... | collective-permute-start | bytes 36872 | tf_op jit(solution)/shard_map/ppermute | solution.py:30
  87.2 5.3 %collective-permute-start.24 = (bf16[6,1024]{1,0:T(8,128)(2,1)S(1)}, bf16[6,1024]{1,0:T(8,128)(2,1)S(1)}, u32[]{:S(2)}, u32[]{:S(2)}) collective-permute-start(bf16[6,1024]{1,0:T(8,128)(2,1)S(1)} %fusion.30), channel_id=1, source_target_pairs={{16,24},{48,56},{80,88},{112,120},{144,152},{176,184},{208,216},{2... | collective-permute-start | bytes 36872 | tf_op jit(solution)/shard_map/ppermute | solution.py:30
  92.9 28.7 %collective-permute-start.25 = (bf16[6,1024]{1,0:T(8,128)(2,1)S(1)}, bf16[6,1024]{1,0:T(8,128)(2,1)S(1)}, u32[]{:S(2)}, u32[]{:S(2)}) collective-permute-start(bf16[6,1024]{1,0:T(8,128)(2,1)S(1)} %fusion.29), channel_id=1, source_target_pairs={{8,0},{24,16},{40,32},{56,48},{72,64},{88,80},{104,96},{120,112},{... | collective-permute-start | bytes 36872 | tf_op jit(solution)/shard_map/ppermute | solution.py:30
  122.6 2.5 %collective-permute-start.26 = (bf16[6,1024]{1,0:T(8,128)(2,1)S(1)}, bf16[6,1024]{1,0:T(8,128)(2,1)S(1)}, u32[]{:S(2)}, u32[]{:S(2)}) collective-permute-start(bf16[6,1024]{1,0:T(8,128)(2,1)S(1)} %convolution_convert_fusion.5), channel_id=1, source_target_pairs={{0,8},{16,24},{32,40},{48,56},{64,72},{80,88},{96,104},{112,120},{... | collective-permute-start | bytes 36872 | tf_op jit(solution)/shard_map/ppermute | solution.py:30
  125.8 1.3 collective-permute-start.28
  126.4 0.7 collective-permute-start.27
  127.8 1.3 collective-permute-start.30
  128.5 0.7 collective-permute-start.29
  129.8 1.3 collective-permute-start.32
  130.5 0.7 collective-permute-start.31
  131.2 4.0 %copy-start.1 = (bf16[1024,1024]{1,0:T(8,128)(2,1)S(1)}, bf16[1024,1024]{1,0:T(8,128)(2,1)}, u32[]{:S(2)}) copy-start(bf16[1024,1024]{1,0:T(8,128)(2,1)} %copy-done) | copy-start | bytes 6291460
  131.9 1.3 collective-permute-start.34
  132.5 0.7 collective-permute-start.33
  133.9 1.3 collective-permute-start.36
  134.5 0.7 collective-permute-start.35
  135.6 1.3 collective-permute-start.37
  136.3 0.7 collective-permute-start.38
  137.4 1.3 collective-permute-start.39
  138.0 0.7 collective-permute-start.40
  139.1 1.3 collective-permute-start.41
  139.8 0.7 collective-permute-start.42
  140.9 1.3 collective-permute-start.43
  141.5 0.7 collective-permute-start.44
  142.6 1.7 collective-permute-start.45
  143.3 1.1 collective-permute-start.46
  144.7 44.6 %collective-permute-start.47 = (bf16[6,1024]{1,0:T(8,128)(2,1)S(1)}, bf16[6,1024]{1,0:T(8,128)(2,1)S(1)}, u32[]{:S(2)}, u32[]{:S(2)}) collective-permute-start(bf16[6,1024]{1,0:T(8,128)(2,1)S(1)} %get-tuple-element.15), channel_id=1, source_target_pairs={{8,0},{24,16},{40,32},{56,48},{72,64},{88,80},{104,96},{120,112},{... | collective-permute-start | bytes 36872 | tf_op jit(solution)/shard_map/ppermute | solution.py:30
Sparse Core Ops, SparseCore 0:
  10.6 54.5 all-gather.2

commit v3 on v1

v3 whole, which is shorter than its diff:
```python
import jax
import jax.numpy as jnp
from jax import lax
from jax.sharding import Mesh, PartitionSpec as P

LEAF = ("pair", "side")
FRONT = ("y", "core")
PAIR = ("side",) + FRONT
CONTRACT_LAST = (((1,), (1,)), ((), ()))
CONTRACT_FIRST = (((0,), (0,)), ((), ()))
PAD = 8


def times_transposed(vectors, matrix):
    return lax.dot_general(vectors, matrix, CONTRACT_LAST, preferred_element_type=jnp.float32)


def times(vectors, matrix):
    return jnp.dot(vectors, matrix, preferred_element_type=jnp.float32)


def rounded(values):
    return values.astype(jnp.bfloat16)


def after(value, *earlier):
    return lax.optimization_barrier((value,) + earlier)[0]


def links(height, groups):
    owners = [g for g in range(1, groups) if (g & -g) == 1 << (height - 1)]
    offset = 2 ** (height - 2)
    return [(g - offset, g) for g in owners], [(g + offset, g) for g in owners]


def reverse(pairs):
    return [(b, a) for a, b in pairs]


def send(value, pairs):
    return lax.ppermute(value, LEAF, pairs)


def y_blocks(block):
    count = lax.axis_size("y")

    def shifted(by):
        return lax.ppermute(block, "y", [(k, (k + by) % count) for k in range(count)])

    return [shifted(1), block, shifted(-1), shifted(2)]


def stacked(blocks):
    return jnp.concatenate(blocks, -2)


def core_swap(value):
    return lax.ppermute(value, "core", [(0, 1), (1, 0)])


def near_order(columns):
    count = lax.axis_size("y")
    blocks = columns.reshape(count, 2, -1)
    blocks = jnp.concatenate([blocks, blocks], 0)
    start = (lax.axis_index("y") + count - 1) % count
    blocks = lax.dynamic_slice_in_dim(blocks, start, count, 0)
    first, second = blocks[:, 0].reshape(-1), blocks[:, 1].reshape(-1)
    on_first = lax.axis_index("core") == 0
    return jnp.where(on_first, first, second), jnp.where(on_first, second, first)


def per_device(fields, direction, inverse_blocks, update_blocks, row_map, receivers, weights):
    groups = lax.axis_size(LEAF)
    width = lax.axis_size(FRONT)
    levels = groups.bit_length() - 1
    group = lax.axis_index(LEAF)
    odd = lax.axis_index("side") == 1
    sources, rows = fields.shape[1], fields.shape[2]
    share = sources // width
    whole = rows * width
    pair_up = [(g, g + 1) for g in range(0, groups, 2)]

    def lanes(blocks):
        blocks = blocks.reshape((-1,) + blocks.shape[-2:])
        return blocks.transpose(1, 0, 2).reshape(blocks.shape[1], -1)

    def padded(values):
        return jnp.pad(values.reshape(width, share, rows), ((0, 0), (0, PAD - share), (0, 0)))

    terms = rounded(direction[:, None, :] * fields.astype(jnp.float32))
    leaf_terms = padded(terms[0])
    map_rows = lax.dynamic_slice_in_dim(row_map[0, 0], lax.axis_index(FRONT) * rows, rows)
    digits = jnp.stack([map_rows // 32, map_rows % 32]).astype(jnp.bfloat16)
    digits = jnp.broadcast_to(digits[None], (width, 2, rows))

    def marked(values):
        return jnp.concatenate([values.reshape(width, share, rows), digits], 1)

    own = jnp.broadcast_to(leaf_terms.reshape(1, width * PAD, rows), (width, width * PAD, rows))
    own = jnp.concatenate([padded(fields[1]), padded(terms[1]), own], 1)
    message = jnp.concatenate(
        [jnp.concatenate([marked(terms[0]), own], 1), jnp.concatenate([marked(fields[0]), own], 1)], 0
    )
    node_block = update_blocks[1]
    swapped = after(jnp.where(odd, inverse_blocks[0], update_blocks[0]), message)
    message = lax.all_to_all(message, PAIR, 0, 0, tiled=True)
    message = message.reshape((2, width) + message.shape[1:])
    leaf_pair = lanes(message[:, :, :PAD])
    pair_map = leaf_pair[share].astype(jnp.float32) * 32 + leaf_pair[share + 1].astype(jnp.float32)
    pair_map = pair_map.astype(jnp.int32)
    mine = jnp.where(odd, message[1], message[0])
    field_node = lanes(mine[:, PAD : 2 * PAD])
    term_node = lanes(mine[:, 2 * PAD : 3 * PAD])
    leaf_all = lanes(mine[:, 3 * PAD :])

    def spots(columns):
        return (jnp.arange(whole)[:, None] == columns[None, :]).astype(jnp.bfloat16)

    node_near = stacked(y_blocks(node_block))
    node_far = core_swap(node_near)
    kept = jnp.where(odd, update_blocks[0], inverse_blocks[0])
    swapped = send(swapped, pair_up + reverse(pair_up))
    arrived = message[0, 0, 0, 0]
    held = node_near[0, 0] + node_near[2 * rows, 0] + node_near[3 * rows, 0]
    on_odd = odd ^ (arrived != arrived) ^ (held != held)
    later = jnp.stack([inverse_blocks[1], jnp.where(on_odd, swapped, kept), jnp.where(on_odd, kept, swapped)])
    later = lax.all_gather(later, FRONT, axis=0)
    near_spots, far_spots = [spots(part) for part in near_order(row_map[1, 0])]

    update = rounded(times_transposed(leaf_all, update_blocks[0])).reshape(width, PAD, rows)
    update = lax.all_to_all(jnp.concatenate([update, update], 0), PAIR, 0, 0, tiled=True)
    update = times_transposed(lanes(update), spots(pair_map))
    node_r = term_node.astype(jnp.float32) - jnp.where(odd, update, 0.0)

    first = rounded(node_r)
    update = times_transposed(rounded(times_transposed(first, node_near)), near_spots)
    update = update + times_transposed(rounded(times_transposed(first, node_far)), far_spots)
    update = rounded(update)
    at_station = receivers[0][:, None] == jnp.arange(whole)[None, :]
    station_weight = jnp.sum(jnp.where(at_station, weights[0][:, None], 0.0), axis=0)

    got = {}

    def slot(blocks, k):
        matrix = blocks[:, k + 1].reshape(whole, whole)
        places = pair_map[k * whole : (k + 1) * whole]
        places = (places[:, None] == jnp.arange(whole)[None, :]).astype(jnp.bfloat16)
        return rounded(
            lax.dot_general(
                jnp.where(odd, places, matrix), matrix, CONTRACT_FIRST, preferred_element_type=jnp.float32
            )
        )

    def beside_up(height, token):
        if height == 2:
            near, far, token = lax.optimization_barrier((node_near, node_far, token))
            got["up"] = rounded(times(near_spots, near) + times(far_spots, far))
            return ["up"]
        if height == levels:
            blocks = after(later, token)[:, 0]
            got["inverse"] = rounded(
                lax.dot_general(
                    blocks, blocks, (((0, 1), (0, 1)), ((), ())), preferred_element_type=jnp.float32
                )
            )
            return ["inverse"]
        return []

    def beside_down(height, token):
        names = []
        if height == levels:
            blocks = after(later, token)
            got["leaf"] = [slot(blocks, 0), slot(blocks, 1)]
            send_first_leaf_t(token)
            names.append("leaf")
        if height == levels - 1:
            names.append("leaf_t")
        return names

    def joined(names, *values):
        *values, extra = lax.optimization_barrier(values + ([got[n] for n in names],))
        got.update(zip(names, extra))
        return values

    def forward(update, node_r, beside):
        for height in range(2, levels + 1):
            left, right = links(height, groups)
            from_right, from_left = send(update, right), send(update, left)
            from_left, from_right = joined(beside(height, update), from_left, from_right)
            node_r = node_r - from_left.astype(jnp.float32) - from_right.astype(jnp.float32)
            if height < levels:
                update = rounded(times_transposed(rounded(node_r), got["up"]))
        return rounded(node_r)

    def backward(node_t, beside):
        node_x = rounded(node_t)
        for height in range(levels, 1, -1):
            left, right = links(height, groups)
            from_left, from_right = send(node_x, reverse(left)), send(node_x, reverse(right))
            from_left, from_right = joined(beside(height, node_x), from_left, from_right)
            new_x = rounded(node_t - times(from_left + from_right, got["up"]))
            is_child = (group & -group) == 1 << (height - 2)
            node_x = jnp.where(is_child, new_x, node_x)
        return node_x

    def leaf_step(vectors):
        return jnp.concatenate(
            [times(v, m) for v, m in zip(vectors, got["leaf"])], 1
        )

    def halves(vectors):
        return vectors[:, :whole], vectors[:, whole:]

    def through_inverse(vectors):
        return times(vectors, got["inverse"])

    carried = jnp.concatenate([station_weight, station_weight])[None, :]

    def send_first_leaf_t(token):
        leaf_t = leaf_step(halves(after(leaf_pair, token)))
        leaf_t = jnp.where(jnp.arange(PAD)[:, None] == PAD - 1, carried, leaf_t)
        got["leaf_t"] = send(leaf_t, pair_up)

    node_r = forward(update, node_r, beside_up)
    node_x = backward(through_inverse(node_r), beside_down)
    leaf_t = got["leaf_t"]
    pair_weight = jnp.concatenate([leaf_t[PAD - 1, :whole], station_weight])

    delta = rounded(leaf_t - leaf_step((node_x, node_x)))
    injected = rounded(delta.astype(jnp.float32) * pair_weight[None, :])
    update = sum(times_transposed(v, m) for v, m in zip(halves(injected), got["leaf"]))
    node_r = -jnp.where(odd, update, 0.0)
    update = rounded(times_transposed(rounded(node_r), got["up"]))

    def beside_second(height, token):
        if height == 3:
            back = after(jnp.concatenate([injected, delta[:, :whole]], 1), token)
            got["back"] = send(back, reverse(pair_up))
        if height == min(5, levels):
            back = after(got["back"], token)
            got["leaf_t"] = send(leaf_step(halves(back[:, : 2 * whole])), pair_up)
            delta_own = jnp.where(odd, delta[:, whole:], back[:, 2 * whole :])
            got["station"] = times_transposed(delta_own, at_station.astype(jnp.bfloat16))
        return []

    node_r = forward(update, node_r, beside_second)
    station, leaf_t = got["station"], got["leaf_t"]
    node_x = backward(through_inverse(node_r), lambda height, token: [])
    adjoint = rounded(leaf_t - leaf_step((node_x, node_x)))
    curve_leaf = jnp.sum(leaf_pair[:share].astype(jnp.float32) * adjoint[:share].astype(jnp.float32), axis=0)
    curve_node = jnp.sum(field_node.astype(jnp.float32) * node_x.astype(jnp.float32), axis=0)

    out = jnp.concatenate(
        [
            curve_leaf.reshape(2 * width, 1, rows),
            jnp.tile(curve_node.reshape(width, 1, rows), (2, 1, 1)),
            jnp.broadcast_to(station[None, :share], (2 * width, share, rows)),
        ],
        axis=1,
    )
    out = lax.all_to_all(out, PAIR, 0, 0, tiled=True)
    curve_leaf = jnp.sum(out[width:, 0], axis=0)
    out = jnp.where(odd, out[width:], out[:width])
    curvature = jnp.stack([curve_leaf, jnp.sum(out[:, 1], axis=0)])
    data_change = out[:, 2:].reshape(sources, rows).astype(jnp.bfloat16)
    return data_change, curvature


def solution(mesh):
    groups, width = mesh.devices.shape
    every = ("pair",) + PAIR
    split = Mesh(mesh.devices.reshape(groups // 2, 2, width // 2, 2), every)
    in_specs = (
        P(None, None, every),
        P(None, every),
        P(None, every, None),
        P(None, every, None),
        P(None, LEAF, None),
        P(LEAF, None),
        P(LEAF, None),
    )
    out_specs = (P(None, LEAF), P(None, every))
    return jax.shard_map(
        per_device, mesh=split, in_specs=in_specs, out_specs=out_specs, check_vma=False
    )
```

time: 257 us -> 223 us (0.87)
  waiting for transfers between devices: 133 us -> 41.3 us
  blocking collectives: 20.6 us -> 51.7 us
  starting transfers between devices: 45.8 us -> 63.7 us
  other arithmetic: 0.81 us -> 5.44 us
  between operations: 14.7 us -> 18.6 us
    all_gather x4 -> x1, waiting for transfers between devices: 92.2 us -> 18.1 us  [per_device(): later = lax.all_gather(later, FRONT, axis=0)]
    all_to_all x1, blocking collectives: 20.6 us -> 51.7 us  [per_device(): out = lax.all_to_all(out, PAIR, 0, 0, tiled=True)]
    ppermute x44 -> x48, waiting for transfers between devices: 34.9 us -> 16.5 us  [the longest x44 16.5 us: send(): return lax.ppermute(value, LEAF, pairs)]
    dot_general x18 -> x22, matrix products: 26.9 us -> 11.6 us  [times(): return jnp.dot(vectors, matrix, preferred_element_type=jnp.float32)]
    ppermute x44 -> x48, starting transfers between devices: 35.6 us -> 50.8 us  [the longest x44 37.1 us: send(): return lax.ppermute(value, LEAF, pairs)]
    dot_general x0 -> x3, matrix products: none -> 10.4 us  [the longest x2 5.64 us: slot(): lax.dot_general(jnp.where(odd, places, matrix), matrix, CONTRACT_FIRST, p...]
    dot_general x13 -> x16, matrix products: 7.97 us -> 11.7 us  [times_transposed(): lax.dot_general(vectors, matrix, CONTRACT_LAST, preferred_element_type=jn...]
    all_to_all x1 -> x2, starting transfers between devices: 10.1 us -> 12.9 us  [the longest x1 8.51 us: per_device(): message = lax.all_to_all(message, PAIR, 0, 0, tiled=True)]
  transfers between devices with their start and end apart: 49 -> 51, of which waited for: 7 -> 5; matrix products, arithmetic and copies ran while one was open for 10% -> 15% of each run, Pallas kernels for 0% -> 0%
where the time goes in v3:
time: 223 us; the launch traced here: 221 us
  starting transfers between devices  63.7 us (29%)
  blocking collectives  51.7 us (23%)
  waiting for transfers between devices  41.3 us (19%)
  matrix products  33.7 us (15%)
  between operations  18.6 us (8%)
  local copies, waits for them, and re-layouts  6.96 us (3%)
  other arithmetic  5.44 us (2%)
    all_to_all x1, blocking collectives, per_device(): out = lax.all_to_all(out, PAIR, 0, 0, tiled=True)  51.7 us
    ppermute x44, starting transfers between devices, send(): return lax.ppermute(value, LEAF, pairs)  37.1 us
    all_gather x1, waiting for transfers between devices, per_device(): later = lax.all_gather(later, FRONT, axis=0)  18.1 us
    ppermute x44, waiting for transfers between devices, send(): return lax.ppermute(value, LEAF, pairs)  16.5 us
    dot_general x16, matrix products, times_transposed(): lax.dot_general(vectors, matrix, CONTRACT_LAST, preferred_element_type=jn...  11.7 us
    dot_general x22, matrix products, times(): return jnp.dot(vectors, matrix, preferred_element_type=jnp.float32)  11.6 us
    ppermute x3, starting transfers between devices, shifted(): lax.ppermute(block, 'y', [(k, (k + by) % count) for k in range(count)])  10.9 us
    all_to_all x1, starting transfers between devices, per_device(): message = lax.all_to_all(message, PAIR, 0, 0, tiled=True)  8.51 us
  transfers between devices with their start and end apart: 51, of which 5 were waited for; matrix products, arithmetic and copies ran while one was open for 15% of the time, Pallas kernels for 0%

profile of v3, /device:TPU:1, one launch (start us, length us, event | category | flops | bytes accessed | tf_op | source)
XLA Modules:
  0.0 221.5 jit_solution(865849116238082368)
XLA Ops:
  7.2 1.1 slice_bitcast_fusion.2
  8.2 5.7 %collective-permute-start.2 = (bf16[128,1024]{1,0:T(8,128)(2,1)S(1)}, bf16[128,1024]{1,0:T(8,128)(2,1)S(1)}, u32[]{:S(2)}, u32[]{:S(2)}) collective-permute-start(bf16[128,1024]{1,0:T(8,128)(2,1)S(1)} %slice_bitcast_fusion.2), channel_id=1, source_target_pairs={{0,4},{2,6},{4,0},{6,2},{1,5},{3,7},{5,1},{7,3},{8,12},{10,14},{12... | collective-permute-start | bytes 786440 | tf_op jit(solution)/shard_map/ppermute | solution.py:48
  13.9 2.7 %collective-permute-start.1 = (bf16[128,1024]{1,0:T(8,128)(2,1)S(1)}, bf16[128,1024]{1,0:T(8,128)(2,1)S(1)}, u32[]{:S(2)}, u32[]{:S(2)}) collective-permute-start(bf16[128,1024]{1,0:T(8,128)(2,1)S(1)} %slice_bitcast_fusion.2), channel_id=1, source_target_pairs={{0,6},{2,0},{4,2},{6,4},{1,7},{3,1},{5,3},{7,5},{8,14},{10,8},{12,... | collective-permute-start | bytes 786440 | tf_op jit(solution)/shard_map/ppermute | solution.py:48
  16.6 2.6 %collective-permute-start = (bf16[128,1024]{1,0:T(8,128)(2,1)S(1)}, bf16[128,1024]{1,0:T(8,128)(2,1)S(1)}, u32[]{:S(2)}, u32[]{:S(2)}) collective-permute-start(bf16[128,1024]{1,0:T(8,128)(2,1)S(1)} %slice_bitcast_fusion.2), channel_id=1, source_target_pairs={{0,2},{2,4},{4,6},{6,0},{1,3},{3,5},{5,7},{7,1},{8,10},{10,12},{12... | collective-permute-start | bytes 786440 | tf_op jit(solution)/shard_map/ppermute | solution.py:48
  19.2 0.7 fusion.109
  19.9 0.7 fusion.108
  20.7 0.8 multiply_convert_fusion.1
  21.8 0.8 pad_maximum_fusion.2
  22.6 8.5 %all-to-all-start = ((bf16[16,88,128]{2,1,0:T(8,128)(2,1)}), bf16[16,88,128]{2,1,0:T(8,128)(2,1)S(1)}, u32[]{:S(2)}, u32[]{:S(2)}) async-start(bf16[16,88,128]{2,1,0:T(8,128)(2,1)} %pad_maximum_fusion.2), calls=%async_computation | async-start | bytes 720896 | tf_op jit(solution)/shard_map/all_to_all | solution.py:106
  31.2 3.3 %collective-permute-start.14 = (bf16[128,1024]{1,0:T(8,128)(2,1)S(1)}, bf16[128,1024]{1,0:T(8,128)(2,1)S(1)}, u32[]{:S(2)}, u32[]{:S(2)}) collective-permute-start(bf16[128,1024]{1,0:T(8,128)(2,1)S(1)} %bitcast_select_fusion.1), channel_id=1, source_target_pairs={{0,8},{16,24},{32,40},{48,56},{64,72},{80,88},{96,104},{112,120},{... | collective-permute-start | bytes 786440 | tf_op jit(solution)/shard_map/ppermute | solution.py:41
  38.2 1.0 all-to-all-done
  41.0 2.0 collective-permute-done.14
  43.1 1.0 pad_maximum_fusion.1
  44.2 1.1 pad_maximum_fusion
  45.3 2.8 %collective-permute-start.3 = (bf16[512,1024]{1,0:T(8,128)(2,1)S(1)}, bf16[512,1024]{1,0:T(8,128)(2,1)}, u32[]{:S(2)}, u32[]{:S(2)}) collective-permute-start(bf16[512,1024]{1,0:T(8,128)(2,1)S(1)} %pad_maximum_fusion), channel_id=1, source_target_pairs={{0,1},{1,0},{2,3},{3,2},{4,5},{5,4},{6,7},{7,6},{8,9},{9,8},{10,11... | collective-permute-start | bytes 3145736 | tf_op jit(solution)/shard_map/ppermute | solution.py:58
  49.1 4.4 %all-to-all-start.1 = ((bf16[16,8,128]{2,1,0:T(8,128)(2,1)}), bf16[16,8,128]{2,1,0:T(8,128)(2,1)S(1)}, u32[]{:S(2)}, u32[]{:S(2)}) async-start(bf16[16,8,128]{2,1,0:T(8,128)(2,1)} %pad_maximum_fusion.7), calls=%async_computation.1 | async-start | bytes 65536 | tf_op jit(solution)/shard_map/all_to_all | solution.py:131
  53.5 5.6 %all-to-all-done.1 = bf16[16,8,128]{2,1,0:T(8,128)(2,1)S(1)} async-done(((bf16[16,8,128]{2,1,0:T(8,128)(2,1)}), bf16[16,8,128]{2,1,0:T(8,128)(2,1)S(1)}, u32[]{:S(2)}, u32[]{:S(2)}) %all-to-all-start.1) | async-done | bytes 32800 | tf_op jit(solution)/shard_map/all_to_all | solution.py:131
  59.1 1.5 fusion.23
  60.6 1.9 fusion.17
  62.6 0.7 fusion.36
  63.3 0.7 collective-permute-start.4
  64.0 0.7 collective-permute-start.5
  64.6 2.6 %fusion.16 = f32[1024,1024]{1,0:T(8,128)S(1)} fusion(bf16[512,1024]{1,0:T(8,128)(2,1)} %collective-permute-done.3, s32[512]{0:T(512)S(1)} %bitcast.165), kind=kOutput, calls=%fused_computation.23 | convolution fusion | flops 1074266112 | bytes 5244928 | tf_op jit(solution)/shard_map/dot_general | solution.py:19
  67.2 1.3 add_convert_fusion
  69.2 0.7 collective-permute-start.6
  69.9 0.7 collective-permute-start.7
  71.2 0.7 collective-permute-start.8
  71.9 0.7 collective-permute-start.9
  73.3 0.7 collective-permute-start.10
  73.9 0.7 collective-permute-start.11
  75.3 0.7 collective-permute-start.12
  76.0 0.8 collective-permute-start.13
  76.8 18.1 %all-gather.3.cloned.1.call-done = bf16[24,128,1024]{2,1,0:T(8,128)(2,1)} async-done(((bf16[3,128,1024]{2,1,0:T(8,128)(2,1)}), bf16[24,128,1024]{2,1,0:T(8,128)(2,1)}) %all-gather.3.cloned.1.call-update) | async-done | bytes 6291472 | tf_op jit(solution)/shard_map/all_gather | solution.py:127
  94.9 4.8 %bitcast_convert_fusion.2 = bf16[1024,1024]{1,0:T(8,128)(2,1)S(1)} fusion(bf16[8,3,128,1024]{3,2,1,0:T(8,128)(2,1)} %bitcast.171), kind=kOutput, calls=%fused_computation.4 | convolution fusion | flops 2148532224 | bytes 4194304 | tf_op jit(solution)/shard_map/dot_general | solution.py:162
  100.8 0.7 collective-permute-start.16
  101.5 2.8 %bitcast_convert_fusion.1 = bf16[1024,1024]{1,0:T(8,128)(2,1)S(1)} fusion(s32[8,128]{1,0:T(8,128)S(1)} %get-tuple-element.125, pred[]{:T(512)S(6)} %eq.132, bf16[8,3,128,1024]{3,2,1,0:T(8,128)(2,1)S(1)} %bitcast.174), kind=kOutput, calls=%fused_computation.3 | convolution fusion | flops 2151677952 | bytes 6295553 | tf_op jit(solution)/shard_map/dot_general | solution.py:149
  104.3 2.8 %bitcast_convert_fusion = bf16[1024,1024]{1,0:T(8,128)(2,1)S(1)} fusion(s32[8,128]{1,0:T(8,128)S(1)} %get-tuple-element.124, pred[]{:T(512)S(6)} %eq.132, bf16[8,3,128,1024]{3,2,1,0:T(8,128)(2,1)S(1)} %bitcast.175), kind=kOutput, calls=%fused_computation.2 | convolution fusion | flops 2151677952 | bytes 6295553 | tf_op jit(solution)/shard_map/dot_general | solution.py:149
  108.6 3.1 %collective-permute-start.19 = (f32[8,2048]{1,0:T(8,128)S(1)}, f32[8,2048]{1,0:T(8,128)S(1)}, u32[]{:S(2)}, u32[]{:S(2)}) collective-permute-start(f32[8,2048]{1,0:T(8,128)S(1)} %maximum_select_fusion), channel_id=1, source_target_pairs={{0,8},{16,24},{32,40},{48,56},{64,72},{80,88},{96,104},{112,120},{... | collective-permute-start | bytes 196616 | tf_op jit(solution)/shard_map/ppermute | solution.py:41
  112.7 0.7 collective-permute-start.18
  114.5 0.7 collective-permute-start.21
  116.2 0.7 collective-permute-start.23
  117.3 0.8 collective-permute-start.24
  118.1 0.9 collective-permute-start.25
  119.9 0.8 copy-done.1
  121.7 0.7 fusion.25
  123.0 0.7 collective-permute-start.26
  123.7 0.7 collective-permute-start.27
  125.0 0.7 collective-permute-start.29
  125.7 0.7 collective-permute-start.30
  127.0 0.8 collective-permute-start.31
  127.9 0.7 collective-permute-start.32
  129.2 0.7 collective-permute-start.34
  129.9 0.7 collective-permute-start.35
  131.2 0.7 collective-permute-start.36
  131.9 0.7 collective-permute-start.37
  132.6 1.3 collective-permute-start.28
  135.0 0.7 collective-permute-start.39
  135.6 14.4 %collective-permute-done.28 = bf16[8,3072]{1,0:T(8,128)(2,1)S(1)} collective-permute-done((bf16[8,3072]{1,0:T(8,128)(2,1)S(1)}, bf16[8,3072]{1,0:T(8,128)(2,1)S(1)}, u32[]{:S(2)}, u32[]{:S(2)}) %collective-permute-start.28) | collective-permute-done | bytes 49184 | tf_op jit(solution)/shard_map/ppermute | solution.py:41
  151.1 0.7 collective-permute-start.41
  153.2 0.7 collective-permute-start.43
  155.3 0.7 collective-permute-start.45
  156.0 2.3 %collective-permute-start.33 = (f32[8,2048]{1,0:T(8,128)S(1)}, f32[8,2048]{1,0:T(8,128)S(1)}, u32[]{:S(2)}, u32[]{:S(2)}) collective-permute-start(f32[8,2048]{1,0:T(8,128)S(1)} %pad_maximum_fusion.4), channel_id=1, source_target_pairs={{0,8},{16,24},{32,40},{48,56},{64,72},{80,88},{96,104},{112,120},{... | collective-permute-start | bytes 196616 | tf_op jit(solution)/shard_map/ppermute | solution.py:41
  159.4 0.7 collective-permute-start.47
  161.6 51.7 %all_to_all.15 = f32[16,8,128]{2,1,0:T(8,128)S(1)} all-to-all(f32[16,8,128]{2,1,0:T(8,128)S(1)} %pad_maximum_fusion.5), channel_id=1, replica_groups=mesh['pair'=32,'side'=2,'y'=4,'core'=2] {'side','y','core'}, dimensions={0} | all-to-all | bytes 131072 | tf_op jit(solution)/shard_map/all_to_all | solution.py:261
  (176 shorter events, 26.2 us)
Async XLA Ops:
  7.2 24.0 %copy-start.7 = (bf16[2,128,1024]{2,1,0:T(8,128)(2,1)S(1)}, bf16[2,128,1024]{2,1,0:T(8,128)(2,1)}, u32[]{:S(2)}) copy-start(bf16[2,128,1024]{2,1,0:T(8,128)(2,1)} %param.10) | copy-start | bytes 1572868
  7.2 24.0 %copy-start.6 = (bf16[2,128,1024]{2,1,0:T(8,128)(2,1)S(1)}, bf16[2,128,1024]{2,1,0:T(8,128)(2,1)}, u32[]{:S(2)}) copy-start(bf16[2,128,1024]{2,1,0:T(8,128)(2,1)} %param.9) | copy-start | bytes 1572868
  8.2 28.7 %collective-permute-start.2 = (bf16[128,1024]{1,0:T(8,128)(2,1)S(1)}, bf16[128,1024]{1,0:T(8,128)(2,1)S(1)}, u32[]{:S(2)}, u32[]{:S(2)}) collective-permute-start(bf16[128,1024]{1,0:T(8,128)(2,1)S(1)} %slice_bitcast_fusion.2), channel_id=1, source_target_pairs={{0,4},{2,6},{4,0},{6,2},{1,5},{3,7},{5,1},{7,3},{8,12},{10,14},{12... | collective-permute-start | bytes 786440 | tf_op jit(solution)/shard_map/ppermute | solution.py:48
  13.9 21.2 %collective-permute-start.1 = (bf16[128,1024]{1,0:T(8,128)(2,1)S(1)}, bf16[128,1024]{1,0:T(8,128)(2,1)S(1)}, u32[]{:S(2)}, u32[]{:S(2)}) collective-permute-start(bf16[128,1024]{1,0:T(8,128)(2,1)S(1)} %slice_bitcast_fusion.2), channel_id=1, source_target_pairs={{0,6},{2,0},{4,2},{6,4},{1,7},{3,1},{5,3},{7,5},{8,14},{10,8},{12,... | collective-permute-start | bytes 786440 | tf_op jit(solution)/shard_map/ppermute | solution.py:48
  16.6 18.0 %collective-permute-start = (bf16[128,1024]{1,0:T(8,128)(2,1)S(1)}, bf16[128,1024]{1,0:T(8,128)(2,1)S(1)}, u32[]{:S(2)}, u32[]{:S(2)}) collective-permute-start(bf16[128,1024]{1,0:T(8,128)(2,1)S(1)} %slice_bitcast_fusion.2), channel_id=1, source_target_pairs={{0,2},{2,4},{4,6},{6,0},{1,3},{3,5},{5,7},{7,1},{8,10},{10,12},{12... | collective-permute-start | bytes 786440 | tf_op jit(solution)/shard_map/ppermute | solution.py:48
  21.8 21.2 %slice-start = ((bf16[2,128,1024]{2,1,0:T(8,128)(2,1)}), bf16[1,128,1024]{2,1,0:T(8,128)(2,1)S(1)}, s32[]{:S(2)}) async-start(bf16[2,128,1024]{2,1,0:T(8,128)(2,1)} %param.9), calls=%async_computation.4 | async-start | bytes 524288 | tf_op jit(solution)/shard_map/slice | solution.py:126
  22.6 16.6 %all-to-all-start = ((bf16[16,88,128]{2,1,0:T(8,128)(2,1)}), bf16[16,88,128]{2,1,0:T(8,128)(2,1)S(1)}, u32[]{:S(2)}, u32[]{:S(2)}) async-start(bf16[16,88,128]{2,1,0:T(8,128)(2,1)} %pad_maximum_fusion.2), calls=%async_computation | async-start | bytes 720896 | tf_op jit(solution)/shard_map/all_to_all | solution.py:106
  31.1 63.8 %all-gather.3.cloned.1.call-start = ((), (), s32[]{:S(2)}) async-start(), calls=%async_computation.3 | async-start | bytes 7077888 | tf_op jit(solution)/shard_map/all_gather | solution.py:127
  31.2 11.7 %collective-permute-start.14 = (bf16[128,1024]{1,0:T(8,128)(2,1)S(1)}, bf16[128,1024]{1,0:T(8,128)(2,1)S(1)}, u32[]{:S(2)}, u32[]{:S(2)}) collective-permute-start(bf16[128,1024]{1,0:T(8,128)(2,1)S(1)} %bitcast_select_fusion.1), channel_id=1, source_target_pairs={{0,8},{16,24},{32,40},{48,56},{64,72},{80,88},{96,104},{112,120},{... | collective-permute-start | bytes 786440 | tf_op jit(solution)/shard_map/ppermute | solution.py:41
  34.6 9.6 %copy-start.9 = (bf16[128,1024]{1,0:T(8,128)(2,1)}, bf16[128,1024]{1,0:T(8,128)(2,1)S(1)}, u32[]{:S(2)}) copy-start(bf16[128,1024]{1,0:T(8,128)(2,1)S(1)} %collective-permute-done) | copy-start | bytes 786436
  35.1 9.1 %copy-start.8 = (bf16[128,1024]{1,0:T(8,128)(2,1)}, bf16[128,1024]{1,0:T(8,128)(2,1)S(1)}, u32[]{:S(2)}) copy-start(bf16[128,1024]{1,0:T(8,128)(2,1)S(1)} %collective-permute-done.1) | copy-start | bytes 786436
  43.0 5.1 %copy-start.11 = (f32[1,128]{1,0:T(1,128)S(1)}, f32[1,128]{1,0:T(1,128)}, u32[]{:S(2)}) copy-start(f32[1,128]{1,0:T(1,128)} %param.13) | copy-start | bytes 1540
  43.0 5.1 %copy-start.12 = (s32[1,128]{1,0:T(1,128)S(1)}, s32[1,128]{1,0:T(1,128)}, u32[]{:S(2)}) copy-start(s32[1,128]{1,0:T(1,128)} %param.12) | copy-start | bytes 1540
  45.3 15.3 %collective-permute-start.3 = (bf16[512,1024]{1,0:T(8,128)(2,1)S(1)}, bf16[512,1024]{1,0:T(8,128)(2,1)}, u32[]{:S(2)}, u32[]{:S(2)}) collective-permute-start(bf16[512,1024]{1,0:T(8,128)(2,1)S(1)} %pad_maximum_fusion), channel_id=1, source_target_pairs={{0,1},{1,0},{2,3},{3,2},{4,5},{5,4},{6,7},{7,6},{8,9},{9,8},{10,11... | collective-permute-start | bytes 3145736 | tf_op jit(solution)/shard_map/ppermute | solution.py:58
  49.1 10.0 %all-to-all-start.1 = ((bf16[16,8,128]{2,1,0:T(8,128)(2,1)}), bf16[16,8,128]{2,1,0:T(8,128)(2,1)S(1)}, u32[]{:S(2)}, u32[]{:S(2)}) async-start(bf16[16,8,128]{2,1,0:T(8,128)(2,1)} %pad_maximum_fusion.7), calls=%async_computation.1 | async-start | bytes 65536 | tf_op jit(solution)/shard_map/all_to_all | solution.py:131
  63.3 5.2 %collective-permute-start.4 = (bf16[8,1024]{1,0:T(8,128)(2,1)S(1)}, bf16[8,1024]{1,0:T(8,128)(2,1)S(1)}, u32[]{:S(2)}, u32[]{:S(2)}) collective-permute-start(bf16[8,1024]{1,0:T(8,128)(2,1)S(1)} %fusion.36), channel_id=1, source_target_pairs={{8,16},{40,48},{72,80},{104,112},{136,144},{168,176},{200,208},{23... | collective-permute-start | bytes 49160 | tf_op jit(solution)/shard_map/ppermute | solution.py:41
  64.0 4.6 %collective-permute-start.5 = (bf16[8,1024]{1,0:T(8,128)(2,1)S(1)}, bf16[8,1024]{1,0:T(8,128)(2,1)S(1)}, u32[]{:S(2)}, u32[]{:S(2)}) collective-permute-start(bf16[8,1024]{1,0:T(8,128)(2,1)S(1)} %fusion.36), channel_id=1, source_target_pairs={{24,16},{56,48},{88,80},{120,112},{152,144},{184,176},{216,208},{2... | collective-permute-start | bytes 49160 | tf_op jit(solution)/shard_map/ppermute | solution.py:41
  69.2 1.4 collective-permute-start.6
  69.9 0.7 collective-permute-start.7
  71.2 1.4 collective-permute-start.8
  71.9 0.7 collective-permute-start.9
  73.3 1.4 collective-permute-start.10
  73.9 0.7 collective-permute-start.11
  75.3 24.4 %collective-permute-start.12 = (bf16[8,1024]{1,0:T(8,128)(2,1)S(1)}, bf16[8,1024]{1,0:T(8,128)(2,1)S(1)}, u32[]{:S(2)}, u32[]{:S(2)}) collective-permute-start(bf16[8,1024]{1,0:T(8,128)(2,1)S(1)} %convolution_convert_fusion.5), channel_id=1, source_target_pairs={{128,256},{129,257},{130,258},{131,259},{132,260},{133,261},{134,2... | collective-permute-start | bytes 49160 | tf_op jit(solution)/shard_map/ppermute | solution.py:41
  76.0 23.7 %collective-permute-start.13 = (bf16[8,1024]{1,0:T(8,128)(2,1)S(1)}, bf16[8,1024]{1,0:T(8,128)(2,1)S(1)}, u32[]{:S(2)}, u32[]{:S(2)}) collective-permute-start(bf16[8,1024]{1,0:T(8,128)(2,1)S(1)} %convolution_convert_fusion.5), channel_id=1, source_target_pairs={{384,256},{385,257},{386,258},{387,259},{388,260},{389,261},{390,2... | collective-permute-start | bytes 49160 | tf_op jit(solution)/shard_map/ppermute | solution.py:41
  94.9 6.5 %slice-start.2 = ((s8[6291456]{0:T(1024)(128)(4,1)}), s8[4194304]{0:T(1024)(128)(4,1)S(1)}, s32[]{:S(2)}) async-start(s8[6291456]{0:T(1024)(128)(4,1)} %bitcast.172), calls=%async_computation.6 | async-start | bytes 8388608
  94.9 6.5 %slice-start.3 = ((s8[6291456]{0:T(1024)(128)(4,1)}), s8[2097152]{0:T(1024)(128)(4,1)S(1)}, s32[]{:S(2)}) async-start(s8[6291456]{0:T(1024)(128)(4,1)} %bitcast.172), calls=%async_computation.7 | async-start | bytes 4194304
  100.1 11.5 %collective-permute-start.15 = (bf16[8,1024]{1,0:T(8,128)(2,1)S(1)}, bf16[8,1024]{1,0:T(8,128)(2,1)S(1)}, u32[]{:S(2)}, u32[]{:S(2)}) collective-permute-start(bf16[8,1024]{1,0:T(8,128)(2,1)S(1)} %get-tuple-element.130), channel_id=1, source_target_pairs={{256,128},{257,129},{258,130},{259,131},{260,132},{261,133},{262,1... | collective-permute-start | bytes 49160 | tf_op jit(solution)/shard_map/ppermute | solution.py:41
  100.8 10.9 %collective-permute-start.16 = (bf16[8,1024]{1,0:T(8,128)(2,1)S(1)}, bf16[8,1024]{1,0:T(8,128)(2,1)S(1)}, u32[]{:S(2)}, u32[]{:S(2)}) collective-permute-start(bf16[8,1024]{1,0:T(8,128)(2,1)S(1)} %get-tuple-element.130), channel_id=1, source_target_pairs={{256,384},{257,385},{258,386},{259,387},{260,388},{261,389},{262,3... | collective-permute-start | bytes 49160 | tf_op jit(solution)/shard_map/ppermute | solution.py:41
  104.3 3.2 %copy-start = (bf16[1024,1024]{1,0:T(8,128)(2,1)}, bf16[1024,1024]{1,0:T(8,128)(2,1)S(1)}, u32[]{:S(2)}) copy-start(bf16[1024,1024]{1,0:T(8,128)(2,1)S(1)} %bitcast_convert_fusion.1) | copy-start | bytes 6291460
  108.6 4.9 %collective-permute-start.19 = (f32[8,2048]{1,0:T(8,128)S(1)}, f32[8,2048]{1,0:T(8,128)S(1)}, u32[]{:S(2)}, u32[]{:S(2)}) collective-permute-start(f32[8,2048]{1,0:T(8,128)S(1)} %maximum_select_fusion), channel_id=1, source_target_pairs={{0,8},{16,24},{32,40},{48,56},{64,72},{80,88},{96,104},{112,120},{... | collective-permute-start | bytes 196616 | tf_op jit(solution)/shard_map/ppermute | solution.py:41
  112.1 1.3 collective-permute-start.17
  112.7 0.7 collective-permute-start.18
  113.8 1.3 collective-permute-start.20
  114.5 0.7 collective-permute-start.21
  115.6 1.4 collective-permute-start.22
  116.2 0.7 collective-permute-start.23
  117.3 1.7 collective-permute-start.24
  118.1 0.9 collective-permute-start.25
  123.0 1.3 collective-permute-start.26
  123.7 0.7 collective-permute-start.27
  125.0 1.3 collective-permute-start.29
  125.7 0.7 collective-permute-start.30
  127.0 6.8 %copy-start.5 = (bf16[1024,1024]{1,0:T(8,128)(2,1)S(1)}, bf16[1024,1024]{1,0:T(8,128)(2,1)}, u32[]{:S(2)}) copy-start(bf16[1024,1024]{1,0:T(8,128)(2,1)} %copy-done.4) | copy-start | bytes 6291460
  127.0 1.5 collective-permute-start.31
  127.9 0.7 collective-permute-start.32
  129.2 1.4 collective-permute-start.34
  129.9 0.7 collective-permute-start.35
  131.2 2.7 %collective-permute-start.36 = (bf16[8,1024]{1,0:T(8,128)(2,1)S(1)}, bf16[8,1024]{1,0:T(8,128)(2,1)S(1)}, u32[]{:S(2)}, u32[]{:S(2)}) collective-permute-start(bf16[8,1024]{1,0:T(8,128)(2,1)S(1)} %convolution_convert_fusion), channel_id=1, source_target_pairs={{128,256},{129,257},{130,258},{131,259},{132,260},{133,261},{134,2... | collective-permute-start | bytes 49160 | tf_op jit(solution)/shard_map/ppermute | solution.py:41
  131.9 2.0 collective-permute-start.37
  132.6 17.5 %collective-permute-start.28 = (bf16[8,3072]{1,0:T(8,128)(2,1)S(1)}, bf16[8,3072]{1,0:T(8,128)(2,1)S(1)}, u32[]{:S(2)}, u32[]{:S(2)}) collective-permute-start(bf16[8,3072]{1,0:T(8,128)(2,1)S(1)} %pad_maximum_fusion.6), channel_id=1, source_target_pairs={{8,0},{24,16},{40,32},{56,48},{72,64},{88,80},{104,96},{120,112},{... | collective-permute-start | bytes 147464 | tf_op jit(solution)/shard_map/ppermute | solution.py:41
  134.3 15.8 %collective-permute-start.38 = (bf16[8,1024]{1,0:T(8,128)(2,1)S(1)}, bf16[8,1024]{1,0:T(8,128)(2,1)S(1)}, u32[]{:S(2)}, u32[]{:S(2)}) collective-permute-start(bf16[8,1024]{1,0:T(8,128)(2,1)S(1)} %get-tuple-element.132), channel_id=1, source_target_pairs={{256,128},{257,129},{258,130},{259,131},{260,132},{261,133},{262,1... | collective-permute-start | bytes 49160 | tf_op jit(solution)/shard_map/ppermute | solution.py:41
  135.0 15.1 %collective-permute-start.39 = (bf16[8,1024]{1,0:T(8,128)(2,1)S(1)}, bf16[8,1024]{1,0:T(8,128)(2,1)S(1)}, u32[]{:S(2)}, u32[]{:S(2)}) collective-permute-start(bf16[8,1024]{1,0:T(8,128)(2,1)S(1)} %get-tuple-element.132), channel_id=1, source_target_pairs={{256,384},{257,385},{258,386},{259,387},{260,388},{261,389},{262,3... | collective-permute-start | bytes 49160 | tf_op jit(solution)/shard_map/ppermute | solution.py:41
  150.0 6.0 %copy-start.10 = (bf16[8,3072]{1,0:T(8,128)(2,1)}, bf16[8,3072]{1,0:T(8,128)(2,1)S(1)}, u32[]{:S(2)}) copy-start(bf16[8,3072]{1,0:T(8,128)(2,1)S(1)} %collective-permute-done.28) | copy-start | bytes 147460
  150.4 1.7 collective-permute-start.40
  151.1 1.1 collective-permute-start.41
  152.6 1.7 collective-permute-start.42
  153.2 1.1 collective-permute-start.43
  154.7 3.6 %collective-permute-start.44 = (bf16[8,1024]{1,0:T(8,128)(2,1)S(1)}, bf16[8,1024]{1,0:T(8,128)(2,1)S(1)}, u32[]{:S(2)}, u32[]{:S(2)}) collective-permute-start(bf16[8,1024]{1,0:T(8,128)(2,1)S(1)} %fusion.39), channel_id=1, source_target_pairs={{32,16},{96,80},{160,144},{224,208},{288,272},{352,336},{416,400},... | collective-permute-start | bytes 49160 | tf_op jit(solution)/shard_map/ppermute | solution.py:41
  155.3 3.0 %collective-permute-start.45 = (bf16[8,1024]{1,0:T(8,128)(2,1)S(1)}, bf16[8,1024]{1,0:T(8,128)(2,1)S(1)}, u32[]{:S(2)}, u32[]{:S(2)}) collective-permute-start(bf16[8,1024]{1,0:T(8,128)(2,1)S(1)} %fusion.39), channel_id=1, source_target_pairs={{32,48},{96,112},{160,176},{224,240},{288,304},{352,368},{416,432}... | collective-permute-start | bytes 49160 | tf_op jit(solution)/shard_map/ppermute | solution.py:41
  156.0 4.0 %slice-start.1 = ((bf16[8,3072]{1,0:T(8,128)(2,1)}), bf16[8,1024]{1,0:T(8,128)(2,1)S(1)}, s32[]{:S(2)}) async-start(bf16[8,3072]{1,0:T(8,128)(2,1)} %copy-done.10), calls=%async_computation.5 | async-start | bytes 32768 | tf_op jit(solution)/shard_map/slice | solution.py:242
  156.0 5.5 %collective-permute-start.33 = (f32[8,2048]{1,0:T(8,128)S(1)}, f32[8,2048]{1,0:T(8,128)S(1)}, u32[]{:S(2)}, u32[]{:S(2)}) collective-permute-start(f32[8,2048]{1,0:T(8,128)S(1)} %pad_maximum_fusion.4), channel_id=1, source_target_pairs={{0,8},{16,24},{32,40},{48,56},{64,72},{80,88},{96,104},{112,120},{... | collective-permute-start | bytes 196616 | tf_op jit(solution)/shard_map/ppermute | solution.py:41
  158.7 1.6 collective-permute-start.46
  159.4 0.9 collective-permute-start.47
  (4 other events, 7.2 us)
Sparse Core Ops, SparseCore 0:
  44.2 50.6 all-gather.2

commit v4 on v3

--- a/solution.py
+++ b/solution.py
@@ -171,6 +171,7 @@
         if height == levels:
             blocks = after(later, token)
             got["leaf"] = [slot(blocks, 0), slot(blocks, 1)]
+            got["both"] = jnp.concatenate(got["leaf"], 1)
             send_first_leaf_t(token)
             names.append("leaf")
         if height == levels - 1:
@@ -185,7 +186,10 @@
     def forward(update, node_r, beside):
         for height in range(2, levels + 1):
             left, right = links(height, groups)
-            from_right, from_left = send(update, right), send(update, left)
+            if height == 3:
+                from_left, from_right = send(update, left), send(update, right)
+            else:
+                from_right, from_left = send(update, right), send(update, left)
             from_left, from_right = joined(beside(height, update), from_left, from_right)
             node_r = node_r - from_left.astype(jnp.float32) - from_right.astype(jnp.float32)
             if height < levels:
@@ -226,9 +230,9 @@
     leaf_t = got["leaf_t"]
     pair_weight = jnp.concatenate([leaf_t[PAD - 1, :whole], station_weight])
 
-    delta = rounded(leaf_t - leaf_step((node_x, node_x)))
+    delta = rounded(leaf_t - times(node_x, got["both"]))
     injected = rounded(delta.astype(jnp.float32) * pair_weight[None, :])
-    update = sum(times_transposed(v, m) for v, m in zip(halves(injected), got["leaf"]))
+    update = times_transposed(injected, got["both"])
     node_r = -jnp.where(odd, update, 0.0)
     update = rounded(times_transposed(rounded(node_r), got["up"]))
 
@@ -246,7 +250,7 @@
     node_r = forward(update, node_r, beside_second)
     station, leaf_t = got["station"], got["leaf_t"]
     node_x = backward(through_inverse(node_r), lambda height, token: [])
-    adjoint = rounded(leaf_t - leaf_step((node_x, node_x)))
+    adjoint = rounded(leaf_t - times(node_x, got["both"]))
     curve_leaf = jnp.sum(leaf_pair[:share].astype(jnp.float32) * adjoint[:share].astype(jnp.float32), axis=0)
     curve_node = jnp.sum(field_node.astype(jnp.float32) * node_x.astype(jnp.float32), axis=0)
 

time: 223 us -> 238 us (1.067)
  local copies, waits for them, and re-layouts: 6.96 us -> 15.5 us
  matrix products: 33.7 us -> 40.7 us
    optimization_barrier x0 -> x1, local copies, waits for them, and re-layouts: none -> 8.61 us  [after(): return lax.optimization_barrier((value,) + earlier)[0]]
    dot_general x22 -> x19, matrix products: 11.6 us -> 15.5 us  [times(): return jnp.dot(vectors, matrix, preferred_element_type=jnp.float32)]
    dot_general x16 -> x15, matrix products: 11.7 us -> 13.4 us  [times_transposed(): lax.dot_general(vectors, matrix, CONTRACT_LAST, preferred_element_type=jn...]
  transfers between devices with their start and end apart: 51 -> 51, of which waited for: 5 -> 5; matrix products, arithmetic and copies ran while one was open for 15% -> 19% of each run, Pallas kernels for 0% -> 0%
where the time goes in v4:
time: 238 us; the launch traced here: 237 us
  starting transfers between devices  65 us (27%)
  blocking collectives  51.2 us (22%)
  matrix products  40.7 us (17%)
  waiting for transfers between devices  40.1 us (17%)
  between operations  18.6 us (8%)
  local copies, waits for them, and re-layouts  15.5 us (7%)
  other arithmetic  5.41 us (2%)
    all_to_all x1, blocking collectives, per_device(): out = lax.all_to_all(out, PAIR, 0, 0, tiled=True)  51.2 us
    ppermute x44, starting transfers between devices, send(): return lax.ppermute(value, LEAF, pairs)  37.2 us
    ppermute x44, waiting for transfers between devices, send(): return lax.ppermute(value, LEAF, pairs)  17.3 us
    all_gather x1, waiting for transfers between devices, per_device(): later = lax.all_gather(later, FRONT, axis=0)  16 us
    dot_general x19, matrix products, times(): return jnp.dot(vectors, matrix, preferred_element_type=jnp.float32)  15.5 us
    dot_general x15, matrix products, times_transposed(): lax.dot_general(vectors, matrix, CONTRACT_LAST, preferred_element_type=jn...  13.4 us
    ppermute x3, starting transfers between devices, shifted(): lax.ppermute(block, 'y', [(k, (k + by) % count) for k in range(count)])  10.9 us
    all_to_all x1, starting transfers between devices, per_device(): message = lax.all_to_all(message, PAIR, 0, 0, tiled=True)  9.72 us
  transfers between devices with their start and end apart: 51, of which 5 were waited for; matrix products, arithmetic and copies ran while one was open for 19% of the time, Pallas kernels for 0%

profile of v4, /device:TPU:1, one launch (start us, length us, event | category | flops | bytes accessed | tf_op | source)
XLA Modules:
  0.0 236.6 jit_solution(2924516365557388071)
XLA Ops:
  7.2 1.1 slice_bitcast_fusion.2
  8.2 4.0 %collective-permute-start = (bf16[128,1024]{1,0:T(8,128)(2,1)S(1)}, bf16[128,1024]{1,0:T(8,128)(2,1)S(1)}, u32[]{:S(2)}, u32[]{:S(2)}) collective-permute-start(bf16[128,1024]{1,0:T(8,128)(2,1)S(1)} %slice_bitcast_fusion.2), channel_id=1, source_target_pairs={{0,2},{2,4},{4,6},{6,0},{1,3},{3,5},{5,7},{7,1},{8,10},{10,12},{12... | collective-permute-start | bytes 786440 | tf_op jit(solution)/shard_map/ppermute | solution.py:48
  12.3 3.4 %collective-permute-start.1 = (bf16[128,1024]{1,0:T(8,128)(2,1)S(1)}, bf16[128,1024]{1,0:T(8,128)(2,1)S(1)}, u32[]{:S(2)}, u32[]{:S(2)}) collective-permute-start(bf16[128,1024]{1,0:T(8,128)(2,1)S(1)} %slice_bitcast_fusion.2), channel_id=1, source_target_pairs={{0,6},{2,0},{4,2},{6,4},{1,7},{3,1},{5,3},{7,5},{8,14},{10,8},{12,... | collective-permute-start | bytes 786440 | tf_op jit(solution)/shard_map/ppermute | solution.py:48
  15.7 3.5 %collective-permute-start.2 = (bf16[128,1024]{1,0:T(8,128)(2,1)S(1)}, bf16[128,1024]{1,0:T(8,128)(2,1)S(1)}, u32[]{:S(2)}, u32[]{:S(2)}) collective-permute-start(bf16[128,1024]{1,0:T(8,128)(2,1)S(1)} %slice_bitcast_fusion.2), channel_id=1, source_target_pairs={{0,4},{2,6},{4,0},{6,2},{1,5},{3,7},{5,1},{7,3},{8,12},{10,14},{12... | collective-permute-start | bytes 786440 | tf_op jit(solution)/shard_map/ppermute | solution.py:48
  19.2 0.7 fusion.112
  19.9 0.7 fusion.111
  20.7 0.7 multiply_convert_fusion.1
  21.8 0.8 pad_maximum_fusion.10
  22.6 9.7 %all-to-all-start = ((bf16[16,88,128]{2,1,0:T(8,128)(2,1)}), bf16[16,88,128]{2,1,0:T(8,128)(2,1)S(1)}, u32[]{:S(2)}, u32[]{:S(2)}) async-start(bf16[16,88,128]{2,1,0:T(8,128)(2,1)} %pad_maximum_fusion.10), calls=%async_computation | async-start | bytes 720896 | tf_op jit(solution)/shard_map/all_to_all | solution.py:106
  32.4 3.3 %collective-permute-start.14 = (bf16[128,1024]{1,0:T(8,128)(2,1)S(1)}, bf16[128,1024]{1,0:T(8,128)(2,1)S(1)}, u32[]{:S(2)}, u32[]{:S(2)}) collective-permute-start(bf16[128,1024]{1,0:T(8,128)(2,1)S(1)} %bitcast_select_fusion.1), channel_id=1, source_target_pairs={{0,8},{16,24},{32,40},{48,56},{64,72},{80,88},{96,104},{112,120},{... | collective-permute-start | bytes 786440 | tf_op jit(solution)/shard_map/ppermute | solution.py:41
  39.4 1.0 all-to-all-done
  42.2 2.0 collective-permute-done.14
  44.3 1.0 pad_maximum_fusion.9
  45.4 1.1 pad_maximum_fusion.8
  46.5 2.8 %collective-permute-start.3 = (bf16[512,1024]{1,0:T(8,128)(2,1)S(1)}, bf16[512,1024]{1,0:T(8,128)(2,1)}, u32[]{:S(2)}, u32[]{:S(2)}) collective-permute-start(bf16[512,1024]{1,0:T(8,128)(2,1)S(1)} %pad_maximum_fusion.8), channel_id=1, source_target_pairs={{0,1},{1,0},{2,3},{3,2},{4,5},{5,4},{6,7},{7,6},{8,9},{9,8},{10,11... | collective-permute-start | bytes 3145736 | tf_op jit(solution)/shard_map/ppermute | solution.py:58
  50.3 4.4 %all-to-all-start.1 = ((bf16[16,8,128]{2,1,0:T(8,128)(2,1)}), bf16[16,8,128]{2,1,0:T(8,128)(2,1)S(1)}, u32[]{:S(2)}, u32[]{:S(2)}) async-start(bf16[16,8,128]{2,1,0:T(8,128)(2,1)} %pad_maximum_fusion.14), calls=%async_computation.1 | async-start | bytes 65536 | tf_op jit(solution)/shard_map/all_to_all | solution.py:131
  54.7 5.8 %all-to-all-done.1 = bf16[16,8,128]{2,1,0:T(8,128)(2,1)S(1)} async-done(((bf16[16,8,128]{2,1,0:T(8,128)(2,1)}), bf16[16,8,128]{2,1,0:T(8,128)(2,1)S(1)}, u32[]{:S(2)}, u32[]{:S(2)}) %all-to-all-start.1) | async-done | bytes 32800 | tf_op jit(solution)/shard_map/all_to_all | solution.py:131
  60.5 1.5 fusion.26
  62.0 2.0 fusion.18
  64.0 0.7 fusion.37
  65.4 0.7 collective-permute-start.5
  66.1 2.5 %fusion.17 = f32[1024,1024]{1,0:T(8,128)S(1)} fusion(bf16[512,1024]{1,0:T(8,128)(2,1)} %collective-permute-done.3, s32[512]{0:T(512)S(1)} %bitcast.159), kind=kOutput, calls=%fused_computation.26 | convolution fusion | flops 1074266112 | bytes 5244928 | tf_op jit(solution)/shard_map/dot_general | solution.py:19
  68.5 1.3 add_convert_fusion
  70.5 0.7 collective-permute-start.6
  71.2 0.7 collective-permute-start.7
  72.6 0.7 collective-permute-start.8
  73.2 0.7 collective-permute-start.9
  74.6 0.7 collective-permute-start.10
  75.3 0.7 collective-permute-start.11
  76.6 0.7 collective-permute-start.12
  77.3 0.8 collective-permute-start.13
  78.2 16.0 %all-gather.3.cloned.1.call-done = bf16[24,128,1024]{2,1,0:T(8,128)(2,1)} async-done(((bf16[3,128,1024]{2,1,0:T(8,128)(2,1)}), bf16[24,128,1024]{2,1,0:T(8,128)(2,1)}) %all-gather.3.cloned.1.call-update) | async-done | bytes 6291472 | tf_op jit(solution)/shard_map/all_gather | solution.py:127
  94.2 4.6 %bitcast_convert_fusion.2 = bf16[1024,1024]{1,0:T(8,128)(2,1)S(1)} fusion(bf16[8,3,128,1024]{3,2,1,0:T(8,128)(2,1)} %bitcast.142), kind=kOutput, calls=%fused_computation.5 | convolution fusion | flops 2148532224 | bytes 4194304 | tf_op jit(solution)/shard_map/dot_general | solution.py:162
  98.8 1.3 copy-done.4
  101.2 0.7 collective-permute-start.16
  101.8 8.6 %copy.37 = bf16[8,3,128,1024]{2,3,0,1:T(8,128)(2,1)} copy(bf16[8,3,128,1024]{3,2,1,0:T(8,128)(2,1)} %bitcast.143) | data formatting | bytes 12582912 | tf_op jit(solution)/shard_map/optimization_barrier | solution.py:27
  110.4 4.8 %bitcast_convert_fusion.1 = bf16[1024,1024]{0,1:T(8,128)(2,1)S(1)} fusion(bf16[8,3,128,1024]{2,3,0,1:T(8,128)(2,1)} %copy.37, s32[8,128]{1,0:T(8,128)S(1)} %get-tuple-element.123, pred[]{:T(512)S(6)} %eq.132), kind=kOutput, calls=%fused_computation.4 | convolution fusion | flops 2151677952 | bytes 6295553 | tf_op jit(solution)/shard_map/dot_general | solution.py:149
  115.2 2.4 %bitcast_convert_fusion = bf16[1024,1024]{0,1:T(8,128)(2,1)S(1)} fusion(bf16[8,3,128,1024]{2,3,0,1:T(8,128)(2,1)S(1)} %copy-done.6, s32[8,128]{1,0:T(8,128)S(1)} %get-tuple-element.122, pred[]{:T(512)S(6)} %eq.132), kind=kOutput, calls=%fused_computation.3 | convolution fusion | flops 2151677952 | bytes 6295553 | tf_op jit(solution)/shard_map/dot_general | solution.py:149
  119.1 3.1 %collective-permute-start.19 = (f32[8,2048]{1,0:T(8,128)S(1)}, f32[8,2048]{1,0:T(8,128)S(1)}, u32[]{:S(2)}, u32[]{:S(2)}) collective-permute-start(f32[8,2048]{1,0:T(8,128)S(1)} %maximum_select_fusion), channel_id=1, source_target_pairs={{0,8},{16,24},{32,40},{48,56},{64,72},{80,88},{96,104},{112,120},{... | collective-permute-start | bytes 196616 | tf_op jit(solution)/shard_map/ppermute | solution.py:41
  123.2 0.7 collective-permute-start.18
  125.0 0.7 collective-permute-start.21
  126.7 0.7 collective-permute-start.23
  128.5 0.7 collective-permute-start.25
  129.2 3.7 %multiply_convert_fusion = (bf16[8,2048]{1,0:T(8,128)(2,1)S(1)}, bf16[8,2048]{1,0:T(8,128)(2,1)S(1)}) fusion(f32[2048]{0:T(1024)S(1)} %pad_maximum_fusion.15, f32[8,2048]{1,0:T(8,128)S(1)} %collective-permute-done.19, bf16[1024,1024]{0,1:T(8,128)(2,1)} %copy-done.2, bf16[1024,1024]{0,1:T(8,128)(2,1)} %copy-done, bf16[8,1024]{1,0:T(8,128)(2,1)S(1)} %fusion.46, ...), kind=kOutput, calls=%fused_computation.112 | convolution fusion | flops 58834944 | bytes 6512641 | tf_op jit(solution)/shard_map/dot_general | solution.py:19
  132.9 2.9 %fusion.39 = f32[8,1024]{1,0:T(8,128)S(1)} fusion(bf16[8,2048]{1,0:T(8,128)(2,1)S(1)} %get-tuple-element.130, bf16[1024,1024]{0,1:T(8,128)(2,1)} %copy-done.2, bf16[1024,1024]{0,1:T(8,128)(2,1)} %copy-done, pred[]{:T(512)S(6)} %eq.132), kind=kOutput, calls=%fused_computation.69 | convolution fusion | flops 41959424 | bytes 4259841 | tf_op jit(solution)/shard_map/dot_general | solution.py:15
  136.4 0.7 collective-permute-start.26
  137.1 0.9 collective-permute-start.27
  138.7 0.7 collective-permute-start.29
  139.3 0.7 collective-permute-start.30
  140.7 0.8 collective-permute-start.31
  141.5 0.7 collective-permute-start.32
  142.8 0.7 collective-permute-start.34
  143.5 0.7 collective-permute-start.35
  144.9 0.7 collective-permute-start.36
  145.5 0.7 collective-permute-start.37
  146.2 1.4 collective-permute-start.28
  148.7 0.7 collective-permute-start.39
  149.4 15.2 %collective-permute-done.28 = bf16[8,3072]{1,0:T(8,128)(2,1)S(1)} collective-permute-done((bf16[8,3072]{1,0:T(8,128)(2,1)S(1)}, bf16[8,3072]{1,0:T(8,128)(2,1)S(1)}, u32[]{:S(2)}, u32[]{:S(2)}) %collective-permute-start.28) | collective-permute-done | bytes 49184 | tf_op jit(solution)/shard_map/ppermute | solution.py:41
  165.0 0.8 collective-permute-start.40
  165.8 0.7 collective-permute-start.41
  168.2 0.7 collective-permute-start.43
  171.3 2.3 collective-permute-start.33
  176.0 1.2 fusion.22
  177.3 51.2 %all_to_all.15 = f32[16,8,128]{2,1,0:T(8,128)S(1)} all-to-all(f32[16,8,128]{2,1,0:T(8,128)S(1)} %pad_maximum_fusion.12), channel_id=1, replica_groups=mesh['pair'=32,'side'=2,'y'=4,'core'=2] {'side','y','core'}, dimensions={0} | all-to-all | bytes 131072 | tf_op jit(solution)/shard_map/all_to_all | solution.py:265
  (169 shorter events, 26.1 us)
Async XLA Ops:
  7.2 25.2 %copy-start.8 = (bf16[2,128,1024]{2,1,0:T(8,128)(2,1)S(1)}, bf16[2,128,1024]{2,1,0:T(8,128)(2,1)}, u32[]{:S(2)}) copy-start(bf16[2,128,1024]{2,1,0:T(8,128)(2,1)} %param.10) | copy-start | bytes 1572868
  7.2 25.2 %copy-start.7 = (bf16[2,128,1024]{2,1,0:T(8,128)(2,1)S(1)}, bf16[2,128,1024]{2,1,0:T(8,128)(2,1)}, u32[]{:S(2)}) copy-start(bf16[2,128,1024]{2,1,0:T(8,128)(2,1)} %param.9) | copy-start | bytes 1572868
  8.2 27.5 %collective-permute-start = (bf16[128,1024]{1,0:T(8,128)(2,1)S(1)}, bf16[128,1024]{1,0:T(8,128)(2,1)S(1)}, u32[]{:S(2)}, u32[]{:S(2)}) collective-permute-start(bf16[128,1024]{1,0:T(8,128)(2,1)S(1)} %slice_bitcast_fusion.2), channel_id=1, source_target_pairs={{0,2},{2,4},{4,6},{6,0},{1,3},{3,5},{5,7},{7,1},{8,10},{10,12},{12... | collective-permute-start | bytes 786440 | tf_op jit(solution)/shard_map/ppermute | solution.py:48
  12.3 24.0 %collective-permute-start.1 = (bf16[128,1024]{1,0:T(8,128)(2,1)S(1)}, bf16[128,1024]{1,0:T(8,128)(2,1)S(1)}, u32[]{:S(2)}, u32[]{:S(2)}) collective-permute-start(bf16[128,1024]{1,0:T(8,128)(2,1)S(1)} %slice_bitcast_fusion.2), channel_id=1, source_target_pairs={{0,6},{2,0},{4,2},{6,4},{1,7},{3,1},{5,3},{7,5},{8,14},{10,8},{12,... | collective-permute-start | bytes 786440 | tf_op jit(solution)/shard_map/ppermute | solution.py:48
  15.7 22.5 %collective-permute-start.2 = (bf16[128,1024]{1,0:T(8,128)(2,1)S(1)}, bf16[128,1024]{1,0:T(8,128)(2,1)S(1)}, u32[]{:S(2)}, u32[]{:S(2)}) collective-permute-start(bf16[128,1024]{1,0:T(8,128)(2,1)S(1)} %slice_bitcast_fusion.2), channel_id=1, source_target_pairs={{0,4},{2,6},{4,0},{6,2},{1,5},{3,7},{5,1},{7,3},{8,12},{10,14},{12... | collective-permute-start | bytes 786440 | tf_op jit(solution)/shard_map/ppermute | solution.py:48
  21.8 22.4 %slice-start = ((bf16[2,128,1024]{2,1,0:T(8,128)(2,1)}), bf16[1,128,1024]{2,1,0:T(8,128)(2,1)S(1)}, s32[]{:S(2)}) async-start(bf16[2,128,1024]{2,1,0:T(8,128)(2,1)} %param.9), calls=%async_computation.4 | async-start | bytes 524288 | tf_op jit(solution)/shard_map/slice | solution.py:126
  22.6 17.8 %all-to-all-start = ((bf16[16,88,128]{2,1,0:T(8,128)(2,1)}), bf16[16,88,128]{2,1,0:T(8,128)(2,1)S(1)}, u32[]{:S(2)}, u32[]{:S(2)}) async-start(bf16[16,88,128]{2,1,0:T(8,128)(2,1)} %pad_maximum_fusion.10), calls=%async_computation | async-start | bytes 720896 | tf_op jit(solution)/shard_map/all_to_all | solution.py:106
  32.3 61.9 %all-gather.3.cloned.1.call-start = ((), (), s32[]{:S(2)}) async-start(), calls=%async_computation.3 | async-start | bytes 7077888 | tf_op jit(solution)/shard_map/all_gather | solution.py:127
  32.4 11.7 %collective-permute-start.14 = (bf16[128,1024]{1,0:T(8,128)(2,1)S(1)}, bf16[128,1024]{1,0:T(8,128)(2,1)S(1)}, u32[]{:S(2)}, u32[]{:S(2)}) collective-permute-start(bf16[128,1024]{1,0:T(8,128)(2,1)S(1)} %bitcast_select_fusion.1), channel_id=1, source_target_pairs={{0,8},{16,24},{32,40},{48,56},{64,72},{80,88},{96,104},{112,120},{... | collective-permute-start | bytes 786440 | tf_op jit(solution)/shard_map/ppermute | solution.py:41
  36.3 9.1 %copy-start.9 = (bf16[128,1024]{1,0:T(8,128)(2,1)}, bf16[128,1024]{1,0:T(8,128)(2,1)S(1)}, u32[]{:S(2)}) copy-start(bf16[128,1024]{1,0:T(8,128)(2,1)S(1)} %collective-permute-done.1) | copy-start | bytes 786436
  38.1 7.2 %copy-start.10 = (bf16[128,1024]{1,0:T(8,128)(2,1)}, bf16[128,1024]{1,0:T(8,128)(2,1)S(1)}, u32[]{:S(2)}) copy-start(bf16[128,1024]{1,0:T(8,128)(2,1)S(1)} %collective-permute-done.2) | copy-start | bytes 786436
  44.2 5.1 %copy-start.12 = (f32[1,128]{1,0:T(1,128)S(1)}, f32[1,128]{1,0:T(1,128)}, u32[]{:S(2)}) copy-start(f32[1,128]{1,0:T(1,128)} %param.13) | copy-start | bytes 1540
  44.2 5.1 %copy-start.13 = (s32[1,128]{1,0:T(1,128)S(1)}, s32[1,128]{1,0:T(1,128)}, u32[]{:S(2)}) copy-start(s32[1,128]{1,0:T(1,128)} %param.12) | copy-start | bytes 1540
  46.5 15.5 %collective-permute-start.3 = (bf16[512,1024]{1,0:T(8,128)(2,1)S(1)}, bf16[512,1024]{1,0:T(8,128)(2,1)}, u32[]{:S(2)}, u32[]{:S(2)}) collective-permute-start(bf16[512,1024]{1,0:T(8,128)(2,1)S(1)} %pad_maximum_fusion.8), channel_id=1, source_target_pairs={{0,1},{1,0},{2,3},{3,2},{4,5},{5,4},{6,7},{7,6},{8,9},{9,8},{10,11... | collective-permute-start | bytes 3145736 | tf_op jit(solution)/shard_map/ppermute | solution.py:58
  50.3 10.2 %all-to-all-start.1 = ((bf16[16,8,128]{2,1,0:T(8,128)(2,1)}), bf16[16,8,128]{2,1,0:T(8,128)(2,1)S(1)}, u32[]{:S(2)}, u32[]{:S(2)}) async-start(bf16[16,8,128]{2,1,0:T(8,128)(2,1)} %pad_maximum_fusion.14), calls=%async_computation.1 | async-start | bytes 65536 | tf_op jit(solution)/shard_map/all_to_all | solution.py:131
  64.7 5.1 %collective-permute-start.4 = (bf16[8,1024]{1,0:T(8,128)(2,1)S(1)}, bf16[8,1024]{1,0:T(8,128)(2,1)S(1)}, u32[]{:S(2)}, u32[]{:S(2)}) collective-permute-start(bf16[8,1024]{1,0:T(8,128)(2,1)S(1)} %fusion.37), channel_id=1, source_target_pairs={{8,16},{40,48},{72,80},{104,112},{136,144},{168,176},{200,208},{23... | collective-permute-start | bytes 49160 | tf_op jit(solution)/shard_map/ppermute | solution.py:41
  65.4 4.5 %collective-permute-start.5 = (bf16[8,1024]{1,0:T(8,128)(2,1)S(1)}, bf16[8,1024]{1,0:T(8,128)(2,1)S(1)}, u32[]{:S(2)}, u32[]{:S(2)}) collective-permute-start(bf16[8,1024]{1,0:T(8,128)(2,1)S(1)} %fusion.37), channel_id=1, source_target_pairs={{24,16},{56,48},{88,80},{120,112},{152,144},{184,176},{216,208},{2... | collective-permute-start | bytes 49160 | tf_op jit(solution)/shard_map/ppermute | solution.py:41
  70.5 1.4 collective-permute-start.6
  71.2 0.7 collective-permute-start.7
  72.6 1.4 collective-permute-start.8
  73.2 0.7 collective-permute-start.9
  74.6 1.4 collective-permute-start.10
  75.3 0.7 collective-permute-start.11
  76.6 22.2 %collective-permute-start.12 = (bf16[8,1024]{1,0:T(8,128)(2,1)S(1)}, bf16[8,1024]{1,0:T(8,128)(2,1)S(1)}, u32[]{:S(2)}, u32[]{:S(2)}) collective-permute-start(bf16[8,1024]{1,0:T(8,128)(2,1)S(1)} %convolution_convert_fusion.5), channel_id=1, source_target_pairs={{128,256},{129,257},{130,258},{131,259},{132,260},{133,261},{134,2... | collective-permute-start | bytes 49160 | tf_op jit(solution)/shard_map/ppermute | solution.py:41
  77.3 21.5 %collective-permute-start.13 = (bf16[8,1024]{1,0:T(8,128)(2,1)S(1)}, bf16[8,1024]{1,0:T(8,128)(2,1)S(1)}, u32[]{:S(2)}, u32[]{:S(2)}) collective-permute-start(bf16[8,1024]{1,0:T(8,128)(2,1)S(1)} %convolution_convert_fusion.5), channel_id=1, source_target_pairs={{384,256},{385,257},{386,258},{387,259},{388,260},{389,261},{390,2... | collective-permute-start | bytes 49160 | tf_op jit(solution)/shard_map/ppermute | solution.py:41
  100.5 21.7 %collective-permute-start.15 = (bf16[8,1024]{1,0:T(8,128)(2,1)S(1)}, bf16[8,1024]{1,0:T(8,128)(2,1)S(1)}, u32[]{:S(2)}, u32[]{:S(2)}) collective-permute-start(bf16[8,1024]{1,0:T(8,128)(2,1)S(1)} %get-tuple-element.128), channel_id=1, source_target_pairs={{256,128},{257,129},{258,130},{259,131},{260,132},{261,133},{262,1... | collective-permute-start | bytes 49160 | tf_op jit(solution)/shard_map/ppermute | solution.py:41
  101.2 21.0 %collective-permute-start.16 = (bf16[8,1024]{1,0:T(8,128)(2,1)S(1)}, bf16[8,1024]{1,0:T(8,128)(2,1)S(1)}, u32[]{:S(2)}, u32[]{:S(2)}) collective-permute-start(bf16[8,1024]{1,0:T(8,128)(2,1)S(1)} %get-tuple-element.128), channel_id=1, source_target_pairs={{256,384},{257,385},{258,386},{259,387},{260,388},{261,389},{262,3... | collective-permute-start | bytes 49160 | tf_op jit(solution)/shard_map/ppermute | solution.py:41
  110.4 4.8 %copy-start.6 = (bf16[8,3,128,1024]{2,3,0,1:T(8,128)(2,1)S(1)}, bf16[8,3,128,1024]{2,3,0,1:T(8,128)(2,1)}, u32[]{:S(2)}) copy-start(bf16[8,3,128,1024]{2,3,0,1:T(8,128)(2,1)} %copy.37) | copy-start | bytes 18874372
  119.1 4.9 %collective-permute-start.19 = (f32[8,2048]{1,0:T(8,128)S(1)}, f32[8,2048]{1,0:T(8,128)S(1)}, u32[]{:S(2)}, u32[]{:S(2)}) collective-permute-start(f32[8,2048]{1,0:T(8,128)S(1)} %maximum_select_fusion), channel_id=1, source_target_pairs={{0,8},{16,24},{32,40},{48,56},{64,72},{80,88},{96,104},{112,120},{... | collective-permute-start | bytes 196616 | tf_op jit(solution)/shard_map/ppermute | solution.py:41
  122.6 1.3 collective-permute-start.17
  123.2 0.7 collective-permute-start.18
  124.3 1.3 collective-permute-start.20
  125.0 0.7 collective-permute-start.21
  126.1 1.4 collective-permute-start.22
  126.7 0.7 collective-permute-start.23
  127.8 1.3 collective-permute-start.24
  128.5 0.7 collective-permute-start.25
  136.4 1.6 collective-permute-start.26
  137.1 0.9 collective-permute-start.27
  138.7 1.3 collective-permute-start.29
  139.3 0.7 collective-permute-start.30
  140.7 7.0 %copy-start.5 = (bf16[1024,1024]{1,0:T(8,128)(2,1)S(1)}, bf16[1024,1024]{1,0:T(8,128)(2,1)}, u32[]{:S(2)}) copy-start(bf16[1024,1024]{1,0:T(8,128)(2,1)} %copy-done.4) | copy-start | bytes 6291460
  140.7 1.5 collective-permute-start.31
  141.5 0.7 collective-permute-start.32
  142.8 1.4 collective-permute-start.34
  143.5 0.7 collective-permute-start.35
  144.9 2.8 %collective-permute-start.36 = (bf16[8,1024]{1,0:T(8,128)(2,1)S(1)}, bf16[8,1024]{1,0:T(8,128)(2,1)S(1)}, u32[]{:S(2)}, u32[]{:S(2)}) collective-permute-start(bf16[8,1024]{1,0:T(8,128)(2,1)S(1)} %convolution_convert_fusion), channel_id=1, source_target_pairs={{128,256},{129,257},{130,258},{131,259},{132,260},{133,261},{134,2... | collective-permute-start | bytes 49160 | tf_op jit(solution)/shard_map/ppermute | solution.py:41
  145.5 2.1 collective-permute-start.37
  146.2 20.3 %copy-start.1 = (bf16[1024,1024]{0,1:T(8,128)(2,1)S(1)}, bf16[1024,1024]{0,1:T(8,128)(2,1)}, u32[]{:S(2)}) copy-start(bf16[1024,1024]{0,1:T(8,128)(2,1)} %copy-done) | copy-start | bytes 6291460
  146.2 18.4 %collective-permute-start.28 = (bf16[8,3072]{1,0:T(8,128)(2,1)S(1)}, bf16[8,3072]{1,0:T(8,128)(2,1)S(1)}, u32[]{:S(2)}, u32[]{:S(2)}) collective-permute-start(bf16[8,3072]{1,0:T(8,128)(2,1)S(1)} %pad_maximum_fusion.13), channel_id=1, source_target_pairs={{8,0},{24,16},{40,32},{56,48},{72,64},{88,80},{104,96},{120,112},{... | collective-permute-start | bytes 147464 | tf_op jit(solution)/shard_map/ppermute | solution.py:41
  148.1 16.5 %collective-permute-start.38 = (bf16[8,1024]{1,0:T(8,128)(2,1)S(1)}, bf16[8,1024]{1,0:T(8,128)(2,1)S(1)}, u32[]{:S(2)}, u32[]{:S(2)}) collective-permute-start(bf16[8,1024]{1,0:T(8,128)(2,1)S(1)} %get-tuple-element.132), channel_id=1, source_target_pairs={{256,128},{257,129},{258,130},{259,131},{260,132},{261,133},{262,1... | collective-permute-start | bytes 49160 | tf_op jit(solution)/shard_map/ppermute | solution.py:41
  148.7 15.9 %collective-permute-start.39 = (bf16[8,1024]{1,0:T(8,128)(2,1)S(1)}, bf16[8,1024]{1,0:T(8,128)(2,1)S(1)}, u32[]{:S(2)}, u32[]{:S(2)}) collective-permute-start(bf16[8,1024]{1,0:T(8,128)(2,1)S(1)} %get-tuple-element.132), channel_id=1, source_target_pairs={{256,384},{257,385},{258,386},{259,387},{260,388},{261,389},{262,3... | collective-permute-start | bytes 49160 | tf_op jit(solution)/shard_map/ppermute | solution.py:41
  164.6 6.7 %copy-start.11 = (bf16[8,3072]{1,0:T(8,128)(2,1)}, bf16[8,3072]{1,0:T(8,128)(2,1)S(1)}, u32[]{:S(2)}) copy-start(bf16[8,3072]{1,0:T(8,128)(2,1)S(1)} %collective-permute-done.28) | copy-start | bytes 147460
  165.0 3.9 %copy-start.3 = (bf16[1024,1024]{0,1:T(8,128)(2,1)S(1)}, bf16[1024,1024]{0,1:T(8,128)(2,1)}, u32[]{:S(2)}) copy-start(bf16[1024,1024]{0,1:T(8,128)(2,1)} %copy-done.2) | copy-start | bytes 6291460
  165.0 2.1 collective-permute-start.40
  165.8 1.3 collective-permute-start.41
  167.5 2.0 collective-permute-start.42
  168.2 1.3 collective-permute-start.43
  169.9 3.6 %collective-permute-start.44 = (bf16[8,1024]{1,0:T(8,128)(2,1)S(1)}, bf16[8,1024]{1,0:T(8,128)(2,1)S(1)}, u32[]{:S(2)}, u32[]{:S(2)}) collective-permute-start(bf16[8,1024]{1,0:T(8,128)(2,1)S(1)} %fusion.42), channel_id=1, source_target_pairs={{32,16},{96,80},{160,144},{224,208},{288,272},{352,336},{416,400},... | collective-permute-start | bytes 49160 | tf_op jit(solution)/shard_map/ppermute | solution.py:41
  170.6 3.0 %collective-permute-start.45 = (bf16[8,1024]{1,0:T(8,128)(2,1)S(1)}, bf16[8,1024]{1,0:T(8,128)(2,1)S(1)}, u32[]{:S(2)}, u32[]{:S(2)}) collective-permute-start(bf16[8,1024]{1,0:T(8,128)(2,1)S(1)} %fusion.42), channel_id=1, source_target_pairs={{32,48},{96,112},{160,176},{224,240},{288,304},{352,368},{416,432}... | collective-permute-start | bytes 49160 | tf_op jit(solution)/shard_map/ppermute | solution.py:41
  171.3 4.0 %slice-start.1 = ((bf16[8,3072]{1,0:T(8,128)(2,1)}), bf16[8,1024]{1,0:T(8,128)(2,1)S(1)}, s32[]{:S(2)}) async-start(bf16[8,3072]{1,0:T(8,128)(2,1)} %copy-done.11), calls=%async_computation.5 | async-start | bytes 32768 | tf_op jit(solution)/shard_map/slice | solution.py:246
  171.3 5.9 %collective-permute-start.33 = (f32[8,2048]{1,0:T(8,128)S(1)}, f32[8,2048]{1,0:T(8,128)S(1)}, u32[]{:S(2)}, u32[]{:S(2)}) collective-permute-start(f32[8,2048]{1,0:T(8,128)S(1)} %pad_maximum_fusion.11), channel_id=1, source_target_pairs={{0,8},{16,24},{32,40},{48,56},{64,72},{80,88},{96,104},{112,120},{... | collective-permute-start | bytes 196616 | tf_op jit(solution)/shard_map/ppermute | solution.py:41
  174.0 1.6 collective-permute-start.46
  174.6 0.9 collective-permute-start.47
  (3 other events, 5.1 us)
Sparse Core Ops, SparseCore 0:
  45.4 48.7 all-gather.2

commit v5 on v3

--- a/solution.py
+++ b/solution.py
@@ -89,25 +89,16 @@
 
     terms = rounded(direction[:, None, :] * fields.astype(jnp.float32))
     leaf_terms = padded(terms[0])
-    map_rows = lax.dynamic_slice_in_dim(row_map[0, 0], lax.axis_index(FRONT) * rows, rows)
-    digits = jnp.stack([map_rows // 32, map_rows % 32]).astype(jnp.bfloat16)
-    digits = jnp.broadcast_to(digits[None], (width, 2, rows))
-
-    def marked(values):
-        return jnp.concatenate([values.reshape(width, share, rows), digits], 1)
-
     own = jnp.broadcast_to(leaf_terms.reshape(1, width * PAD, rows), (width, width * PAD, rows))
     own = jnp.concatenate([padded(fields[1]), padded(terms[1]), own], 1)
     message = jnp.concatenate(
-        [jnp.concatenate([marked(terms[0]), own], 1), jnp.concatenate([marked(fields[0]), own], 1)], 0
+        [jnp.concatenate([leaf_terms, own], 1), jnp.concatenate([padded(fields[0]), own], 1)], 0
     )
     node_block = update_blocks[1]
     swapped = after(jnp.where(odd, inverse_blocks[0], update_blocks[0]), message)
     message = lax.all_to_all(message, PAIR, 0, 0, tiled=True)
     message = message.reshape((2, width) + message.shape[1:])
     leaf_pair = lanes(message[:, :, :PAD])
-    pair_map = leaf_pair[share].astype(jnp.float32) * 32 + leaf_pair[share + 1].astype(jnp.float32)
-    pair_map = pair_map.astype(jnp.int32)
     mine = jnp.where(odd, message[1], message[0])
     field_node = lanes(mine[:, PAD : 2 * PAD])
     term_node = lanes(mine[:, 2 * PAD : 3 * PAD])
@@ -127,19 +118,25 @@
     later = lax.all_gather(later, FRONT, axis=0)
     near_spots, far_spots = [spots(part) for part in near_order(row_map[1, 0])]
 
+    map_rows = lax.dynamic_slice_in_dim(row_map[0, 0], lax.axis_index(FRONT) * rows, rows)
+    digits = jnp.stack([map_rows // 32, map_rows % 32]).astype(jnp.bfloat16)
+    digits = jnp.broadcast_to(digits[None], (width, 2, rows))
     update = rounded(times_transposed(leaf_all, update_blocks[0])).reshape(width, PAD, rows)
+    update = jnp.concatenate([update[:, :share], digits], 1)
     update = lax.all_to_all(jnp.concatenate([update, update], 0), PAIR, 0, 0, tiled=True)
-    update = times_transposed(lanes(update), spots(pair_map))
+    update = lanes(update)
+    pair_map = update[share].astype(jnp.float32) * 32 + update[share + 1].astype(jnp.float32)
+    pair_map = pair_map.astype(jnp.int32)
+    update = times_transposed(update, spots(pair_map))
     node_r = term_node.astype(jnp.float32) - jnp.where(odd, update, 0.0)
 
-    first = rounded(node_r)
-    update = times_transposed(rounded(times_transposed(first, node_near)), near_spots)
-    update = update + times_transposed(rounded(times_transposed(first, node_far)), far_spots)
-    update = rounded(update)
+    node_up = rounded(times(near_spots, node_near) + times(far_spots, node_far))
+    update = rounded(times_transposed(rounded(node_r), node_up))
+
     at_station = receivers[0][:, None] == jnp.arange(whole)[None, :]
     station_weight = jnp.sum(jnp.where(at_station, weights[0][:, None], 0.0), axis=0)
 
-    got = {}
+    got = {"up": node_up}
 
     def slot(blocks, k):
         matrix = blocks[:, k + 1].reshape(whole, whole)
@@ -152,22 +149,21 @@
         )
 
     def beside_up(height, token):
-        if height == 2:
-            near, far, token = lax.optimization_barrier((node_near, node_far, token))
-            got["up"] = rounded(times(near_spots, near) + times(far_spots, far))
-            return ["up"]
         if height == levels:
-            blocks = after(later, token)[:, 0]
+            got["factor"] = later[:, 0]
+            return []
+        return []
+
+    def beside_down(height, token):
+        names = []
+        if height == levels - 1:
+            blocks = got["factor"]
             got["inverse"] = rounded(
                 lax.dot_general(
                     blocks, blocks, (((0, 1), (0, 1)), ((), ())), preferred_element_type=jnp.float32
                 )
             )
-            return ["inverse"]
-        return []
-
-    def beside_down(height, token):
-        names = []
+            names.append("inverse")
         if height == levels:
             blocks = after(later, token)
             got["leaf"] = [slot(blocks, 0), slot(blocks, 1)]
@@ -185,7 +181,10 @@
     def forward(update, node_r, beside):
         for height in range(2, levels + 1):
             left, right = links(height, groups)
-            from_right, from_left = send(update, right), send(update, left)
+            if height == 3:
+                from_left, from_right = send(update, left), send(update, right)
+            else:
+                from_right, from_left = send(update, right), send(update, left)
             from_left, from_right = joined(beside(height, update), from_left, from_right)
             node_r = node_r - from_left.astype(jnp.float32) - from_right.astype(jnp.float32)
             if height < levels:
@@ -212,7 +211,15 @@
         return vectors[:, :whole], vectors[:, whole:]
 
     def through_inverse(vectors):
-        return times(vectors, got["inverse"])
+        if "inverse" in got:
+            return times(vectors, got["inverse"])
+        blocks = got["factor"]
+        solved = lax.dot_general(
+            vectors, blocks, (((1,), (2,)), ((), ())), preferred_element_type=jnp.float32
+        )
+        return lax.dot_general(
+            rounded(solved), blocks, (((1, 2), (0, 1)), ((), ())), preferred_element_type=jnp.float32
+        )
 
     carried = jnp.concatenate([station_weight, station_weight])[None, :]
 

time: 223 us -> 222 us (level)
  waiting for transfers between devices: 41.3 us -> 37.3 us
  matrix products: 33.7 us -> 36.5 us
    ppermute x44, waiting for transfers between devices: 16.5 us -> 12.6 us  [send(): return lax.ppermute(value, LEAF, pairs)]
    dot_general x2, matrix products: 5.64 us -> 7.92 us  [slot(): lax.dot_general(jnp.where(odd, places, matrix), matrix, CONTRACT_FIRST, p...]
    dot_general x1 -> x2, matrix products: 4.76 us -> 6.93 us  [the longest x1 3.78 us: beside_down(): lax.dot_general(blocks, blocks, (((0, 1), (0, 1)), ((), ())), preferred_e...]
    dot_general x16 -> x15, matrix products: 11.7 us -> 9.7 us  [times_transposed(): lax.dot_general(vectors, matrix, CONTRACT_LAST, preferred_element_type=jn...]
    dot_general x22 -> x21, matrix products: 11.6 us -> 12 us  [times(): return jnp.dot(vectors, matrix, preferred_element_type=jnp.float32)]
where the time goes in v5:
time: 222 us; the launch traced here: 221 us
  starting transfers between devices  64.9 us (29%)
  blocking collectives  51.9 us (23%)
  waiting for transfers between devices  37.3 us (17%)
  matrix products  36.5 us (16%)
  between operations  18.7 us (8%)
  local copies, waits for them, and re-layouts  6.13 us (3%)
  other arithmetic  5.5 us (2%)
    all_to_all x1, blocking collectives, per_device(): out = lax.all_to_all(out, PAIR, 0, 0, tiled=True)  51.9 us
    ppermute x44, starting transfers between devices, send(): return lax.ppermute(value, LEAF, pairs)  37.1 us
    all_gather x1, waiting for transfers between devices, per_device(): later = lax.all_gather(later, FRONT, axis=0)  17.9 us
    ppermute x44, waiting for transfers between devices, send(): return lax.ppermute(value, LEAF, pairs)  12.6 us
    dot_general x21, matrix products, times(): return jnp.dot(vectors, matrix, preferred_element_type=jnp.float32)  12 us
    ppermute x3, starting transfers between devices, shifted(): lax.ppermute(block, 'y', [(k, (k + by) % count) for k in range(count)])  10.9 us
    all_to_all x1, starting transfers between devices, per_device(): message = lax.all_to_all(message, PAIR, 0, 0, tiled=True)  9.72 us
    dot_general x15, matrix products, times_transposed(): lax.dot_general(vectors, matrix, CONTRACT_LAST, preferred_element_type=jn...  9.7 us
  transfers between devices with their start and end apart: 51, of which 5 were waited for; matrix products, arithmetic and copies ran while one was open for 15% of the time, Pallas kernels for 0%

profile of v5, /device:TPU:1, one launch (start us, length us, event | category | flops | bytes accessed | tf_op | source)
XLA Modules:
  0.0 220.9 jit_solution(4190957253140072934)
XLA Ops:
  7.2 1.1 slice_bitcast_fusion.10
  8.3 4.0 %collective-permute-start = (bf16[128,1024]{1,0:T(8,128)(2,1)S(1)}, bf16[128,1024]{1,0:T(8,128)(2,1)S(1)}, u32[]{:S(2)}, u32[]{:S(2)}) collective-permute-start(bf16[128,1024]{1,0:T(8,128)(2,1)S(1)} %slice_bitcast_fusion.10), channel_id=1, source_target_pairs={{0,2},{2,4},{4,6},{6,0},{1,3},{3,5},{5,7},{7,1},{8,10},{10,12},{12... | collective-permute-start | bytes 786440 | tf_op jit(solution)/shard_map/ppermute | solution.py:48
  12.3 3.4 %collective-permute-start.1 = (bf16[128,1024]{1,0:T(8,128)(2,1)S(1)}, bf16[128,1024]{1,0:T(8,128)(2,1)S(1)}, u32[]{:S(2)}, u32[]{:S(2)}) collective-permute-start(bf16[128,1024]{1,0:T(8,128)(2,1)S(1)} %slice_bitcast_fusion.10), channel_id=1, source_target_pairs={{0,6},{2,0},{4,2},{6,4},{1,7},{3,1},{5,3},{7,5},{8,14},{10,8},{12,... | collective-permute-start | bytes 786440 | tf_op jit(solution)/shard_map/ppermute | solution.py:48
  15.7 3.5 %collective-permute-start.2 = (bf16[128,1024]{1,0:T(8,128)(2,1)S(1)}, bf16[128,1024]{1,0:T(8,128)(2,1)S(1)}, u32[]{:S(2)}, u32[]{:S(2)}) collective-permute-start(bf16[128,1024]{1,0:T(8,128)(2,1)S(1)} %slice_bitcast_fusion.10), channel_id=1, source_target_pairs={{0,4},{2,6},{4,0},{6,2},{1,5},{3,7},{5,1},{7,3},{8,12},{10,14},{12... | collective-permute-start | bytes 786440 | tf_op jit(solution)/shard_map/ppermute | solution.py:48
  19.2 0.7 fusion.113
  19.9 0.7 multiply_convert_fusion.1
  20.9 0.8 fusion.57
  21.7 9.7 %all-to-all-start = ((bf16[16,88,128]{2,1,0:T(8,128)(2,1)}), bf16[16,88,128]{2,1,0:T(8,128)(2,1)S(1)}, u32[]{:S(2)}, u32[]{:S(2)}) async-start(bf16[16,88,128]{2,1,0:T(8,128)(2,1)} %fusion.57), calls=%async_computation | async-start | bytes 720896 | tf_op jit(solution)/shard_map/all_to_all | solution.py:99
  31.5 3.3 %collective-permute-start.14 = (bf16[128,1024]{1,0:T(8,128)(2,1)S(1)}, bf16[128,1024]{1,0:T(8,128)(2,1)S(1)}, u32[]{:S(2)}, u32[]{:S(2)}) collective-permute-start(bf16[128,1024]{1,0:T(8,128)(2,1)S(1)} %bitcast_select_fusion.1), channel_id=1, source_target_pairs={{0,8},{16,24},{32,40},{48,56},{64,72},{80,88},{96,104},{112,120},{... | collective-permute-start | bytes 786440 | tf_op jit(solution)/shard_map/ppermute | solution.py:41
  38.5 0.9 all-to-all-done
  41.3 2.0 collective-permute-done.14
  43.3 1.1 pad_maximum_fusion.1
  44.5 1.1 pad_maximum_fusion
  45.7 2.8 %collective-permute-start.3 = (bf16[512,1024]{1,0:T(8,128)(2,1)S(1)}, bf16[512,1024]{1,0:T(8,128)(2,1)}, u32[]{:S(2)}, u32[]{:S(2)}) collective-permute-start(bf16[512,1024]{1,0:T(8,128)(2,1)S(1)} %pad_maximum_fusion), channel_id=1, source_target_pairs={{0,1},{1,0},{2,3},{3,2},{4,5},{5,4},{6,7},{7,6},{8,9},{9,8},{10,11... | collective-permute-start | bytes 3145736 | tf_op jit(solution)/shard_map/ppermute | solution.py:58
  49.3 4.4 %all-to-all-start.1 = ((bf16[16,8,128]{2,1,0:T(8,128)(2,1)}), bf16[16,8,128]{2,1,0:T(8,128)(2,1)S(1)}, u32[]{:S(2)}, u32[]{:S(2)}) async-start(bf16[16,8,128]{2,1,0:T(8,128)(2,1)} %maximum_maximum_fusion), calls=%async_computation.1 | async-start | bytes 65536 | tf_op jit(solution)/shard_map/all_to_all | solution.py:126
  53.7 5.8 %all-to-all-done.1 = bf16[16,8,128]{2,1,0:T(8,128)(2,1)S(1)} async-done(((bf16[16,8,128]{2,1,0:T(8,128)(2,1)}), bf16[16,8,128]{2,1,0:T(8,128)(2,1)S(1)}, u32[]{:S(2)}, u32[]{:S(2)}) %all-to-all-start.1) | async-done | bytes 32800 | tf_op jit(solution)/shard_map/all_to_all | solution.py:126
  59.5 1.5 fusion.23
  61.1 2.7 %fusion.16 = f32[1024,1024]{1,0:T(8,128)S(1)} fusion(bf16[512,1024]{1,0:T(8,128)(2,1)} %collective-permute-done.3, s32[512]{0:T(512)S(1)} %bitcast.188), kind=kOutput, calls=%fused_computation.24 | convolution fusion | flops 1074266112 | bytes 5244928 | tf_op jit(solution)/shard_map/dot_general | solution.py:19
  63.8 1.3 add_convert_fusion
  65.7 0.7 collective-permute-start.4
  66.4 0.7 collective-permute-start.5
  67.7 0.7 collective-permute-start.6
  68.4 0.7 collective-permute-start.7
  69.9 0.7 collective-permute-start.8
  70.6 0.7 collective-permute-start.9
  71.9 0.7 collective-permute-start.10
  72.6 0.7 collective-permute-start.11
  74.0 0.7 collective-permute-start.12
  74.7 0.7 collective-permute-start.13
  75.4 17.9 %all-gather.3.cloned.1.call-done = bf16[24,128,1024]{2,1,0:T(8,128)(2,1)} async-done(((bf16[3,128,1024]{2,1,0:T(8,128)(2,1)}), bf16[24,128,1024]{2,1,0:T(8,128)(2,1)}) %all-gather.3.cloned.1.call-update) | async-done | bytes 6291472 | tf_op jit(solution)/shard_map/all_gather | solution.py:118
  93.3 3.2 %fusion.118 = (bf16[8,1024]{1,0:T(8,128)(2,1)S(1)}, f32[8,1024]{1,0:T(8,128)S(1)}) fusion(bf16[8,3,128,1024]{3,2,1,0:T(8,128)(2,1)} %bitcast.167, bf16[8,1024]{1,0:T(8,128)(2,1)S(1)} %collective-permute-done.13, bf16[8,1024]{1,0:T(8,128)(2,1)S(1)} %collective-permute-done.12, bf16[8,1024]{1,0:T(8,128)(2,1)S(1)} %collective-permute-done.11, ...), kind=kOutput, calls=%fused_computation.208 | convolution fusion | flops 33677312 | bytes 4374528 | tf_op jit(solution)/shard_map/dot_general | solution.py:220
  96.4 0.7 collective-permute-start.15
  97.1 0.8 collective-permute-start.16
  98.0 5.1 %bitcast_convert_fusion.2 = bf16[1024,1024]{1,0:T(8,128)(2,1)S(1)} fusion(s32[8,128]{1,0:T(8,128)S(1)} %bitcast.186, pred[]{:T(512)S(6)} %eq.132, bf16[8,3,128,1024]{3,2,1,0:T(8,128)(2,1)} %bitcast.168), kind=kOutput, calls=%fused_computation.4 | convolution fusion | flops 2151677952 | bytes 6295553 | tf_op jit(solution)/shard_map/dot_general | solution.py:146
  103.1 2.8 %bitcast_convert_fusion.1 = bf16[1024,1024]{1,0:T(8,128)(2,1)S(1)} fusion(s32[8,128]{1,0:T(8,128)S(1)} %bitcast.185, pred[]{:T(512)S(6)} %eq.132, bf16[8,3,128,1024]{3,2,1,0:T(8,128)(2,1)S(1)} %bitcast.169), kind=kOutput, calls=%fused_computation.3 | convolution fusion | flops 2151677952 | bytes 6295553 | tf_op jit(solution)/shard_map/dot_general | solution.py:146
  107.3 3.1 %collective-permute-start.19 = (f32[8,2048]{1,0:T(8,128)S(1)}, f32[8,2048]{1,0:T(8,128)S(1)}, u32[]{:S(2)}, u32[]{:S(2)}) collective-permute-start(f32[8,2048]{1,0:T(8,128)S(1)} %maximum_select_fusion), channel_id=1, source_target_pairs={{0,8},{16,24},{32,40},{48,56},{64,72},{80,88},{96,104},{112,120},{... | collective-permute-start | bytes 196616 | tf_op jit(solution)/shard_map/ppermute | solution.py:41
  111.5 0.7 collective-permute-start.18
  112.1 3.8 %bitcast_convert_fusion = bf16[1024,1024]{1,0:T(8,128)(2,1)} fusion(bf16[8,3,128,1024]{3,2,1,0:T(8,128)(2,1)S(1)} %bitcast.170), kind=kOutput, calls=%fused_computation.2 | convolution fusion | flops 2148532224 | bytes 4194304 | tf_op jit(solution)/shard_map/dot_general | solution.py:162
  117.0 0.7 collective-permute-start.21
  118.7 0.7 collective-permute-start.23
  119.8 0.8 collective-permute-start.24
  120.6 0.7 collective-permute-start.25
  122.1 0.8 copy-done.3
  123.9 0.7 fusion.25
  125.3 0.7 collective-permute-start.26
  125.9 0.9 collective-permute-start.27
  127.5 0.7 collective-permute-start.29
  128.2 0.7 collective-permute-start.30
  129.5 0.8 collective-permute-start.31
  130.3 0.7 collective-permute-start.32
  131.7 0.7 collective-permute-start.34
  132.4 0.7 collective-permute-start.35
  133.7 0.7 collective-permute-start.36
  134.4 0.7 collective-permute-start.37
  135.1 1.3 collective-permute-start.28
  137.4 0.7 collective-permute-start.39
  138.1 10.5 %collective-permute-done.28 = bf16[8,3072]{1,0:T(8,128)(2,1)S(1)} collective-permute-done((bf16[8,3072]{1,0:T(8,128)(2,1)S(1)}, bf16[8,3072]{1,0:T(8,128)(2,1)S(1)}, u32[]{:S(2)}, u32[]{:S(2)}) %collective-permute-start.28) | collective-permute-done | bytes 49184 | tf_op jit(solution)/shard_map/ppermute | solution.py:41
  149.7 0.7 collective-permute-start.41
  151.8 0.7 collective-permute-start.43
  153.9 0.7 collective-permute-start.45
  154.7 2.2 %collective-permute-start.33 = (f32[8,2048]{1,0:T(8,128)S(1)}, f32[8,2048]{1,0:T(8,128)S(1)}, u32[]{:S(2)}, u32[]{:S(2)}) collective-permute-start(f32[8,2048]{1,0:T(8,128)S(1)} %pad_maximum_fusion.3), channel_id=1, source_target_pairs={{0,8},{16,24},{32,40},{48,56},{64,72},{80,88},{96,104},{112,120},{... | collective-permute-start | bytes 196616 | tf_op jit(solution)/shard_map/ppermute | solution.py:41
  158.0 0.7 collective-permute-start.47
  158.9 1.1 fusion.66
  160.9 51.9 %all_to_all.15 = f32[16,8,128]{2,1,0:T(8,128)S(1)} all-to-all(f32[16,8,128]{2,1,0:T(8,128)S(1)} %pad_maximum_fusion.4), channel_id=1, replica_groups=mesh['pair'=32,'side'=2,'y'=4,'core'=2] {'side','y','core'}, dimensions={0} | all-to-all | bytes 131072 | tf_op jit(solution)/shard_map/all_to_all | solution.py:268
  (186 shorter events, 25.3 us)
Async XLA Ops:
  7.2 24.3 %copy-start.7 = (bf16[2,128,1024]{2,1,0:T(8,128)(2,1)S(1)}, bf16[2,128,1024]{2,1,0:T(8,128)(2,1)}, u32[]{:S(2)}) copy-start(bf16[2,128,1024]{2,1,0:T(8,128)(2,1)} %param.10) | copy-start | bytes 1572868
  7.2 24.3 %copy-start.6 = (bf16[2,128,1024]{2,1,0:T(8,128)(2,1)S(1)}, bf16[2,128,1024]{2,1,0:T(8,128)(2,1)}, u32[]{:S(2)}) copy-start(bf16[2,128,1024]{2,1,0:T(8,128)(2,1)} %param.9) | copy-start | bytes 1572868
  8.2 36.3 %copy-start.8 = (bf16[128,1024]{1,0:T(8,128)(2,1)}, bf16[128,1024]{1,0:T(8,128)(2,1)S(1)}, u32[]{:S(2)}) copy-start(bf16[128,1024]{1,0:T(8,128)(2,1)S(1)} %slice_bitcast_fusion.10) | copy-start | bytes 786436
  8.3 26.6 %collective-permute-start = (bf16[128,1024]{1,0:T(8,128)(2,1)S(1)}, bf16[128,1024]{1,0:T(8,128)(2,1)S(1)}, u32[]{:S(2)}, u32[]{:S(2)}) collective-permute-start(bf16[128,1024]{1,0:T(8,128)(2,1)S(1)} %slice_bitcast_fusion.10), channel_id=1, source_target_pairs={{0,2},{2,4},{4,6},{6,0},{1,3},{3,5},{5,7},{7,1},{8,10},{10,12},{12... | collective-permute-start | bytes 786440 | tf_op jit(solution)/shard_map/ppermute | solution.py:48
  12.3 23.1 %collective-permute-start.1 = (bf16[128,1024]{1,0:T(8,128)(2,1)S(1)}, bf16[128,1024]{1,0:T(8,128)(2,1)S(1)}, u32[]{:S(2)}, u32[]{:S(2)}) collective-permute-start(bf16[128,1024]{1,0:T(8,128)(2,1)S(1)} %slice_bitcast_fusion.10), channel_id=1, source_target_pairs={{0,6},{2,0},{4,2},{6,4},{1,7},{3,1},{5,3},{7,5},{8,14},{10,8},{12,... | collective-permute-start | bytes 786440 | tf_op jit(solution)/shard_map/ppermute | solution.py:48
  15.7 21.6 %collective-permute-start.2 = (bf16[128,1024]{1,0:T(8,128)(2,1)S(1)}, bf16[128,1024]{1,0:T(8,128)(2,1)S(1)}, u32[]{:S(2)}, u32[]{:S(2)}) collective-permute-start(bf16[128,1024]{1,0:T(8,128)(2,1)S(1)} %slice_bitcast_fusion.10), channel_id=1, source_target_pairs={{0,4},{2,6},{4,0},{6,2},{1,5},{3,7},{5,1},{7,3},{8,12},{10,14},{12... | collective-permute-start | bytes 786440 | tf_op jit(solution)/shard_map/ppermute | solution.py:48
  20.8 22.5 %slice-start = ((bf16[2,128,1024]{2,1,0:T(8,128)(2,1)}), bf16[1,128,1024]{2,1,0:T(8,128)(2,1)S(1)}, s32[]{:S(2)}) async-start(bf16[2,128,1024]{2,1,0:T(8,128)(2,1)} %param.9), calls=%async_computation.4 | async-start | bytes 524288 | tf_op jit(solution)/shard_map/slice | solution.py:117
  21.7 17.8 %all-to-all-start = ((bf16[16,88,128]{2,1,0:T(8,128)(2,1)}), bf16[16,88,128]{2,1,0:T(8,128)(2,1)S(1)}, u32[]{:S(2)}, u32[]{:S(2)}) async-start(bf16[16,88,128]{2,1,0:T(8,128)(2,1)} %fusion.57), calls=%async_computation | async-start | bytes 720896 | tf_op jit(solution)/shard_map/all_to_all | solution.py:99
  31.4 61.9 %all-gather.3.cloned.1.call-start = ((), (), s32[]{:S(2)}) async-start(), calls=%async_computation.3 | async-start | bytes 7077888 | tf_op jit(solution)/shard_map/all_gather | solution.py:118
  31.5 12.9 %copy-start.19 = (s32[2,1,1024]{2,1,0:T(1,128)S(1)}, s32[2,1,1024]{2,1,0:T(1,128)}, u32[]{:S(2)}) copy-start(s32[2,1,1024]{2,1,0:T(1,128)} %param.11) | copy-start | bytes 24580
  31.5 11.7 %collective-permute-start.14 = (bf16[128,1024]{1,0:T(8,128)(2,1)S(1)}, bf16[128,1024]{1,0:T(8,128)(2,1)S(1)}, u32[]{:S(2)}, u32[]{:S(2)}) collective-permute-start(bf16[128,1024]{1,0:T(8,128)(2,1)S(1)} %bitcast_select_fusion.1), channel_id=1, source_target_pairs={{0,8},{16,24},{32,40},{48,56},{64,72},{80,88},{96,104},{112,120},{... | collective-permute-start | bytes 786440 | tf_op jit(solution)/shard_map/ppermute | solution.py:41
  34.8 6.4 %copy-start.10 = (bf16[128,1024]{1,0:T(8,128)(2,1)}, bf16[128,1024]{1,0:T(8,128)(2,1)S(1)}, u32[]{:S(2)}) copy-start(bf16[128,1024]{1,0:T(8,128)(2,1)S(1)} %collective-permute-done) | copy-start | bytes 786436
  35.4 9.1 %copy-start.13 = (bf16[128,1024]{1,0:T(8,128)(2,1)}, bf16[128,1024]{1,0:T(8,128)(2,1)S(1)}, u32[]{:S(2)}) copy-start(bf16[128,1024]{1,0:T(8,128)(2,1)S(1)} %collective-permute-done.1) | copy-start | bytes 786436
  37.3 7.2 %copy-start.15 = (bf16[128,1024]{1,0:T(8,128)(2,1)}, bf16[128,1024]{1,0:T(8,128)(2,1)S(1)}, u32[]{:S(2)}) copy-start(bf16[128,1024]{1,0:T(8,128)(2,1)S(1)} %collective-permute-done.2) | copy-start | bytes 786436
  45.7 15.4 %collective-permute-start.3 = (bf16[512,1024]{1,0:T(8,128)(2,1)S(1)}, bf16[512,1024]{1,0:T(8,128)(2,1)}, u32[]{:S(2)}, u32[]{:S(2)}) collective-permute-start(bf16[512,1024]{1,0:T(8,128)(2,1)S(1)} %pad_maximum_fusion), channel_id=1, source_target_pairs={{0,1},{1,0},{2,3},{3,2},{4,5},{5,4},{6,7},{7,6},{8,9},{9,8},{10,11... | collective-permute-start | bytes 3145736 | tf_op jit(solution)/shard_map/ppermute | solution.py:58
  48.5 15.3 %copy-start.17 = (bf16[8,88,128]{2,1,0:T(8,128)(2,1)}, bf16[8,88,128]{2,1,0:T(8,128)(2,1)S(1)}, u32[]{:S(2)}) copy-start(bf16[8,88,128]{2,1,0:T(8,128)(2,1)S(1)} %slice_select_fusion) | copy-start | bytes 540676
  49.3 10.2 %all-to-all-start.1 = ((bf16[16,8,128]{2,1,0:T(8,128)(2,1)}), bf16[16,8,128]{2,1,0:T(8,128)(2,1)S(1)}, u32[]{:S(2)}, u32[]{:S(2)}) async-start(bf16[16,8,128]{2,1,0:T(8,128)(2,1)} %maximum_maximum_fusion), calls=%async_computation.1 | async-start | bytes 65536 | tf_op jit(solution)/shard_map/all_to_all | solution.py:126
  65.0 4.0 %copy-start.20 = (f32[1,128]{1,0:T(1,128)S(1)}, f32[1,128]{1,0:T(1,128)}, u32[]{:S(2)}) copy-start(f32[1,128]{1,0:T(1,128)} %param.13) | copy-start | bytes 1540
  65.7 1.3 collective-permute-start.4
  66.4 0.7 collective-permute-start.5
  67.7 1.5 collective-permute-start.6
  68.4 0.8 collective-permute-start.7
  69.9 1.4 collective-permute-start.8
  70.6 0.7 collective-permute-start.9
  71.9 1.4 collective-permute-start.10
  72.6 0.8 collective-permute-start.11
  74.0 1.4 collective-permute-start.12
  74.7 0.7 collective-permute-start.13
  96.4 14.0 %collective-permute-start.15 = (bf16[8,1024]{1,0:T(8,128)(2,1)S(1)}, bf16[8,1024]{1,0:T(8,128)(2,1)S(1)}, u32[]{:S(2)}, u32[]{:S(2)}) collective-permute-start(bf16[8,1024]{1,0:T(8,128)(2,1)S(1)} %get-tuple-element.122), channel_id=1, source_target_pairs={{256,128},{257,129},{258,130},{259,131},{260,132},{261,133},{262,1... | collective-permute-start | bytes 49160 | tf_op jit(solution)/shard_map/ppermute | solution.py:41
  97.1 13.3 %collective-permute-start.16 = (bf16[8,1024]{1,0:T(8,128)(2,1)S(1)}, bf16[8,1024]{1,0:T(8,128)(2,1)S(1)}, u32[]{:S(2)}, u32[]{:S(2)}) collective-permute-start(bf16[8,1024]{1,0:T(8,128)(2,1)S(1)} %get-tuple-element.122), channel_id=1, source_target_pairs={{256,384},{257,385},{258,386},{259,387},{260,388},{261,389},{262,3... | collective-permute-start | bytes 49160 | tf_op jit(solution)/shard_map/ppermute | solution.py:41
  97.9 5.1 %copy-start.4 = (bf16[24,128,1024]{2,1,0:T(8,128)(2,1)S(1)}, bf16[24,128,1024]{2,1,0:T(8,128)(2,1)}, u32[]{:S(2)}) copy-start(bf16[24,128,1024]{2,1,0:T(8,128)(2,1)} %all-gather.3.cloned.1.call-done) | copy-start | bytes 18874372
  107.3 8.6 %collective-permute-start.19 = (f32[8,2048]{1,0:T(8,128)S(1)}, f32[8,2048]{1,0:T(8,128)S(1)}, u32[]{:S(2)}, u32[]{:S(2)}) collective-permute-start(f32[8,2048]{1,0:T(8,128)S(1)} %maximum_select_fusion), channel_id=1, source_target_pairs={{0,8},{16,24},{32,40},{48,56},{64,72},{80,88},{96,104},{112,120},{... | collective-permute-start | bytes 196616 | tf_op jit(solution)/shard_map/ppermute | solution.py:41
  110.8 5.1 %collective-permute-start.17 = (bf16[8,1024]{1,0:T(8,128)(2,1)S(1)}, bf16[8,1024]{1,0:T(8,128)(2,1)S(1)}, u32[]{:S(2)}, u32[]{:S(2)}) collective-permute-start(bf16[8,1024]{1,0:T(8,128)(2,1)S(1)} %fusion.46), channel_id=1, source_target_pairs={{128,64},{384,320},{129,65},{385,321},{130,66},{386,322},{131,67},... | collective-permute-start | bytes 49160 | tf_op jit(solution)/shard_map/ppermute | solution.py:41
  111.5 4.5 %collective-permute-start.18 = (bf16[8,1024]{1,0:T(8,128)(2,1)S(1)}, bf16[8,1024]{1,0:T(8,128)(2,1)S(1)}, u32[]{:S(2)}, u32[]{:S(2)}) collective-permute-start(bf16[8,1024]{1,0:T(8,128)(2,1)S(1)} %fusion.46), channel_id=1, source_target_pairs={{128,192},{384,448},{129,193},{385,449},{130,194},{386,450},{131,1... | collective-permute-start | bytes 49160 | tf_op jit(solution)/shard_map/ppermute | solution.py:41
  116.3 1.3 collective-permute-start.20
  117.0 0.7 collective-permute-start.21
  118.1 1.4 collective-permute-start.22
  118.7 0.7 collective-permute-start.23
  119.8 1.5 collective-permute-start.24
  120.6 0.7 collective-permute-start.25
  125.3 1.6 collective-permute-start.26
  125.9 0.9 collective-permute-start.27
  127.5 1.3 collective-permute-start.29
  128.2 0.7 collective-permute-start.30
  129.5 6.9 %copy-start.5 = (bf16[1024,1024]{1,0:T(8,128)(2,1)S(1)}, bf16[1024,1024]{1,0:T(8,128)(2,1)}, u32[]{:S(2)}) copy-start(bf16[1024,1024]{1,0:T(8,128)(2,1)} %bitcast_convert_fusion) | copy-start | bytes 6291460
  129.5 1.5 collective-permute-start.31
  130.3 0.7 collective-permute-start.32
  131.7 1.4 collective-permute-start.34
  132.4 0.7 collective-permute-start.35
  133.7 2.7 %collective-permute-start.36 = (bf16[8,1024]{1,0:T(8,128)(2,1)S(1)}, bf16[8,1024]{1,0:T(8,128)(2,1)S(1)}, u32[]{:S(2)}, u32[]{:S(2)}) collective-permute-start(bf16[8,1024]{1,0:T(8,128)(2,1)S(1)} %convolution_convert_fusion), channel_id=1, source_target_pairs={{128,256},{129,257},{130,258},{131,259},{132,260},{133,261},{134,2... | collective-permute-start | bytes 49160 | tf_op jit(solution)/shard_map/ppermute | solution.py:41
  134.4 2.0 collective-permute-start.37
  135.1 13.6 %collective-permute-start.28 = (bf16[8,3072]{1,0:T(8,128)(2,1)S(1)}, bf16[8,3072]{1,0:T(8,128)(2,1)S(1)}, u32[]{:S(2)}, u32[]{:S(2)}) collective-permute-start(bf16[8,3072]{1,0:T(8,128)(2,1)S(1)} %pad_maximum_fusion.5), channel_id=1, source_target_pairs={{8,0},{24,16},{40,32},{56,48},{72,64},{88,80},{104,96},{120,112},{... | collective-permute-start | bytes 147464 | tf_op jit(solution)/shard_map/ppermute | solution.py:41
  136.8 11.9 %collective-permute-start.38 = (bf16[8,1024]{1,0:T(8,128)(2,1)S(1)}, bf16[8,1024]{1,0:T(8,128)(2,1)S(1)}, u32[]{:S(2)}, u32[]{:S(2)}) collective-permute-start(bf16[8,1024]{1,0:T(8,128)(2,1)S(1)} %get-tuple-element.124), channel_id=1, source_target_pairs={{256,128},{257,129},{258,130},{259,131},{260,132},{261,133},{262,1... | collective-permute-start | bytes 49160 | tf_op jit(solution)/shard_map/ppermute | solution.py:41
  137.4 11.2 %collective-permute-start.39 = (bf16[8,1024]{1,0:T(8,128)(2,1)S(1)}, bf16[8,1024]{1,0:T(8,128)(2,1)S(1)}, u32[]{:S(2)}, u32[]{:S(2)}) collective-permute-start(bf16[8,1024]{1,0:T(8,128)(2,1)S(1)} %get-tuple-element.124), channel_id=1, source_target_pairs={{256,384},{257,385},{258,386},{259,387},{260,388},{261,389},{262,3... | collective-permute-start | bytes 49160 | tf_op jit(solution)/shard_map/ppermute | solution.py:41
  148.6 6.0 %copy-start.18 = (bf16[8,3072]{1,0:T(8,128)(2,1)}, bf16[8,3072]{1,0:T(8,128)(2,1)S(1)}, u32[]{:S(2)}) copy-start(bf16[8,3072]{1,0:T(8,128)(2,1)S(1)} %collective-permute-done.28) | copy-start | bytes 147460
  149.0 1.7 collective-permute-start.40
  149.7 1.1 collective-permute-start.41
  151.2 1.7 collective-permute-start.42
  151.8 1.1 collective-permute-start.43
  153.3 3.6 %collective-permute-start.44 = (bf16[8,1024]{1,0:T(8,128)(2,1)S(1)}, bf16[8,1024]{1,0:T(8,128)(2,1)S(1)}, u32[]{:S(2)}, u32[]{:S(2)}) collective-permute-start(bf16[8,1024]{1,0:T(8,128)(2,1)S(1)} %fusion.39), channel_id=1, source_target_pairs={{32,16},{96,80},{160,144},{224,208},{288,272},{352,336},{416,400},... | collective-permute-start | bytes 49160 | tf_op jit(solution)/shard_map/ppermute | solution.py:41
  153.9 3.0 %collective-permute-start.45 = (bf16[8,1024]{1,0:T(8,128)(2,1)S(1)}, bf16[8,1024]{1,0:T(8,128)(2,1)S(1)}, u32[]{:S(2)}, u32[]{:S(2)}) collective-permute-start(bf16[8,1024]{1,0:T(8,128)(2,1)S(1)} %fusion.39), channel_id=1, source_target_pairs={{32,48},{96,112},{160,176},{224,240},{288,304},{352,368},{416,432}... | collective-permute-start | bytes 49160 | tf_op jit(solution)/shard_map/ppermute | solution.py:41
  154.7 6.2 %collective-permute-start.33 = (f32[8,2048]{1,0:T(8,128)S(1)}, f32[8,2048]{1,0:T(8,128)S(1)}, u32[]{:S(2)}, u32[]{:S(2)}) collective-permute-start(f32[8,2048]{1,0:T(8,128)S(1)} %pad_maximum_fusion.3), channel_id=1, source_target_pairs={{0,8},{16,24},{32,40},{48,56},{64,72},{80,88},{96,104},{112,120},{... | collective-permute-start | bytes 196616 | tf_op jit(solution)/shard_map/ppermute | solution.py:41
  157.3 1.6 collective-permute-start.46
  158.0 0.9 collective-permute-start.47
  (11 other events, 28.2 us)
Sparse Core Ops, SparseCore 0:
  44.5 48.7 all-gather.2
